TPU v7x, 768 devices: a whole 4x8x12 slice. The times are simulated.
768 devices in a mesh: curve: 24 (over x, z_lo), col: 32 (over y, z_hi, core).
Axes of the slice: x: 4, y: 8, z: 12 (z_hi: 2, z_lo: 6; z = z_hi * 6 + z_lo), core: 2. Of those that a mesh axis runs over, the one named last changes fastest.
Arguments:
- evolving_state_array: float32 [5, 8, 589824], P(None, None, ('curve', 'col')), may hold values from -6 to 6
- point_id: int32 [589824], P(('curve', 'col')), may hold values from 0 to 143, as said below
- neighbours: int32 [8, 36864], P(None, ('curve', 'col')), may hold values from -1 to 36863, as said below
- jacobian: float32 [589824], P(('curve', 'col')), may hold values from 0.7 to 1.4
- inverse_metric: float32 [4, 589824], P(None, ('curve', 'col')), may hold values from -0.3 to 0.3
- coriolis: float32 [589824], P(('curve', 'col')), may hold values from -2 to 2
- column_slot: int32 [589824], P(('curve', 'col')), may hold values from 0 to 24575, as said below
Outputs:
- updated: float32 [5, 8, 589824], P(None, None, ('curve', 'col'))
- physics: float32 [5, 8, 589824], P(None, None, ('curve', 'col'))
Inputs may be any that keep to these rules, and one draw needn't show every extreme that they name: `point_id`: the points lie on a lattice around the band of 96 rows and 384 elements around. Among the points of one element and its listed neighbours, coinciding points of different elements share one number and all other points have distinct numbers; numbers repeat farther away. neighbours[k, e] names the element beside e toward the lower and the higher position around the band, the lower and the higher row, then the diagonal ones (lower row and lower position, lower row and higher position, higher row and lower position, higher row and higher position); -1 where the band ends. The lists are symmetric, the band closes around, and an element shares points only with itself and its listed ones. Element g lies on device g // 48 of curve+col; device d holds exactly the elements of rows 4 (d // 32) to 4 (d // 32) + 3 at positions 12 (d % 32) to 12 (d % 32) + 11 around the band, in some order. Within each group of rows, column_slot maps the group's columns one to one onto the slots; slot s belongs to device s // 768 of the group's col axis. Every device receives 768 columns and sends at most 72 to any one device of its group; that count is reached.
All inputs are finite; a program needn't handle non-finite values.
Results may differ from a plain program's by a relative error of at most 0.0003.
Values sent between devices are 32-bit elements; how exact they have to be, the bound alone decides.
No kernel may reach another device: no remote copies, remote signals or barrier semaphores. Data moves between devices by JAX's collectives and lax.ppermute only.
A program may use at most 32 MiB of HBM per device.

v0:
```python
import functools
import math

import jax
import jax.numpy as jnp
import numpy as np
from jax import lax
from jax.experimental import pallas as pl
from jax.experimental.pallas import tpu as pltpu
from jax.sharding import PartitionSpec as P

FIELDS = 5
LEV = 8
STATE = FIELDS * LEV
TILE = 48
LANES = 128
ELEMS_DEV = 48
POINTS_DEV = 768
N_COL = 32
CAP = 72
CAP_ROWS = CAP // 3
TIME_STEP = 0.1
HYPER_NU = 0.002
F32 = jnp.float32
BF16 = jnp.bfloat16
VMEM_LIMIT = 48 * 1024 * 1024


def gll_tables():
    root_fifth = 1.0 / math.sqrt(5.0)
    nodes = np.array([-1.0, -root_fifth, root_fifth, 1.0])
    weights = np.array([1.0, 5.0, 5.0, 1.0]) / 6.0
    table = np.zeros((4, 4))
    for i in range(4):
        for m in range(4):
            if i == m:
                table[i, m] = sum(1.0 / (nodes[i] - nodes[o]) for o in range(4) if o != i)
            else:
                upper = np.prod([nodes[i] - nodes[o] for o in range(4) if o != i])
                lower = np.prod([nodes[m] - nodes[o] for o in range(4) if o != m])
                table[i, m] = upper / (lower * (nodes[i] - nodes[m]))
    return table, weights


def two_parts(matrix):
    upper = matrix.astype(np.float32).astype(jnp.bfloat16)
    lower = (matrix - upper.astype(np.float64)).astype(np.float32).astype(jnp.bfloat16)
    return upper, lower


@functools.lru_cache(maxsize=None)
def operators():
    table, weights = gll_tables()
    eye4, eye8 = np.eye(4), np.eye(8)
    along_cycle = np.kron(eye4, table.T)
    along_rows = np.kron(table.T, eye4)
    grad = np.concatenate([np.kron(eye8, along_cycle), np.kron(eye8, along_rows)], axis=1)
    weight = np.diag(np.outer(weights, weights).reshape(16))
    div = np.concatenate(
        [np.kron(eye8, along_cycle @ weight), np.kron(eye8, along_rows @ weight)], axis=0
    )
    join = np.eye(256)
    for place in range(15):
        for j in range(4):
            low, high = place * 16 + 4 * j + 3, place * 16 + 16 + 4 * j
            join[low, high] = 1.0
            join[high, low] = 1.0
    both = np.zeros((512, 256))
    both[:256, :128] = div
    both[256:, 128:] = div
    div_join = both @ join
    grad_hi, grad_lo = two_parts(grad)
    div_hi, div_lo = two_parts(div_join)
    mass_weight = np.tile(np.outer(weights, weights).reshape(16), 8).astype(np.float32)
    return (
        np.concatenate([grad_hi, grad_hi], axis=0),
        grad_lo,
        div_hi,
        div_lo,
        join.astype(jnp.bfloat16),
        np.broadcast_to(mass_weight, (8, 128)).copy(),
    )


def dot(left, right):
    return jnp.dot(left, right, preferred_element_type=F32)


def dot_last(left, right):
    return lax.dot_general(left, right, (((1,), (1,)), ((), ())), preferred_element_type=F32)


def halves(value):
    upper = value.astype(BF16)
    lower = (value - upper.astype(F32)).astype(BF16)
    return upper, lower


def lane_iota(shape):
    return lax.broadcasted_iota(jnp.int32, shape, 1)


def row_iota(shape):
    return lax.broadcasted_iota(jnp.int32, shape, 0)


def chain_length(local, index, doublings):
    present = jnp.broadcast_to(local.astype(F32), (8, ELEMS_DEV))
    hit = (row_iota((ELEMS_DEV, ELEMS_DEV)) == index) & local
    step = hit.astype(F32).astype(BF16)
    length = present
    for k in range(doublings):
        length = length + dot(length.astype(BF16), step)
        if k + 1 < doublings:
            step = dot(step, step).astype(BF16)
    return length


def arrange_kernel(state_ref, geo_ref, near_ref, low_ref, high_ref, right_ref, left_ref, place_ref):
    base = (lax.axis_index("curve") * N_COL + lax.axis_index("col")) * ELEMS_DEV
    index = near_ref[...] - base
    local = (index >= 0) & (index < ELEMS_DEV)
    place = chain_length(local[0:1], index[0:1], 4)
    row = chain_length(local[2:3], index[2:3], 2)
    spot = row * 16.0 + place + 2.0
    points = (ELEMS_DEV, POINTS_DEV)
    spread = (lane_iota(points) // 16 == row_iota(points)).astype(F32).astype(BF16)
    spot_of_point = dot(spot.astype(BF16), spread)[0:1].astype(jnp.int32)
    target = spot_of_point * 16 + lane_iota((1, POINTS_DEV)) % 16
    place_ref[...] = jnp.broadcast_to(target, (8, POINTS_DEV))
    hits = (row_iota((1024, POINTS_DEV)) == target).astype(F32).astype(BF16)
    values = jnp.concatenate([state_ref[...], geo_ref[...]], axis=0)
    first = values.astype(BF16)
    rest = values - first.astype(F32)
    second = rest.astype(BF16)
    third = (rest - second.astype(F32)).astype(BF16)
    parts = dot_last(jnp.concatenate([first, second, third], axis=0), hits)
    ordered = parts[0:TILE] + parts[TILE : 2 * TILE] + parts[2 * TILE :]
    lane = lane_iota((TILE, LANES))
    to_right = jnp.zeros((TILE, LANES), F32)
    to_left = jnp.zeros((TILE, LANES), F32)
    for r in range(4):
        for g in range(2):
            block = ordered[:, (2 * r + g) * LANES : (2 * r + g + 1) * LANES]
            ref = low_ref if r < 2 else high_ref
            start = ((r % 2) * 2 + g) * TILE
            ref[start : start + TILE, :] = block
            inside = (lane >= 32 * r) & (lane < 32 * r + 32)
            if g == 1:
                to_right = jnp.where(inside, turned(block, 32 * r - 64), to_right)
            else:
                to_left = jnp.where(inside, turned(block, 32 * r - 32), to_left)
    right_ref[...] = to_right
    left_ref[...] = to_left


def turned(block, by):
    by = by % LANES
    return block if by == 0 else pltpu.roll(block, by, 1)


def margin_kernel(low_in, high_in, from_left, from_right, low_ref, high_ref):
    lane = lane_iota((TILE, LANES))
    for r in range(4):
        source = low_in if r < 2 else high_in
        ref = low_ref if r < 2 else high_ref
        start = (r % 2) * 2 * TILE
        first = source[start : start + TILE, :]
        ref[start : start + TILE, :] = jnp.where(lane < 32, turned(from_left[...], -32 * r), first)
        start += TILE
        second = source[start : start + TILE, :]
        ref[start : start + TILE, :] = jnp.where(
            lane >= 96, turned(from_right[...], 96 - 32 * r), second
        )


def send_kernel(slot_ref, map_ref):
    slot = slot_ref[...]
    slot_value = slot.astype(F32)
    device = jnp.floor((slot_value + 0.5) * (1.0 / POINTS_DEV))
    within = slot_value - device * POINTS_DEV
    wanted = jnp.broadcast_to(device.astype(jnp.int32), (N_COL, POINTS_DEV))
    chosen = (wanted == row_iota((N_COL, POINTS_DEV))).astype(F32)
    square = (LANES, LANES)
    upto = (row_iota(square) <= lane_iota(square)).astype(F32)
    count = jnp.concatenate([upto, jnp.ones(square, F32)], axis=1).astype(BF16)
    groups = POINTS_DEV // LANES
    stacked = jnp.concatenate(
        [chosen[:, i * LANES : (i + 1) * LANES] for i in range(groups)], axis=0
    )
    counted = dot(stacked.astype(BF16), count)
    before = jnp.zeros((N_COL, LANES), F32)
    ranks = []
    for i in range(groups):
        rows = counted[i * N_COL : (i + 1) * N_COL]
        here = (rows[:, :LANES] + before) * stacked[i * N_COL : (i + 1) * N_COL]
        ranks.append(jnp.sum(here, axis=0, keepdims=True))
        before = before + rows[:, LANES:]
    rank = jnp.concatenate(ranks, axis=1) - 1.0
    third = (rank >= CAP_ROWS).astype(F32) + (rank >= 2 * CAP_ROWS).astype(F32)
    line = device * CAP_ROWS + rank - third * CAP_ROWS
    lists = [jnp.where(third == float(k), line, -1.0) for k in range(3)]
    filler = jnp.zeros((4, POINTS_DEV), F32)
    map_ref[...] = jnp.concatenate(lists + [within + 1.0, filler], axis=0)


def fluxes(slope, coefficients):
    along_cycle, along_rows = slope[:, :LANES], slope[:, LANES:]
    caa, cab, cbb = coefficients
    return caa * along_cycle + cab * along_rows, cab * along_cycle + cbb * along_rows


def gradient(values, grad2_ref, grad_lo_ref):
    upper, lower = halves(values)
    return dot(jnp.concatenate([upper, lower], axis=1), grad2_ref[...]) + dot(
        upper, grad_lo_ref[...]
    )


def divergence_joined(values, div_hi_ref, div_lo_ref):
    upper, lower = halves(values)
    return dot(upper, div_hi_ref[...]) + dot(lower, div_hi_ref[...]) + dot(upper, div_lo_ref[...])


def rows_joined(below, here, above, low_mask, high_mask):
    parts = []
    for g in range(2):
        part = slice(g * LANES, (g + 1) * LANES)
        parts.append(
            here[:, part]
            + low_mask * turned(below[:, part], -12)
            + high_mask * turned(above[:, part], 12)
        )
    return parts


def section_kernel(
    below_ref,
    low_ref,
    high_ref,
    above_ref,
    place_ref,
    map_ref,
    grad2_ref,
    grad_lo_ref,
    div_hi_ref,
    div_lo_ref,
    join_ref,
    weight_ref,
    updated_ref,
    send_ref,
    slopes,
    flux,
    plain,
    coefs,
):
    quarters = (below_ref, low_ref, high_ref, above_ref)

    def tile(r, g, start=0, size=TILE):
        offset = ((r % 2) * 2 + g) * TILE + start
        return quarters[r // 2][offset : offset + size, :]

    cells = [(r, g) for r in range(8) for g in range(2)]
    stacked = []
    for r, g in cells:
        zonal, meridional = tile(r, g, 0, 8), tile(r, g, 8, 8)
        energy = 0.5 * (zonal * zonal + meridional * meridional) + tile(r, g, 16, 8)
        stacked += [tile(r, g, 0, STATE), energy]
    slopes[...] = gradient(jnp.concatenate(stacked, axis=0), grad2_ref, grad_lo_ref)

    for r, g in cells:
        def line(k):
            return jnp.broadcast_to(tile(r, g, STATE + k, 1), (8, LANES))

        jacobian, coriolis = line(0), line(1)
        m11, m12, m21, m22 = 1.0 + line(2), line(3), line(4), 1.0 + line(5)
        caa = jacobian * (m11 * m11 + m12 * m12)
        cab = jacobian * (m11 * m21 + m12 * m22)
        cbb = jacobian * (m21 * m21 + m22 * m22)
        at = (2 * r + g) * 24
        coefs[at : at + 8, :] = caa
        coefs[at + 8 : at + 16, :] = cab
        coefs[at + 16 : at + 24, :] = cbb
        mass = jacobian * weight_ref[...]
        at = (2 * r + g) * TILE
        first = slice(g * 2 * LANES, (g * 2 + 1) * LANES)
        second = slice((g * 2 + 1) * LANES, (g * 2 + 2) * LANES)
        for f in range(FIELDS):
            one, two = fluxes(slopes[at + 8 * f : at + 8 * f + 8, :], (caa, cab, cbb))
            flux[r * 56 + 8 * f : r * 56 + 8 * f + 8, first] = one
            flux[r * 56 + 8 * f : r * 56 + 8 * f + 8, second] = two
        zonal, meridional = tile(r, g, 0, 8), tile(r, g, 8, 8)
        flow1 = jacobian * (m11 * zonal + m12 * meridional)
        flow2 = jacobian * (m21 * zonal + m22 * meridional)
        for k in range(2):
            carried = tile(r, g, 24 + 8 * k, 8)
            flux[r * 56 + 40 + 8 * k : r * 56 + 48 + 8 * k, first] = carried * flow1
            flux[r * 56 + 40 + 8 * k : r * 56 + 48 + 8 * k, second] = carried * flow2
        ea, eb = slopes[at + 40 : at + 48, :LANES], slopes[at + 40 : at + 48, LANES:]
        ta, tb = slopes[at + 16 : at + 24, :LANES], slopes[at + 16 : at + 24, LANES:]
        part = slice(g * LANES, (g + 1) * LANES)
        plain[r * 32 : r * 32 + 8, part] = mass * (
            coriolis * meridional - (m11 * ea + m21 * eb)
        )
        plain[r * 32 + 8 : r * 32 + 16, part] = -mass * (
            coriolis * zonal + (m12 * ea + m22 * eb)
        )
        plain[r * 32 + 16 : r * 32 + 24, part] = -mass * (
            zonal * (m11 * ta + m21 * tb) + meridional * (m12 * ta + m22 * tb)
        )
        plain[r * 32 + 24 : r * 32 + 32, part] = mass

    spread = divergence_joined(flux[...], div_hi_ref, div_lo_ref)
    upper, lower = halves(plain[...])
    direct = dot(upper, join_ref[...]) + dot(lower, join_ref[...])

    lane = lane_iota((1, LANES)) % 16
    low_mask = (lane < 4).astype(F32)
    high_mask = (lane >= 12).astype(F32)

    def joined(value, size, r, start, count):
        def rows(k):
            return value[k * size + start : k * size + start + count, :]

        return rows_joined(rows(r - 1), rows(r), rows(r + 1), low_mask, high_mask)

    inverse = {}
    smooth = []
    for r in range(1, 7):
        mass_sum = joined(direct, 32, r, 24, 8)
        smoothing = joined(spread, 56, r, 0, STATE)
        for g in range(2):
            inverse[r, g] = 1.0 / jnp.where(mass_sum[g] > 0.0, mass_sum[g], 1.0)
            smooth.append(smoothing[g] * jnp.concatenate([inverse[r, g]] * FIELDS, axis=0))
    again = gradient(jnp.concatenate(smooth, axis=0), grad2_ref, grad_lo_ref)
    flat = []
    for r in range(1, 7):
        parts = []
        for g in range(2):
            at = (2 * r + g) * 24
            triple = tuple(
                jnp.concatenate([coefs[at + 8 * k : at + 8 * k + 8, :]] * FIELDS, axis=0)
                for k in range(3)
            )
            start = (2 * (r - 1) + g) * STATE
            parts += list(fluxes(again[start : start + STATE, :], triple))
        flat.append(jnp.concatenate(parts, axis=1))
    damped = divergence_joined(jnp.concatenate(flat, axis=0), div_hi_ref, div_lo_ref)

    ordered = []
    for r in range(2, 6):
        straight = joined(direct, 32, r, 0, 24)
        carried = joined(spread, 56, r, STATE, 16)
        damping = rows_joined(
            damped[(r - 2) * STATE : (r - 1) * STATE, :],
            damped[(r - 1) * STATE : r * STATE, :],
            damped[r * STATE : (r + 1) * STATE, :],
            low_mask,
            high_mask,
        )
        for g in range(2):
            change = (
                TIME_STEP * jnp.concatenate([straight[g], -carried[g]], axis=0)
                - (TIME_STEP * HYPER_NU) * damping[g]
            )
            scale = jnp.concatenate([inverse[r, g]] * FIELDS, axis=0)
            ordered.append(tile(r, g, 0, STATE) + change * scale)
    whole = jnp.concatenate(ordered, axis=1)
    upper, lower = halves(whole)
    hits = (row_iota((1024, POINTS_DEV)) == place_ref[0:1, :]).astype(F32).astype(BF16)
    updated = dot(upper, hits) + dot(lower, hits)
    updated_ref[...] = updated

    columns = []
    picks = []
    for k in range(3):
        pieces = []
        if k > 0:
            pieces.append(jnp.zeros((STATE * k, POINTS_DEV), F32))
        pieces.append(updated)
        if k < 2:
            pieces.append(jnp.zeros((STATE * (2 - k), POINTS_DEV), F32))
        slot_row = jnp.where(
            row_iota((8, POINTS_DEV)) == k, jnp.broadcast_to(map_ref[3:4, :], (8, POINTS_DEV)), 0.0
        )
        columns.append(jnp.concatenate(pieces + [slot_row], axis=0))
        line = map_ref[k : k + 1, :].astype(jnp.int32)
        picks.append((row_iota((POINTS_DEV, POINTS_DEV)) == line).astype(F32).astype(BF16))
    upper, lower = halves(jnp.concatenate(columns, axis=1))
    sent = dot_last(jnp.concatenate(picks, axis=1), jnp.concatenate([upper, lower], axis=0))
    send_ref[...] = sent[:, :LANES] + sent[:, LANES:]


def receive_kernel(received_ref, physics_ref):
    turned_over = received_ref[...].T
    values = jnp.concatenate(
        [turned_over[STATE * k : STATE * (k + 1), :] for k in range(3)], axis=1
    )
    first = values.astype(BF16).astype(F32)
    both = jnp.concatenate([first, values - first], axis=0).astype(BF16)
    hits = []
    for k in range(3):
        slot = turned_over[3 * STATE + k : 3 * STATE + k + 1, :].astype(jnp.int32) - 1
        hits.append((row_iota((POINTS_DEV, POINTS_DEV)) == slot).astype(F32).astype(BF16))
    placed = dot_last(both, jnp.concatenate(hits, axis=1))
    physics_ref[...] = placed[:STATE] + placed[STATE:]


def call(kernel, shapes, scratch=(), flops=0, moved=0):
    single = not isinstance(shapes, list)
    outs = [jax.ShapeDtypeStruct(s, d) for s, d in ([shapes] if single else shapes)]
    return pl.pallas_call(
        kernel,
        out_shape=outs[0] if single else outs,
        scratch_shapes=list(scratch),
        compiler_params=pltpu.CompilerParams(vmem_limit_bytes=VMEM_LIMIT),
        cost_estimate=pl.CostEstimate(flops=flops, bytes_accessed=moved, transcendentals=0),
    )


def ring(axis, by):
    count = lax.axis_size(axis)
    return [(i, (i + by) % count) for i in range(count)]


def open_line(axis, by):
    count = lax.axis_size(axis)
    return [(i, i + by) for i in range(count) if 0 <= i + by < count]


def body(
    evolving_state_array, point_id, neighbours, jacobian, inverse_metric, coriolis, column_slot
):
    state = evolving_state_array.reshape(STATE, POINTS_DEV)
    geo = jnp.concatenate(
        [jacobian[None], coriolis[None], inverse_metric, jnp.zeros((2, POINTS_DEV), F32)], axis=0
    )
    half = ((4 * TILE, LANES), F32)
    strip = ((TILE, LANES), F32)
    low, high, to_right, to_left, place = call(
        arrange_kernel, [half, half, strip, strip, ((8, POINTS_DEV), jnp.int32)]
    )(state, geo, neighbours)
    from_left = lax.ppermute(to_right, "col", ring("col", 1))
    from_right = lax.ppermute(to_left, "col", ring("col", -1))
    sends = call(send_kernel, ((8, POINTS_DEV), F32))(column_slot[None])
    low, high = call(margin_kernel, [half, half])(low, high, from_left, from_right)
    below = lax.ppermute(high, "curve", open_line("curve", 1))
    above = lax.ppermute(low, "curve", open_line("curve", -1))
    updated, sent = call(
        section_kernel,
        [((STATE, POINTS_DEV), F32), ((POINTS_DEV, LANES), F32)],
        scratch=[
            pltpu.VMEM((16 * TILE, 2 * LANES), F32),
            pltpu.VMEM((8 * 56, 4 * LANES), F32),
            pltpu.VMEM((8 * 32, 2 * LANES), F32),
            pltpu.VMEM((16 * 24, LANES), F32),
        ],
    )(below, low, high, above, place, sends, *[jnp.asarray(m) for m in operators()])
    received = lax.all_to_all(sent, "col", split_axis=0, concat_axis=0, tiled=True)
    physics = call(receive_kernel, ((STATE, POINTS_DEV), F32))(received)
    shape = evolving_state_array.shape
    return updated.reshape(shape), physics.reshape(shape)


def solution(mesh):
    split = ("curve", "col")
    return jax.shard_map(
        body,
        mesh=mesh,
        in_specs=(
            P(None, None, split),
            P(split),
            P(None, split),
            P(split),
            P(None, split),
            P(split),
            P(split),
        ),
        out_specs=(P(None, None, split), P(None, None, split)),
        check_vma=False,
    )
```

profile of v0, /device:TPU:6, one launch (start us, length us, event | category | flops | bytes accessed | tf_op | source)
XLA Modules:
  0.0 83.3 jit_solution(14362715027706646329)
XLA Ops:
  0.6 0.0 copy-start
  0.6 0.7 broadcast_in_dim.12
  1.4 0.7 broadcast_in_dim.13
  2.1 0.1 pad.3.clone
  2.1 0.8 maximum_maximum_fusion.geo_ref
  2.9 0.0 copy-start.4
  2.9 0.9 %copy-done.4 = f32[5,8,768]{2,1,0:T(8,128)S(1)} copy-done((f32[5,8,768]{2,1,0:T(8,128)S(1)}, f32[5,8,768]{2,1,0:T(8,128)}, u32[]{:S(2)}) %copy-start.4) | copy-done | bytes 122904
  3.8 0.0 copy-start.7
  3.8 0.7 copy-done.7
  4.5 1.5 %shard_map.131 = (f32[192,128]{1,0:T(8,128)S(1)}, f32[192,128]{1,0:T(8,128)S(1)}, f32[48,128]{1,0:T(8,128)S(1)}, f32[48,128]{1,0:T(8,128)S(1)}, s32[8,768]{1,0:T(8,128)S(1)}) custom-call(f32[40,768]{1,0:T(8,128)S(1)} %bitcast.7, f32[8,768]{1,0:T(8,128)S(1)} %maximum_maximum_fusion.geo_ref, s32[8,48]{1,0:T(8,128)S(1)} %copy-done.7), custom_call_target="tpu_custom_call" | custom-call | tf_op jit(solution)/shard_map/pallas_call | solution.py:440
  6.0 1.9 %collective-permute-start = (f32[48,128]{1,0:T(8,128)S(1)}, f32[48,128]{1,0:T(8,128)S(1)}, u32[]{:S(2)}, u32[]{:S(2)}) collective-permute-start(f32[48,128]{1,0:T(8,128)S(1)} %get-tuple-element.13), channel_id=1, source_target_pairs={{0,1},{1,2},{2,3},{3,4},{4,5},{5,6},{6,7},{7,8},{8,9},{9,10},{10,1... | collective-permute-start | bytes 73736 | tf_op jit(solution)/shard_map/ppermute | solution.py:443
  7.9 17.5 %collective-permute-start.1 = (f32[48,128]{1,0:T(8,128)S(1)}, f32[48,128]{1,0:T(8,128)S(1)}, u32[]{:S(2)}, u32[]{:S(2)}) collective-permute-start(f32[48,128]{1,0:T(8,128)S(1)} %get-tuple-element.14), channel_id=1, source_target_pairs={{0,31},{1,0},{2,1},{3,2},{4,3},{5,4},{6,5},{7,6},{8,7},{9,8},{10,9... | collective-permute-start | bytes 73736 | tf_op jit(solution)/shard_map/ppermute | solution.py:444
  25.4 0.0 collective-permute-done.from_left
  25.4 1.5 %collective-permute-done.1.from_right = f32[48,128]{1,0:T(8,128)S(1)} collective-permute-done((f32[48,128]{1,0:T(8,128)S(1)}, f32[48,128]{1,0:T(8,128)S(1)}, u32[]{:S(2)}, u32[]{:S(2)}) %collective-permute-start.1) | collective-permute-done | bytes 24608 | tf_op jit(solution)/shard_map/ppermute | solution.py:444
  26.9 0.0 copy-start.8
  26.9 0.0 copy-start.2
  26.9 0.0 copy-start.5
  26.9 0.1 shard_map.132
  27.0 3.4 %collective-permute-start.2 = (f32[192,128]{1,0:T(8,128)S(1)}, f32[192,128]{1,0:T(8,128)S(1)}, u32[]{:S(2)}, u32[]{:S(2)}) collective-permute-start(f32[192,128]{1,0:T(8,128)S(1)} %get-tuple-element.15.high_ref), channel_id=1, source_target_pairs={{0,32},{32,64},{64,96},{96,128},{128,160},{160,192},{192,224},{224... | collective-permute-start | bytes 294920 | tf_op jit(solution)/shard_map/ppermute | solution.py:447
  30.4 8.2 %collective-permute-start.3 = (f32[192,128]{1,0:T(8,128)S(1)}, f32[192,128]{1,0:T(8,128)S(1)}, u32[]{:S(2)}, u32[]{:S(2)}) collective-permute-start(f32[192,128]{1,0:T(8,128)S(1)} %get-tuple-element.16.low_ref), channel_id=1, source_target_pairs={{32,0},{64,32},{96,64},{128,96},{160,128},{192,160},{224,192},{256... | collective-permute-start | bytes 294920 | tf_op jit(solution)/shard_map/ppermute | solution.py:448
  38.6 0.0 copy-done.8
  38.6 0.0 copy-start.6
  38.6 0.2 shard_map.133.map_ref
  38.9 0.5 collective-permute-done.2.below_ref
  39.4 1.4 %collective-permute-done.3.above_ref = f32[192,128]{1,0:T(8,128)S(1)} collective-permute-done((f32[192,128]{1,0:T(8,128)S(1)}, f32[192,128]{1,0:T(8,128)S(1)}, u32[]{:S(2)}, u32[]{:S(2)}) %collective-permute-start.3) | collective-permute-done | bytes 98336 | tf_op jit(solution)/shard_map/ppermute | solution.py:448
  40.8 0.0 copy-done
  40.8 0.0 copy-done.2
  40.8 0.0 copy-done.5
  40.8 0.0 copy-done.6
  40.8 0.0 copy-start.1
  40.8 0.9 %copy-done.1 = bf16[512,256]{1,0:T(8,128)(2,1)S(1)} copy-done((bf16[512,256]{1,0:T(8,128)(2,1)S(1)}, bf16[512,256]{1,0:T(8,128)(2,1)}, u32[]{:S(2)}) %copy-start.1) | copy-done | bytes 262168
  41.8 0.0 copy-start.3
  41.8 0.9 %copy-done.3 = bf16[256,256]{1,0:T(8,128)(2,1)S(1)} copy-done((bf16[256,256]{1,0:T(8,128)(2,1)S(1)}, bf16[256,256]{1,0:T(8,128)(2,1)}, u32[]{:S(2)}) %copy-start.3) | copy-done | bytes 131096
  42.7 4.2 %shard_map.134 = (f32[40,768]{1,0:T(8,128)}, f32[768,128]{1,0:T(8,128)S(1)}) custom-call(f32[192,128]{1,0:T(8,128)S(1)} %collective-permute-done.2.below_ref, f32[192,128]{1,0:T(8,128)S(1)} %get-tuple-element.16.low_ref, f32[192,128]{1,0:T(8,128)S(1)} %get-tuple-element.15.high_ref, f32[192,128]{1,0:T(8,128)S(1)} %collective-permute-done.3.above_ref, ...), custom_call_target="tpu_custom_call" | custom-call | tf_op jit(solution)/shard_map/pallas_call | solution.py:449
  46.9 34.5 %all_to_all.11 = f32[32,24,128]{2,1,0:T(8,128)S(1)} all-to-all(f32[32,24,128]{2,1,0:T(8,128)S(1)} %bitcast.6), channel_id=1, replica_groups=mesh['curve'=24,'col'=32] {'col'}, dimensions={0} | all-to-all | bytes 786432 | tf_op jit(solution)/shard_map/all_to_all | solution.py:459
  81.4 1.9 %shard_map.135 = f32[40,768]{1,0:T(8,128)} custom-call(f32[768,128]{1,0:T(8,128)S(1)} %bitcast.5), custom_call_target="tpu_custom_call" | custom-call | tf_op jit(solution)/shard_map/pallas_call | solution.py:460
  (2 shorter events, 0.0 us)
Async XLA Ops:
  0.6 40.2 %copy-start = (bf16[512,256]{1,0:T(8,128)(2,1)S(1)}, bf16[512,256]{1,0:T(8,128)(2,1)}, u32[]{:S(2)}) copy-start(bf16[512,256]{1,0:T(8,128)(2,1)} %constant.17.clone.div_lo_ref) | copy-start | bytes 786436
  2.9 0.9 %copy-start.4 = (f32[5,8,768]{2,1,0:T(8,128)S(1)}, f32[5,8,768]{2,1,0:T(8,128)}, u32[]{:S(2)}) copy-start(f32[5,8,768]{2,1,0:T(8,128)} %param.13) | copy-start | bytes 368644
  3.8 0.7 copy-start.7
  6.0 19.4 %collective-permute-start = (f32[48,128]{1,0:T(8,128)S(1)}, f32[48,128]{1,0:T(8,128)S(1)}, u32[]{:S(2)}, u32[]{:S(2)}) collective-permute-start(f32[48,128]{1,0:T(8,128)S(1)} %get-tuple-element.13), channel_id=1, source_target_pairs={{0,1},{1,2},{2,3},{3,4},{4,5},{5,6},{6,7},{7,8},{8,9},{9,10},{10,1... | collective-permute-start | bytes 73736 | tf_op jit(solution)/shard_map/ppermute | solution.py:443
  7.9 19.0 %collective-permute-start.1 = (f32[48,128]{1,0:T(8,128)S(1)}, f32[48,128]{1,0:T(8,128)S(1)}, u32[]{:S(2)}, u32[]{:S(2)}) collective-permute-start(f32[48,128]{1,0:T(8,128)S(1)} %get-tuple-element.14), channel_id=1, source_target_pairs={{0,31},{1,0},{2,1},{3,2},{4,3},{5,4},{6,5},{7,6},{8,7},{9,8},{10,9... | collective-permute-start | bytes 73736 | tf_op jit(solution)/shard_map/ppermute | solution.py:444
  26.9 11.7 %copy-start.8 = (s32[768]{0:T(1024)S(1)}, s32[768]{0:T(1024)}, u32[]{:S(2)}) copy-start(s32[768]{0:T(1024)} %param.18) | copy-start | bytes 9220
  26.9 13.9 %copy-start.2 = (bf16[256,256]{1,0:T(8,128)(2,1)S(1)}, bf16[256,256]{1,0:T(8,128)(2,1)}, u32[]{:S(2)}) copy-start(bf16[256,256]{1,0:T(8,128)(2,1)} %constant.18.clone.join_ref) | copy-start | bytes 393220
  26.9 13.9 %copy-start.5 = (bf16[128,256]{1,0:T(8,128)(2,1)S(1)}, bf16[128,256]{1,0:T(8,128)(2,1)}, u32[]{:S(2)}) copy-start(bf16[128,256]{1,0:T(8,128)(2,1)} %constant.15.clone.grad_lo_ref) | copy-start | bytes 196612
  27.0 12.3 %collective-permute-start.2 = (f32[192,128]{1,0:T(8,128)S(1)}, f32[192,128]{1,0:T(8,128)S(1)}, u32[]{:S(2)}, u32[]{:S(2)}) collective-permute-start(f32[192,128]{1,0:T(8,128)S(1)} %get-tuple-element.15.high_ref), channel_id=1, source_target_pairs={{0,32},{32,64},{64,96},{96,128},{128,160},{160,192},{192,224},{224... | collective-permute-start | bytes 294920 | tf_op jit(solution)/shard_map/ppermute | solution.py:447
  30.4 10.4 %collective-permute-start.3 = (f32[192,128]{1,0:T(8,128)S(1)}, f32[192,128]{1,0:T(8,128)S(1)}, u32[]{:S(2)}, u32[]{:S(2)}) collective-permute-start(f32[192,128]{1,0:T(8,128)S(1)} %get-tuple-element.16.low_ref), channel_id=1, source_target_pairs={{32,0},{64,32},{96,64},{128,96},{160,128},{192,160},{224,192},{256... | collective-permute-start | bytes 294920 | tf_op jit(solution)/shard_map/ppermute | solution.py:448
  38.6 2.2 %copy-start.6 = (f32[8,128]{1,0:T(8,128)S(1)}, f32[8,128]{1,0:T(8,128)}, u32[]{:S(2)}) copy-start(f32[8,128]{1,0:T(8,128)} %constant.19.clone.weight_ref) | copy-start | bytes 12292
  40.8 1.0 %copy-start.1 = (bf16[512,256]{1,0:T(8,128)(2,1)S(1)}, bf16[512,256]{1,0:T(8,128)(2,1)}, u32[]{:S(2)}) copy-start(bf16[512,256]{1,0:T(8,128)(2,1)} %constant.16.clone.div_hi_ref) | copy-start | bytes 786436
  41.8 0.9 %copy-start.3 = (bf16[256,256]{1,0:T(8,128)(2,1)S(1)}, bf16[256,256]{1,0:T(8,128)(2,1)}, u32[]{:S(2)}) copy-start(bf16[256,256]{1,0:T(8,128)(2,1)} %constant.14.clone.grad2_ref) | copy-start | bytes 393220
where the time goes:
time: 84.7 us; the launch traced here: 83.3 us
  blocking collectives  34.5 us (41%)
  starting transfers between devices  31 us (37%)
  Pallas kernels  7.9 us (9%)
  local copies, waits for them, and re-layouts  4.97 us (6%)
  waiting for transfers between devices  3.44 us (4%)
    all_to_all x1, blocking collectives, body(): lax.all_to_all(sent, 'col', split_axis=0, concat_axis=0, tiled=True)  34.5 us
    ppermute x1, starting transfers between devices, body(): from_right = lax.ppermute(to_left, 'col', ring('col', -1))  17.5 us
    ppermute x1, starting transfers between devices, body(): above = lax.ppermute(low, 'curve', open_line('curve', -1))  8.17 us
    pallas_call x1, Pallas kernels, body(): call(section_kernel, [((STATE, POINTS_DEV), F32), ((POINTS_DEV, LANES), F...  4.24 us
    unnamed x18, local copies, waits for them, and re-layouts  3.46 us
    ppermute x1, starting transfers between devices, body(): below = lax.ppermute(high, 'curve', open_line('curve', 1))  3.38 us
    ppermute x1, starting transfers between devices, body(): from_left = lax.ppermute(to_right, 'col', ring('col', 1))  1.92 us
    pallas_call x1, Pallas kernels, body(): physics = call(receive_kernel, ((STATE, POINTS_DEV), F32))(received)  1.87 us
  transfers between devices with their start and end apart: 4, of which 3 were waited for; matrix products, arithmetic and copies ran while one was open for 0% of the time, Pallas kernels for 0%

commit v1 on v0

--- a/solution.py
+++ b/solution.py
@@ -23,7 +23,7 @@
 HYPER_NU = 0.002
 F32 = jnp.float32
 BF16 = jnp.bfloat16
-VMEM_LIMIT = 48 * 1024 * 1024
+VMEM_LIMIT = 32 * 1024 * 1024
 
 
 def gll_tables():
@@ -104,11 +104,18 @@
     return lax.broadcasted_iota(jnp.int32, shape, 0)
 
 
+def one_step(local, index):
+    hit = (row_iota((ELEMS_DEV, ELEMS_DEV)) == index) & local
+    return hit.astype(F32).astype(BF16)
+
+
+def wide(local):
+    return jnp.broadcast_to(local.astype(F32), (8, ELEMS_DEV))
+
+
 def chain_length(local, index, doublings):
-    present = jnp.broadcast_to(local.astype(F32), (8, ELEMS_DEV))
-    hit = (row_iota((ELEMS_DEV, ELEMS_DEV)) == index) & local
-    step = hit.astype(F32).astype(BF16)
-    length = present
+    length = wide(local)
+    step = one_step(local, index)
     for k in range(doublings):
         length = length + dot(length.astype(BF16), step)
         if k + 1 < doublings:
@@ -116,42 +123,98 @@
     return length
 
 
-def arrange_kernel(state_ref, geo_ref, near_ref, low_ref, high_ref, right_ref, left_ref, place_ref):
+def local_lists(near):
     base = (lax.axis_index("curve") * N_COL + lax.axis_index("col")) * ELEMS_DEV
-    index = near_ref[...] - base
-    local = (index >= 0) & (index < ELEMS_DEV)
+    index = near - base
+    return index, (index >= 0) & (index < ELEMS_DEV)
+
+
+def over_points(element_values):
+    shape = (ELEMS_DEV, POINTS_DEV)
+    spread = (lane_iota(shape) // 16 == row_iota(shape)).astype(F32).astype(BF16)
+    return dot(element_values.astype(BF16), spread)[0:1].astype(jnp.int32)
+
+
+def three_parts(value):
+    first = value.astype(BF16)
+    rest = value - first.astype(F32)
+    second = rest.astype(BF16)
+    return first, second, (rest - second.astype(F32)).astype(BF16)
+
+
+def strip_kernel(
+    state_ref, jacobian_ref, coriolis_ref, metric_ref, near_ref, far_ref, close_ref, values_ref,
+    near, jac, cor, metric, state, sems
+):
+    copies = [
+        pltpu.make_async_copy(source, target, sems.at[i])
+        for i, (source, target) in enumerate(
+            [
+                (near_ref, near),
+                (state_ref, state),
+                (jacobian_ref, jac),
+                (coriolis_ref, cor),
+                (metric_ref, metric),
+            ]
+        )
+    ]
+    for copy in copies:
+        copy.start()
+    copies[0].wait()
+    index, local = local_lists(near[...])
+    row = chain_length(local[2:3], index[2:3], 2)
+    sides = []
+    for side in range(2):
+        here, there = local[side : side + 1], index[side : side + 1]
+        second = dot(wide(here).astype(BF16), one_step(here, there))
+        edge = wide(~here)
+        sides.append((edge, wide(here) * (1.0 - second)))
+    (first, second), (last, second_last) = sides
+    unit = (first + second) * (2.0 * row + 1.0 + second)
+    unit = unit + (last + second_last) * (2.0 * row + 9.0 + last)
+    lane = (over_points(unit) - 1) * 16 + lane_iota((1, POINTS_DEV)) % 16
+    hits = (row_iota((2 * LANES, POINTS_DEV)) == lane).astype(F32).astype(BF16)
+    for copy in copies[1:]:
+        copy.wait()
+    values = jnp.concatenate(
+        [
+            state[...].reshape(STATE, POINTS_DEV),
+            jac[...].reshape(1, POINTS_DEV),
+            cor[...].reshape(1, POINTS_DEV),
+            metric[...],
+            jnp.zeros((2, POINTS_DEV), F32),
+        ],
+        axis=0,
+    )
+    values_ref[...] = values
+    parts = dot_last(jnp.concatenate(three_parts(values), axis=0), hits)
+    strips = parts[0:TILE] + parts[TILE : 2 * TILE] + parts[2 * TILE :]
+    even = lax.rem(lax.axis_index("col"), 2) == 0
+    to_left, to_right = strips[:, :LANES], strips[:, LANES:]
+    far_ref[...] = jnp.where(even, to_left, to_right)
+    close_ref[...] = jnp.where(even, to_right, to_left)
+
+
+def arrange_kernel(values_ref, near_ref, slot_ref, low_ref, high_ref, place_ref, lists_ref):
+    index, local = local_lists(near_ref[...])
     place = chain_length(local[0:1], index[0:1], 4)
     row = chain_length(local[2:3], index[2:3], 2)
-    spot = row * 16.0 + place + 2.0
-    points = (ELEMS_DEV, POINTS_DEV)
-    spread = (lane_iota(points) // 16 == row_iota(points)).astype(F32).astype(BF16)
-    spot_of_point = dot(spot.astype(BF16), spread)[0:1].astype(jnp.int32)
-    target = spot_of_point * 16 + lane_iota((1, POINTS_DEV)) % 16
+    target = over_points(row * 16.0 + place + 2.0) * 16 + lane_iota((1, POINTS_DEV)) % 16
     place_ref[...] = jnp.broadcast_to(target, (8, POINTS_DEV))
     hits = (row_iota((1024, POINTS_DEV)) == target).astype(F32).astype(BF16)
-    values = jnp.concatenate([state_ref[...], geo_ref[...]], axis=0)
-    first = values.astype(BF16)
-    rest = values - first.astype(F32)
-    second = rest.astype(BF16)
-    third = (rest - second.astype(F32)).astype(BF16)
-    parts = dot_last(jnp.concatenate([first, second, third], axis=0), hits)
-    ordered = parts[0:TILE] + parts[TILE : 2 * TILE] + parts[2 * TILE :]
-    lane = lane_iota((TILE, LANES))
-    to_right = jnp.zeros((TILE, LANES), F32)
-    to_left = jnp.zeros((TILE, LANES), F32)
+    columns = send_lists(slot_ref[...])
+    left = jnp.concatenate(three_parts(values_ref[...]), axis=0)
+    upper, rest = halves(columns)
+    left = jnp.concatenate([left, jnp.concatenate([columns, columns - upper.astype(F32)], axis=0).astype(BF16)], axis=0)
+    parts = dot_last(left, hits)
+    ordered = parts[0:TILE] + parts[TILE : 2 * TILE] + parts[2 * TILE : 3 * TILE]
     for r in range(4):
         for g in range(2):
             block = ordered[:, (2 * r + g) * LANES : (2 * r + g + 1) * LANES]
             ref = low_ref if r < 2 else high_ref
             start = ((r % 2) * 2 + g) * TILE
             ref[start : start + TILE, :] = block
-            inside = (lane >= 32 * r) & (lane < 32 * r + 32)
-            if g == 1:
-                to_right = jnp.where(inside, turned(block, 32 * r - 64), to_right)
-            else:
-                to_left = jnp.where(inside, turned(block, 32 * r - 32), to_left)
-    right_ref[...] = to_right
-    left_ref[...] = to_left
+    lists_ref[...] = parts[3 * TILE : 3 * TILE + 8] + parts[3 * TILE + 8 :]
 
 
 def turned(block, by):
@@ -159,23 +222,34 @@
     return block if by == 0 else pltpu.roll(block, by, 1)
 
 
-def margin_kernel(low_in, high_in, from_left, from_right, low_ref, high_ref):
+def margin_kernel(low_in, high_in, from_far, from_close, first_ref, second_ref):
     lane = lane_iota((TILE, LANES))
-    for r in range(4):
-        source = low_in if r < 2 else high_in
-        ref = low_ref if r < 2 else high_ref
-        start = (r % 2) * 2 * TILE
-        first = source[start : start + TILE, :]
-        ref[start : start + TILE, :] = jnp.where(lane < 32, turned(from_left[...], -32 * r), first)
-        start += TILE
-        second = source[start : start + TILE, :]
-        ref[start : start + TILE, :] = jnp.where(
-            lane >= 96, turned(from_right[...], 96 - 32 * r), second
-        )
-
-
-def send_kernel(slot_ref, map_ref):
-    slot = slot_ref[...]
+    even = lax.rem(lax.axis_index("col"), 2) == 0
+    from_left = jnp.where(even, from_far[...], from_close[...])
+    from_right = jnp.where(even, from_close[...], from_far[...])
+    halves_of_rows = []
+    for source, start_row in ((low_in, 0), (high_in, 2)):
+        blocks = []
+        for r in range(2):
+            turn = start_row + r
+            start = r * 2 * TILE
+            blocks.append(
+                jnp.where(lane < 32, turned(from_left, -32 * turn), source[start : start + TILE, :])
+            )
+            start += TILE
+            blocks.append(
+                jnp.where(
+                    lane >= 96, turned(from_right, 96 - 32 * turn), source[start : start + TILE, :]
+                )
+            )
+        halves_of_rows.append(jnp.concatenate(blocks, axis=0))
+    low, high = halves_of_rows
+    even = lax.rem(lax.axis_index("curve"), 2) == 0
+    first_ref[...] = jnp.where(even, high, low)
+    second_ref[...] = jnp.where(even, low, high)
+
+
+def send_lists(slot):
     slot_value = slot.astype(F32)
     device = jnp.floor((slot_value + 0.5) * (1.0 / POINTS_DEV))
     within = slot_value - device * POINTS_DEV
@@ -199,9 +273,26 @@
     rank = jnp.concatenate(ranks, axis=1) - 1.0
     third = (rank >= CAP_ROWS).astype(F32) + (rank >= 2 * CAP_ROWS).astype(F32)
     line = device * CAP_ROWS + rank - third * CAP_ROWS
-    lists = [jnp.where(third == float(k), line, -1.0) for k in range(3)]
+    lists = [jnp.where(third == float(k), line + 1.0, 0.0) for k in range(3)]
     filler = jnp.zeros((4, POINTS_DEV), F32)
-    map_ref[...] = jnp.concatenate(lists + [within + 1.0, filler], axis=0)
+    return jnp.concatenate(lists + [within + 1.0, filler], axis=0)
+
+
+def pick_kernel(lists_ref, *refs):
+    count = len(refs) // 2
+    sources, (picks_ref, *targets), sems = refs[: count - 1], refs[count - 1 : -1], refs[-1]
+    copies = [
+        pltpu.make_async_copy(source, target, sems.at[i])
+        for i, (source, target) in enumerate(zip(sources, targets))
+    ]
+    for copy in copies:
+        copy.start()
+    shape = (POINTS_DEV, 1024)
+    for k in range(3):
+        line = lists_ref[k : k + 1, :].astype(jnp.int32) - 1
+        picks_ref[:, k * 1024 : (k + 1) * 1024] = (row_iota(shape) == line).astype(F32).astype(BF16)
+    for copy in copies:
+        copy.wait()
 
 
 def fluxes(slope, coefficients):
@@ -235,30 +326,35 @@
 
 
 def section_kernel(
-    below_ref,
-    low_ref,
-    high_ref,
-    above_ref,
-    place_ref,
-    map_ref,
+    first_far_ref,
+    first_ref,
+    second_ref,
+    second_far_ref,
+    lists_ref,
+    picks_ref,
     grad2_ref,
     grad_lo_ref,
     div_hi_ref,
     div_lo_ref,
     join_ref,
     weight_ref,
-    updated_ref,
+    whole_ref,
     send_ref,
+    quarters,
     slopes,
     flux,
     plain,
     coefs,
 ):
-    quarters = (below_ref, low_ref, high_ref, above_ref)
+    even = lax.rem(lax.axis_index("curve"), 2) == 0
+    quarters[0] = jnp.where(even, second_far_ref[...], first_far_ref[...])
+    quarters[1] = jnp.where(even, second_ref[...], first_ref[...])
+    quarters[2] = jnp.where(even, first_ref[...], second_ref[...])
+    quarters[3] = jnp.where(even, first_far_ref[...], second_far_ref[...])
 
     def tile(r, g, start=0, size=TILE):
         offset = ((r % 2) * 2 + g) * TILE + start
-        return quarters[r // 2][offset : offset + size, :]
+        return quarters[r // 2, offset : offset + size, :]
 
     cells = [(r, g) for r in range(8) for g in range(2)]
     stacked = []
@@ -366,29 +462,28 @@
             scale = jnp.concatenate([inverse[r, g]] * FIELDS, axis=0)
             ordered.append(tile(r, g, 0, STATE) + change * scale)
     whole = jnp.concatenate(ordered, axis=1)
-    upper, lower = halves(whole)
-    hits = (row_iota((1024, POINTS_DEV)) == place_ref[0:1, :]).astype(F32).astype(BF16)
-    updated = dot(upper, hits) + dot(lower, hits)
-    updated_ref[...] = updated
-
+    whole_ref[...] = whole
     columns = []
-    picks = []
     for k in range(3):
         pieces = []
         if k > 0:
-            pieces.append(jnp.zeros((STATE * k, POINTS_DEV), F32))
-        pieces.append(updated)
+            pieces.append(jnp.zeros((STATE * k, 1024), F32))
+        pieces.append(whole)
         if k < 2:
-            pieces.append(jnp.zeros((STATE * (2 - k), POINTS_DEV), F32))
+            pieces.append(jnp.zeros((STATE * (2 - k), 1024), F32))
         slot_row = jnp.where(
-            row_iota((8, POINTS_DEV)) == k, jnp.broadcast_to(map_ref[3:4, :], (8, POINTS_DEV)), 0.0
+            row_iota((8, 1024)) == k, jnp.broadcast_to(lists_ref[3:4, :], (8, 1024)), 0.0
         )
         columns.append(jnp.concatenate(pieces + [slot_row], axis=0))
-        line = map_ref[k : k + 1, :].astype(jnp.int32)
-        picks.append((row_iota((POINTS_DEV, POINTS_DEV)) == line).astype(F32).astype(BF16))
     upper, lower = halves(jnp.concatenate(columns, axis=1))
-    sent = dot_last(jnp.concatenate(picks, axis=1), jnp.concatenate([upper, lower], axis=0))
+    sent = dot_last(picks_ref[...], jnp.concatenate([upper, lower], axis=0))
     send_ref[...] = sent[:, :LANES] + sent[:, LANES:]
+
+
+def restore_kernel(whole_ref, place_ref, updated_ref):
+    first, second, third = three_parts(whole_ref[...])
+    hits = (row_iota((1024, POINTS_DEV)) == place_ref[0:1, :]).astype(F32).astype(BF16)
+    updated_ref[...] = dot(first, hits) + dot(second, hits) + dot(third, hits)
 
 
 def receive_kernel(received_ref, physics_ref):
@@ -406,58 +501,83 @@
     physics_ref[...] = placed[:STATE] + placed[STATE:]
 
 
-def call(kernel, shapes, scratch=(), flops=0, moved=0):
-    single = not isinstance(shapes, list)
-    outs = [jax.ShapeDtypeStruct(s, d) for s, d in ([shapes] if single else shapes)]
+def call(kernel, shapes, scratch=(), flops=0, moved=0, vmem=VMEM_LIMIT, **specs):
     return pl.pallas_call(
         kernel,
-        out_shape=outs[0] if single else outs,
+        out_shape=[jax.ShapeDtypeStruct(s, d) for s, d in shapes],
         scratch_shapes=list(scratch),
-        compiler_params=pltpu.CompilerParams(vmem_limit_bytes=VMEM_LIMIT),
+        **specs,
+        compiler_params=pltpu.CompilerParams(vmem_limit_bytes=vmem),
         cost_estimate=pl.CostEstimate(flops=flops, bytes_accessed=moved, transcendentals=0),
     )
 
 
-def ring(axis, by):
-    count = lax.axis_size(axis)
-    return [(i, (i + by) % count) for i in range(count)]
-
-
-def open_line(axis, by):
-    count = lax.axis_size(axis)
-    return [(i, i + by) for i in range(count) if 0 <= i + by < count]
+def swaps(count, pairs_from):
+    route = []
+    for i in range(pairs_from, count - 1, 2):
+        route += [(i, i + 1), (i + 1, i)]
+    return route
 
 
 def body(
     evolving_state_array, point_id, neighbours, jacobian, inverse_metric, coriolis, column_slot
 ):
-    state = evolving_state_array.reshape(STATE, POINTS_DEV)
-    geo = jnp.concatenate(
-        [jacobian[None], coriolis[None], inverse_metric, jnp.zeros((2, POINTS_DEV), F32)], axis=0
-    )
+    anywhere = pl.BlockSpec(memory_space=pltpu.HBM)
+    vmem = pl.BlockSpec(memory_space=pltpu.VMEM)
     half = ((4 * TILE, LANES), F32)
     strip = ((TILE, LANES), F32)
-    low, high, to_right, to_left, place = call(
-        arrange_kernel, [half, half, strip, strip, ((8, POINTS_DEV), jnp.int32)]
-    )(state, geo, neighbours)
-    from_left = lax.ppermute(to_right, "col", ring("col", 1))
-    from_right = lax.ppermute(to_left, "col", ring("col", -1))
-    sends = call(send_kernel, ((8, POINTS_DEV), F32))(column_slot[None])
-    low, high = call(margin_kernel, [half, half])(low, high, from_left, from_right)
-    below = lax.ppermute(high, "curve", open_line("curve", 1))
-    above = lax.ppermute(low, "curve", open_line("curve", -1))
-    updated, sent = call(
+    values_shape = ((TILE, POINTS_DEV), F32)
+    far, close, values = call(
+        strip_kernel,
+        [strip, strip, values_shape],
+        scratch=[
+            pltpu.VMEM((8, ELEMS_DEV), jnp.int32),
+            pltpu.VMEM((POINTS_DEV,), F32),
+            pltpu.VMEM((POINTS_DEV,), F32),
+            pltpu.VMEM((4, POINTS_DEV), F32),
+            pltpu.VMEM((FIELDS, LEV, POINTS_DEV), F32),
+            pltpu.SemaphoreType.DMA((5,)),
+        ],
+        in_specs=[anywhere] * 5,
+        vmem=64 * 1024 * 1024 - 524288,
+    )(evolving_state_array, jacobian, coriolis, inverse_metric, neighbours)
+    cols, rows = lax.axis_size("col"), lax.axis_size("curve")
+    from_far = lax.ppermute(far, "col", swaps(cols, 1) + [(cols - 1, 0), (0, cols - 1)])
+    from_close = lax.ppermute(close, "col", swaps(cols, 0))
+    low, high, place, lists = call(
+        arrange_kernel,
+        [half, half, ((8, POINTS_DEV), jnp.int32), ((8, 1024), F32)],
+        flops=400_000_000,
+        moved=1_000_000,
+    )(values, neighbours, column_slot[None])
+    first, second = call(margin_kernel, [half, half])(low, high, from_far, from_close)
+    second_far = lax.ppermute(second, "curve", swaps(rows, 1))
+    first_far = lax.ppermute(first, "curve", swaps(rows, 0))
+    matrices = [jnp.asarray(m) for m in operators()]
+    picks, *matrices = call(
+        pick_kernel,
+        [((POINTS_DEV, 3 * 1024), BF16)] + [(m.shape, m.dtype) for m in matrices],
+        scratch=[pltpu.SemaphoreType.DMA((len(matrices),))],
+        in_specs=[vmem] + [anywhere] * len(matrices),
+        flops=400_000_000,
+        moved=1_000_000,
+    )(lists, *matrices)
+    whole, sent = call(
         section_kernel,
-        [((STATE, POINTS_DEV), F32), ((POINTS_DEV, LANES), F32)],
+        [((STATE, 1024), F32), ((POINTS_DEV, LANES), F32)],
         scratch=[
+            pltpu.VMEM((4, 4 * TILE, LANES), F32),
             pltpu.VMEM((16 * TILE, 2 * LANES), F32),
             pltpu.VMEM((8 * 56, 4 * LANES), F32),
             pltpu.VMEM((8 * 32, 2 * LANES), F32),
             pltpu.VMEM((16 * 24, LANES), F32),
         ],
-    )(below, low, high, above, place, sends, *[jnp.asarray(m) for m in operators()])
+    )(first_far, first, second, second_far, lists, picks, *matrices)
     received = lax.all_to_all(sent, "col", split_axis=0, concat_axis=0, tiled=True)
-    physics = call(receive_kernel, ((STATE, POINTS_DEV), F32))(received)
+    (updated,) = call(
+        restore_kernel, [((STATE, POINTS_DEV), F32)], flops=400_000_000, moved=1_000_000
+    )(whole, place)
+    (physics,) = call(receive_kernel, [((STATE, POINTS_DEV), F32)])(received)
     shape = evolving_state_array.shape
     return updated.reshape(shape), physics.reshape(shape)
 

time: 84.7 us -> 80.6 us (0.952)
  blocking collectives: 34.5 us -> 0 us
  waiting for transfers between devices: 3.44 us -> 18.6 us
  starting transfers between devices: 31 us -> 39.6 us
  Pallas kernels: 7.9 us -> 13.2 us
  local copies, waits for them, and re-layouts: 4.97 us -> 7.52 us
    all_to_all x1 -> x0, blocking collectives: 34.5 us -> none  [body(): lax.all_to_all(sent, 'col', split_axis=0, concat_axis=0, tiled=True)]
    all_to_all x0 -> x1, waiting for transfers between devices: none -> 18.6 us  [body(): lax.all_to_all(sent, 'col', split_axis=0, concat_axis=0, tiled=True)]
    all_to_all x0 -> x1, starting transfers between devices: none -> 9.86 us  [body(): lax.all_to_all(sent, 'col', split_axis=0, concat_axis=0, tiled=True)]
    pallas_call x5 -> x7, Pallas kernels: 7.9 us -> 13.2 us  [the longest x1 4.56 us: body(): call(section_kernel, [((STATE, 1024), F32), ((POINTS_DEV, LANES), F32)],...]
    ppermute x4, waiting for transfers between devices: 3.44 us -> 0.01 us  [the longest x1 0.01 us: body(): from_close = lax.ppermute(close, 'col', swaps(cols, 0))]
    unnamed x18 -> x16, local copies, waits for them, and re-layouts: 3.46 us -> 6.82 us
    ppermute x4, starting transfers between devices: 31 us -> 29.8 us  [the longest x1 17.5 us: body(): lax.ppermute(far, 'col', swaps(cols, 1) + [(cols - 1, 0), (0, cols - 1)])]
  transfers between devices with their start and end apart: 4 -> 5, of which waited for: 3 -> 1; matrix products, arithmetic and copies ran while one was open for 0% -> 1% of each run, Pallas kernels for 0% -> 6%
where the time goes in v1:
time: 80.6 us; the launch traced here: 79.7 us
  starting transfers between devices  39.6 us (49%)
  waiting for transfers between devices  18.6 us (23%)
  Pallas kernels  13.2 us (16%)
  local copies, waits for them, and re-layouts  7.52 us (9%)
    all_to_all x1, waiting for transfers between devices, body(): lax.all_to_all(sent, 'col', split_axis=0, concat_axis=0, tiled=True)  18.6 us
    ppermute x1, starting transfers between devices, body(): lax.ppermute(far, 'col', swaps(cols, 1) + [(cols - 1, 0), (0, cols - 1)])  17.5 us
    all_to_all x1, starting transfers between devices, body(): lax.all_to_all(sent, 'col', split_axis=0, concat_axis=0, tiled=True)  9.86 us
    ppermute x1, starting transfers between devices, body(): second_far = lax.ppermute(second, 'curve', swaps(rows, 1))  6.97 us
    unnamed x16, local copies, waits for them, and re-layouts  6.82 us
    pallas_call x1, Pallas kernels, body(): call(section_kernel, [((STATE, 1024), F32), ((POINTS_DEV, LANES), F32)],...  4.56 us
    ppermute x1, starting transfers between devices, body(): first_far = lax.ppermute(first, 'curve', swaps(rows, 0))  3.38 us
    pallas_call x1, Pallas kernels, body(): call(strip_kernel, [strip, strip, values_shape], scratch=[pltpu.VMEM((8,...  2.2 us
  transfers between devices with their start and end apart: 5, of which 1 were waited for; matrix products, arithmetic and copies ran while one was open for 1% of the time, Pallas kernels for 6%

profile of v1, /device:TPU:6, one launch (start us, length us, event | category | flops | bytes accessed | tf_op | source)
XLA Modules:
  0.0 79.7 jit_solution(6997150382256185731)
XLA Ops:
  0.6 2.2 %shard_map.131 = (f32[48,128]{1,0:T(8,128)}, f32[48,128]{1,0:T(8,128)}, f32[48,768]{1,0:T(8,128)}) custom-call(f32[5,8,768]{2,1,0:T(8,128)} %state_ref.1, f32[768]{0:T(1024)} %jacobian_ref.1, f32[768]{0:T(1024)} %coriolis_ref.1, f32[4,768]{1,0:T(4,128)} %metric_ref.1, s32[8,48]{1,0:T(8,128)} %near_ref.3), custom_call_target="tpu_custom_call" | custom-call | tf_op jit(solution)/shard_map/pallas_call | solution.py:530
  2.8 17.5 %collective-permute-start = (f32[48,128]{1,0:T(8,128)}, f32[48,128]{1,0:T(8,128)S(1)}, u32[]{:S(2)}, u32[]{:S(2)}) collective-permute-start(f32[48,128]{1,0:T(8,128)} %get-tuple-element.23), channel_id=1, source_target_pairs={{1,2},{2,1},{3,4},{4,3},{5,6},{6,5},{7,8},{8,7},{9,10},{10,9},{11,... | collective-permute-start | bytes 73736 | tf_op jit(solution)/shard_map/ppermute | solution.py:545
  20.3 1.9 %collective-permute-start.1 = (f32[48,128]{1,0:T(8,128)}, f32[48,128]{1,0:T(8,128)S(1)}, u32[]{:S(2)}, u32[]{:S(2)}) collective-permute-start(f32[48,128]{1,0:T(8,128)} %get-tuple-element.24), channel_id=1, source_target_pairs={{0,1},{1,0},{2,3},{3,2},{4,5},{5,4},{6,7},{7,6},{8,9},{9,8},{10,11... | collective-permute-start | bytes 73736 | tf_op jit(solution)/shard_map/ppermute | solution.py:546
  22.3 0.7 broadcast_in_dim.3.slot_ref
  22.9 0.0 copy-start
  23.0 0.7 copy-done
  23.6 0.0 copy-start.1
  23.6 0.9 %copy-done.1 = f32[48,768]{1,0:T(8,128)S(1)} copy-done((f32[48,768]{1,0:T(8,128)S(1)}, f32[48,768]{1,0:T(8,128)}, u32[]{:S(2)}) %copy-start.1) | copy-done | bytes 147480
  24.5 1.4 %shard_map.132 = (f32[192,128]{1,0:T(8,128)S(1)}, f32[192,128]{1,0:T(8,128)S(1)}, s32[8,768]{1,0:T(8,128)S(1)}, f32[8,1024]{1,0:T(8,128)S(1)}) custom-call(f32[48,768]{1,0:T(8,128)S(1)} %copy-done.1, s32[8,48]{1,0:T(8,128)S(1)} %copy-done, s32[1,768]{1,0:T(1,128)S(1)} %broadcast_in_dim.3.slot_ref), custom_call_target="tpu_custom_call" | custom-call | flops 400000000 | bytes 1000000 | tf_op jit(solution)/shard_map/pallas_call | solution.py:547
  26.0 0.0 collective-permute-done.from_far
  26.0 0.0 collective-permute-done.1.from_close
  26.0 0.1 shard_map.133
  26.1 3.4 %collective-permute-start.2 = (f32[192,128]{1,0:T(8,128)S(1)}, f32[192,128]{1,0:T(8,128)S(1)}, u32[]{:S(2)}, u32[]{:S(2)}) collective-permute-start(f32[192,128]{1,0:T(8,128)S(1)} %get-tuple-element.25.first_ref), channel_id=1, source_target_pairs={{0,32},{32,0},{64,96},{96,64},{128,160},{160,128},{192,224},{224,1... | collective-permute-start | bytes 294920 | tf_op jit(solution)/shard_map/ppermute | solution.py:555
  29.5 7.0 %collective-permute-start.3 = (f32[192,128]{1,0:T(8,128)S(1)}, f32[192,128]{1,0:T(8,128)S(1)}, u32[]{:S(2)}, u32[]{:S(2)}) collective-permute-start(f32[192,128]{1,0:T(8,128)S(1)} %get-tuple-element.26.second_ref), channel_id=1, source_target_pairs={{32,64},{64,32},{96,128},{128,96},{160,192},{192,160},{224,256},{2... | collective-permute-start | bytes 294920 | tf_op jit(solution)/shard_map/ppermute | solution.py:554
  36.5 0.0 copy-start.2
  36.5 0.9 %copy-done.2 = bf16[512,256]{1,0:T(8,128)(2,1)S(1)} copy-done((bf16[512,256]{1,0:T(8,128)(2,1)S(1)}, bf16[512,256]{1,0:T(8,128)(2,1)}, u32[]{:S(2)}) %copy-start.2) | copy-done | bytes 262168
  37.4 0.0 copy-start.3
  37.4 0.9 %copy-done.3 = bf16[512,256]{1,0:T(8,128)(2,1)S(1)} copy-done((bf16[512,256]{1,0:T(8,128)(2,1)S(1)}, bf16[512,256]{1,0:T(8,128)(2,1)}, u32[]{:S(2)}) %copy-start.3) | copy-done | bytes 262168
  38.4 0.0 copy-start.4
  38.4 0.9 %copy-done.4 = bf16[256,256]{1,0:T(8,128)(2,1)S(1)} copy-done((bf16[256,256]{1,0:T(8,128)(2,1)S(1)}, bf16[256,256]{1,0:T(8,128)(2,1)}, u32[]{:S(2)}) %copy-start.4) | copy-done | bytes 131096
  39.3 0.0 copy-start.5
  39.3 0.9 %copy-done.5 = bf16[256,256]{1,0:T(8,128)(2,1)S(1)} copy-done((bf16[256,256]{1,0:T(8,128)(2,1)S(1)}, bf16[256,256]{1,0:T(8,128)(2,1)}, u32[]{:S(2)}) %copy-start.5) | copy-done | bytes 131096
  40.2 0.0 copy-start.6
  40.2 0.8 %copy-done.6 = bf16[128,256]{1,0:T(8,128)(2,1)S(1)} copy-done((bf16[128,256]{1,0:T(8,128)(2,1)S(1)}, bf16[128,256]{1,0:T(8,128)(2,1)}, u32[]{:S(2)}) %copy-start.6) | copy-done | bytes 65560
  41.0 0.0 copy-start.7
  41.0 0.7 copy-done.7
  41.7 1.4 %shard_map.134 = (bf16[768,3072]{1,0:T(8,128)(2,1)S(1)}, bf16[256,256]{1,0:T(8,128)(2,1)S(1)}, bf16[128,256]{1,0:T(8,128)(2,1)S(1)}, bf16[512,256]{1,0:T(8,128)(...) custom-call(f32[8,1024]{1,0:T(8,128)S(1)} %get-tuple-element.27.lists_ref, ...), custom_call_target="tpu_custom_call" | custom-call | flops 400000000 | bytes 1000000 | tf_op jit(solution)/shard_map/pallas_call | solution.py:557
  43.1 0.0 collective-permute-done.2.first_far_ref
  43.2 0.0 collective-permute-done.3.second_far_ref
  43.2 4.6 %shard_map.135 = (f32[40,1024]{1,0:T(8,128)S(1)}, f32[768,128]{1,0:T(8,128)}) custom-call(f32[192,128]{1,0:T(8,128)S(1)} %collective-permute-done.2.first_far_ref, f32[192,128]{1,0:T(8,128)S(1)} %get-tuple-element.25.first_ref, f32[192,128]{1,0:T(8,128)S(1)} %get-tuple-element.26.second_ref, f32[192,128]{1,0:T(8,128)S(1)} %collective-permute-done.3.second_far_ref, ...), custom_call_target="tpu_custom_call" | custom-call | tf_op jit(solution)/shard_map/pallas_call | solution.py:565
  47.7 9.9 %all-to-all-start = ((f32[32,24,128]{2,1,0:T(8,128)}), f32[32,24,128]{2,1,0:T(8,128)S(1)}, u32[]{:S(2)}, u32[]{:S(2)}) async-start(f32[32,24,128]{2,1,0:T(8,128)} %bitcast.1), calls=%async_computation | async-start | bytes 786432 | tf_op jit(solution)/shard_map/all_to_all | solution.py:576
  57.6 1.6 %shard_map.136 = f32[40,768]{1,0:T(8,128)} custom-call(f32[40,1024]{1,0:T(8,128)S(1)} %get-tuple-element.35.whole_ref, s32[8,768]{1,0:T(8,128)S(1)} %get-tuple-element.36.place_ref), custom_call_target="tpu_custom_call" | custom-call | flops 400000000 | bytes 1000000 | tf_op jit(solution)/shard_map/pallas_call | solution.py:577
  59.2 18.6 %all-to-all-done = f32[32,24,128]{2,1,0:T(8,128)S(1)} async-done(((f32[32,24,128]{2,1,0:T(8,128)}), f32[32,24,128]{2,1,0:T(8,128)S(1)}, u32[]{:S(2)}, u32[]{:S(2)}) %all-to-all-start) | async-done | bytes 393248 | tf_op jit(solution)/shard_map/all_to_all | solution.py:576
  77.8 1.9 %shard_map.137 = f32[40,768]{1,0:T(8,128)} custom-call(f32[768,128]{1,0:T(8,128)S(1)} %bitcast.4), custom_call_target="tpu_custom_call" | custom-call | tf_op jit(solution)/shard_map/pallas_call | solution.py:580
Async XLA Ops:
  2.8 23.1 %collective-permute-start = (f32[48,128]{1,0:T(8,128)}, f32[48,128]{1,0:T(8,128)S(1)}, u32[]{:S(2)}, u32[]{:S(2)}) collective-permute-start(f32[48,128]{1,0:T(8,128)} %get-tuple-element.23), channel_id=1, source_target_pairs={{1,2},{2,1},{3,4},{4,3},{5,6},{6,5},{7,8},{8,7},{9,10},{10,9},{11,... | collective-permute-start | bytes 73736 | tf_op jit(solution)/shard_map/ppermute | solution.py:545
  20.3 5.7 %collective-permute-start.1 = (f32[48,128]{1,0:T(8,128)}, f32[48,128]{1,0:T(8,128)S(1)}, u32[]{:S(2)}, u32[]{:S(2)}) collective-permute-start(f32[48,128]{1,0:T(8,128)} %get-tuple-element.24), channel_id=1, source_target_pairs={{0,1},{1,0},{2,3},{3,2},{4,5},{5,4},{6,7},{7,6},{8,9},{9,8},{10,11... | collective-permute-start | bytes 73736 | tf_op jit(solution)/shard_map/ppermute | solution.py:546
  22.9 0.7 copy-start
  23.6 0.9 %copy-start.1 = (f32[48,768]{1,0:T(8,128)S(1)}, f32[48,768]{1,0:T(8,128)}, u32[]{:S(2)}) copy-start(f32[48,768]{1,0:T(8,128)} %get-tuple-element.20.values_ref) | copy-start | bytes 442372
  26.1 17.0 %collective-permute-start.2 = (f32[192,128]{1,0:T(8,128)S(1)}, f32[192,128]{1,0:T(8,128)S(1)}, u32[]{:S(2)}, u32[]{:S(2)}) collective-permute-start(f32[192,128]{1,0:T(8,128)S(1)} %get-tuple-element.25.first_ref), channel_id=1, source_target_pairs={{0,32},{32,0},{64,96},{96,64},{128,160},{160,128},{192,224},{224,1... | collective-permute-start | bytes 294920 | tf_op jit(solution)/shard_map/ppermute | solution.py:555
  29.5 13.6 %collective-permute-start.3 = (f32[192,128]{1,0:T(8,128)S(1)}, f32[192,128]{1,0:T(8,128)S(1)}, u32[]{:S(2)}, u32[]{:S(2)}) collective-permute-start(f32[192,128]{1,0:T(8,128)S(1)} %get-tuple-element.26.second_ref), channel_id=1, source_target_pairs={{32,64},{64,32},{96,128},{128,96},{160,192},{192,160},{224,256},{2... | collective-permute-start | bytes 294920 | tf_op jit(solution)/shard_map/ppermute | solution.py:554
  36.5 1.0 %copy-start.2 = (bf16[512,256]{1,0:T(8,128)(2,1)S(1)}, bf16[512,256]{1,0:T(8,128)(2,1)}, u32[]{:S(2)}) copy-start(bf16[512,256]{1,0:T(8,128)(2,1)} %constant.15.clone.refs_3_) | copy-start | bytes 786436
  37.4 0.9 %copy-start.3 = (bf16[512,256]{1,0:T(8,128)(2,1)S(1)}, bf16[512,256]{1,0:T(8,128)(2,1)}, u32[]{:S(2)}) copy-start(bf16[512,256]{1,0:T(8,128)(2,1)} %constant.14.clone.refs_2_) | copy-start | bytes 786436
  38.4 0.9 %copy-start.4 = (bf16[256,256]{1,0:T(8,128)(2,1)S(1)}, bf16[256,256]{1,0:T(8,128)(2,1)}, u32[]{:S(2)}) copy-start(bf16[256,256]{1,0:T(8,128)(2,1)} %constant.16.clone.refs_4_) | copy-start | bytes 393220
  39.3 0.9 %copy-start.5 = (bf16[256,256]{1,0:T(8,128)(2,1)S(1)}, bf16[256,256]{1,0:T(8,128)(2,1)}, u32[]{:S(2)}) copy-start(bf16[256,256]{1,0:T(8,128)(2,1)} %constant.12.clone.refs_0_) | copy-start | bytes 393220
  40.2 0.8 %copy-start.6 = (bf16[128,256]{1,0:T(8,128)(2,1)S(1)}, bf16[128,256]{1,0:T(8,128)(2,1)}, u32[]{:S(2)}) copy-start(bf16[128,256]{1,0:T(8,128)(2,1)} %constant.13.clone.refs_1_) | copy-start | bytes 196612
  41.0 0.7 copy-start.7
  47.7 30.1 %all-to-all-start = ((f32[32,24,128]{2,1,0:T(8,128)}), f32[32,24,128]{2,1,0:T(8,128)S(1)}, u32[]{:S(2)}, u32[]{:S(2)}) async-start(f32[32,24,128]{2,1,0:T(8,128)} %bitcast.1), calls=%async_computation | async-start | bytes 786432 | tf_op jit(solution)/shard_map/all_to_all | solution.py:576

commit v2 on v1

--- a/solution.py
+++ b/solution.py
@@ -71,14 +71,8 @@
     div_join = both @ join
     grad_hi, grad_lo = two_parts(grad)
     div_hi, div_lo = two_parts(div_join)
-    mass_weight = np.tile(np.outer(weights, weights).reshape(16), 8).astype(np.float32)
-    return (
-        np.concatenate([grad_hi, grad_hi], axis=0),
-        grad_lo,
-        div_hi,
-        div_lo,
-        join.astype(jnp.bfloat16),
-        np.broadcast_to(mass_weight, (8, 128)).copy(),
+    return np.concatenate(
+        [grad_hi, grad_hi, grad_lo, div_hi, div_lo, join.astype(jnp.bfloat16)], axis=0
     )
 
 
@@ -222,7 +216,9 @@
     return block if by == 0 else pltpu.roll(block, by, 1)
 
 
-def margin_kernel(low_in, high_in, from_far, from_close, first_ref, second_ref):
+def margin_kernel(
+    low_in, high_in, from_far, from_close, first_ref, second_ref, low_ref, high_ref
+):
     lane = lane_iota((TILE, LANES))
     even = lax.rem(lax.axis_index("col"), 2) == 0
     from_left = jnp.where(even, from_far[...], from_close[...])
@@ -244,6 +240,8 @@
             )
         halves_of_rows.append(jnp.concatenate(blocks, axis=0))
     low, high = halves_of_rows
+    low_ref[...] = low
+    high_ref[...] = high
     even = lax.rem(lax.axis_index("curve"), 2) == 0
     first_ref[...] = jnp.where(even, high, low)
     second_ref[...] = jnp.where(even, low, high)
@@ -278,39 +276,96 @@
     return jnp.concatenate(lists + [within + 1.0, filler], axis=0)
 
 
-def pick_kernel(lists_ref, *refs):
-    count = len(refs) // 2
-    sources, (picks_ref, *targets), sems = refs[: count - 1], refs[count - 1 : -1], refs[-1]
-    copies = [
-        pltpu.make_async_copy(source, target, sems.at[i])
-        for i, (source, target) in enumerate(zip(sources, targets))
-    ]
-    for copy in copies:
-        copy.start()
-    shape = (POINTS_DEV, 1024)
-    for k in range(3):
-        line = lists_ref[k : k + 1, :].astype(jnp.int32) - 1
-        picks_ref[:, k * 1024 : (k + 1) * 1024] = (row_iota(shape) == line).astype(F32).astype(BF16)
-    for copy in copies:
-        copy.wait()
-
-
 def fluxes(slope, coefficients):
     along_cycle, along_rows = slope[:, :LANES], slope[:, LANES:]
     caa, cab, cbb = coefficients
     return caa * along_cycle + cab * along_rows, cab * along_cycle + cbb * along_rows
 
 
-def gradient(values, grad2_ref, grad_lo_ref):
+def gradient(values, matrices):
     upper, lower = halves(values)
-    return dot(jnp.concatenate([upper, lower], axis=1), grad2_ref[...]) + dot(
-        upper, grad_lo_ref[...]
-    )
-
-
-def divergence_joined(values, div_hi_ref, div_lo_ref):
+    return dot(jnp.concatenate([upper, lower], axis=1), matrices[0:256, :]) + dot(
+        upper, matrices[256:384, :]
+    )
+
+
+def divergence_joined(values, matrices):
     upper, lower = halves(values)
-    return dot(upper, div_hi_ref[...]) + dot(lower, div_hi_ref[...]) + dot(upper, div_lo_ref[...])
+    first = matrices[384:896, :]
+    return dot(upper, first) + dot(lower, first) + dot(upper, matrices[896:1408, :])
+
+
+def local_terms(rows, tile, matrices, slopes, flux, plain, coefs, coefs_at):
+    cells = [(n, r, g) for n, r in enumerate(rows) for g in range(2)]
+    stacked = []
+    for _, r, g in cells:
+        zonal, meridional = tile(r, g, 0, 8), tile(r, g, 8, 8)
+        energy = 0.5 * (zonal * zonal + meridional * meridional) + tile(r, g, 16, 8)
+        stacked += [tile(r, g, 0, STATE), energy]
+    slopes[...] = gradient(jnp.concatenate(stacked, axis=0), matrices)
+    lane = lane_iota((8, LANES))
+    inner_i = (lane % 4 == 1) | (lane % 4 == 2)
+    inner_j = (lane // 4 % 4 == 1) | (lane // 4 % 4 == 2)
+    weight = jnp.where(inner_i, 5.0 / 6.0, 1.0 / 6.0) * jnp.where(inner_j, 5.0 / 6.0, 1.0 / 6.0)
+    for n, r, g in cells:
+
+        def line(k):
+            return jnp.broadcast_to(tile(r, g, STATE + k, 1), (8, LANES))
+
+        jacobian, coriolis = line(0), line(1)
+        m11, m12, m21, m22 = 1.0 + line(2), line(3), line(4), 1.0 + line(5)
+        caa = jacobian * (m11 * m11 + m12 * m12)
+        cab = jacobian * (m11 * m21 + m12 * m22)
+        cbb = jacobian * (m21 * m21 + m22 * m22)
+        at = coefs_at(r, g)
+        if at is not None:
+            coefs[at : at + 8, :] = caa
+            coefs[at + 8 : at + 16, :] = cab
+            coefs[at + 16 : at + 24, :] = cbb
+        mass = jacobian * weight
+        at = (2 * n + g) * TILE
+        first = slice(g * 2 * LANES, (g * 2 + 1) * LANES)
+        second = slice((g * 2 + 1) * LANES, (g * 2 + 2) * LANES)
+        for f in range(FIELDS):
+            one, two = fluxes(slopes[at + 8 * f : at + 8 * f + 8, :], (caa, cab, cbb))
+            flux[n * 56 + 8 * f : n * 56 + 8 * f + 8, first] = one
+            flux[n * 56 + 8 * f : n * 56 + 8 * f + 8, second] = two
+        zonal, meridional = tile(r, g, 0, 8), tile(r, g, 8, 8)
+        flow1 = jacobian * (m11 * zonal + m12 * meridional)
+        flow2 = jacobian * (m21 * zonal + m22 * meridional)
+        for k in range(2):
+            carried = tile(r, g, 24 + 8 * k, 8)
+            flux[n * 56 + 40 + 8 * k : n * 56 + 48 + 8 * k, first] = carried * flow1
+            flux[n * 56 + 40 + 8 * k : n * 56 + 48 + 8 * k, second] = carried * flow2
+        ea, eb = slopes[at + 40 : at + 48, :LANES], slopes[at + 40 : at + 48, LANES:]
+        ta, tb = slopes[at + 16 : at + 24, :LANES], slopes[at + 16 : at + 24, LANES:]
+        part = slice(g * LANES, (g + 1) * LANES)
+        plain[n * 32 : n * 32 + 8, part] = mass * (coriolis * meridional - (m11 * ea + m21 * eb))
+        plain[n * 32 + 8 : n * 32 + 16, part] = -mass * (coriolis * zonal + (m12 * ea + m22 * eb))
+        plain[n * 32 + 16 : n * 32 + 24, part] = -mass * (
+            zonal * (m11 * ta + m21 * tb) + meridional * (m12 * ta + m22 * tb)
+        )
+        plain[n * 32 + 24 : n * 32 + 32, part] = mass
+    spread = divergence_joined(flux[...], matrices)
+    upper, lower = halves(plain[...])
+    join = matrices[1408:1664, :]
+    return spread, dot(upper, join) + dot(lower, join)
+
+
+def inner_kernel(
+    low_ref, high_ref, lists_ref, matrices, spread_ref, direct_ref, coefs, picks_ref, slopes, flux, plain
+):
+    def tile(r, g, start=0, size=TILE):
+        offset = ((r % 2) * 2 + g) * TILE + start
+        return (low_ref if r < 2 else high_ref)[offset : offset + size, :]
+
+    spread, direct = local_terms(
+        range(4), tile, matrices, slopes, flux, plain, coefs, lambda r, g: (2 * r + g) * 24
+    )
+    spread_ref[...] = spread
+    direct_ref[...] = direct
+    line = (lists_ref[0:1, :] + lists_ref[1:2, :] + lists_ref[2:3, :]).astype(jnp.int32) - 1
+    picks_ref[...] = (row_iota((POINTS_DEV, 1024)) == line).astype(F32).astype(BF16)
 
 
 def rows_joined(below, here, above, low_mask, high_mask):
@@ -327,126 +382,91 @@
 
 def section_kernel(
     first_far_ref,
-    first_ref,
-    second_ref,
     second_far_ref,
+    low_ref,
+    high_ref,
     lists_ref,
     picks_ref,
-    grad2_ref,
-    grad_lo_ref,
-    div_hi_ref,
-    div_lo_ref,
-    join_ref,
-    weight_ref,
+    matrices,
+    inner_spread,
+    inner_direct,
+    inner_coefs,
     whole_ref,
     send_ref,
-    quarters,
+    outside,
     slopes,
     flux,
     plain,
-    coefs,
+    outer_coefs,
 ):
     even = lax.rem(lax.axis_index("curve"), 2) == 0
-    quarters[0] = jnp.where(even, second_far_ref[...], first_far_ref[...])
-    quarters[1] = jnp.where(even, second_ref[...], first_ref[...])
-    quarters[2] = jnp.where(even, first_ref[...], second_ref[...])
-    quarters[3] = jnp.where(even, first_far_ref[...], second_far_ref[...])
+    outside[0] = jnp.where(even, second_far_ref[...], first_far_ref[...])
+    outside[1] = jnp.where(even, first_far_ref[...], second_far_ref[...])
 
     def tile(r, g, start=0, size=TILE):
         offset = ((r % 2) * 2 + g) * TILE + start
-        return quarters[r // 2, offset : offset + size, :]
-
-    cells = [(r, g) for r in range(8) for g in range(2)]
-    stacked = []
-    for r, g in cells:
-        zonal, meridional = tile(r, g, 0, 8), tile(r, g, 8, 8)
-        energy = 0.5 * (zonal * zonal + meridional * meridional) + tile(r, g, 16, 8)
-        stacked += [tile(r, g, 0, STATE), energy]
-    slopes[...] = gradient(jnp.concatenate(stacked, axis=0), grad2_ref, grad_lo_ref)
-
-    for r, g in cells:
-        def line(k):
-            return jnp.broadcast_to(tile(r, g, STATE + k, 1), (8, LANES))
-
-        jacobian, coriolis = line(0), line(1)
-        m11, m12, m21, m22 = 1.0 + line(2), line(3), line(4), 1.0 + line(5)
-        caa = jacobian * (m11 * m11 + m12 * m12)
-        cab = jacobian * (m11 * m21 + m12 * m22)
-        cbb = jacobian * (m21 * m21 + m22 * m22)
-        at = (2 * r + g) * 24
-        coefs[at : at + 8, :] = caa
-        coefs[at + 8 : at + 16, :] = cab
-        coefs[at + 16 : at + 24, :] = cbb
-        mass = jacobian * weight_ref[...]
-        at = (2 * r + g) * TILE
-        first = slice(g * 2 * LANES, (g * 2 + 1) * LANES)
-        second = slice((g * 2 + 1) * LANES, (g * 2 + 2) * LANES)
-        for f in range(FIELDS):
-            one, two = fluxes(slopes[at + 8 * f : at + 8 * f + 8, :], (caa, cab, cbb))
-            flux[r * 56 + 8 * f : r * 56 + 8 * f + 8, first] = one
-            flux[r * 56 + 8 * f : r * 56 + 8 * f + 8, second] = two
-        zonal, meridional = tile(r, g, 0, 8), tile(r, g, 8, 8)
-        flow1 = jacobian * (m11 * zonal + m12 * meridional)
-        flow2 = jacobian * (m21 * zonal + m22 * meridional)
-        for k in range(2):
-            carried = tile(r, g, 24 + 8 * k, 8)
-            flux[r * 56 + 40 + 8 * k : r * 56 + 48 + 8 * k, first] = carried * flow1
-            flux[r * 56 + 40 + 8 * k : r * 56 + 48 + 8 * k, second] = carried * flow2
-        ea, eb = slopes[at + 40 : at + 48, :LANES], slopes[at + 40 : at + 48, LANES:]
-        ta, tb = slopes[at + 16 : at + 24, :LANES], slopes[at + 16 : at + 24, LANES:]
-        part = slice(g * LANES, (g + 1) * LANES)
-        plain[r * 32 : r * 32 + 8, part] = mass * (
-            coriolis * meridional - (m11 * ea + m21 * eb)
-        )
-        plain[r * 32 + 8 : r * 32 + 16, part] = -mass * (
-            coriolis * zonal + (m12 * ea + m22 * eb)
-        )
-        plain[r * 32 + 16 : r * 32 + 24, part] = -mass * (
-            zonal * (m11 * ta + m21 * tb) + meridional * (m12 * ta + m22 * tb)
-        )
-        plain[r * 32 + 24 : r * 32 + 32, part] = mass
-
-    spread = divergence_joined(flux[...], div_hi_ref, div_lo_ref)
-    upper, lower = halves(plain[...])
-    direct = dot(upper, join_ref[...]) + dot(lower, join_ref[...])
+        if r in (0, 1, 6, 7):
+            return outside[r // 6, offset : offset + size, :]
+        return (low_ref if r < 4 else high_ref)[offset : offset + size, :]
+
+    outer_rows = (0, 1, 6, 7)
+    outer_spread, outer_direct = local_terms(
+        outer_rows,
+        tile,
+        matrices,
+        slopes,
+        flux,
+        plain,
+        outer_coefs,
+        lambda r, g: {1: 24 * g, 6: 48 + 24 * g}.get(r),
+    )
 
     lane = lane_iota((1, LANES)) % 16
     low_mask = (lane < 4).astype(F32)
     high_mask = (lane >= 12).astype(F32)
 
-    def joined(value, size, r, start, count):
+    def joined(outer, inner, size, r, start, count):
         def rows(k):
-            return value[k * size + start : k * size + start + count, :]
+            if k in outer_rows:
+                at = outer_rows.index(k) * size + start
+                return outer[at : at + count, :]
+            at = (k - 2) * size + start
+            return inner[at : at + count, :]
 
         return rows_joined(rows(r - 1), rows(r), rows(r + 1), low_mask, high_mask)
+
+    def coefficients(r, g, k):
+        if r in outer_rows:
+            at = (0 if r == 1 else 48) + 24 * g + 8 * k
+            return outer_coefs[at : at + 8, :]
+        at = (2 * (r - 2) + g) * 24 + 8 * k
+        return inner_coefs[at : at + 8, :]
 
     inverse = {}
     smooth = []
     for r in range(1, 7):
-        mass_sum = joined(direct, 32, r, 24, 8)
-        smoothing = joined(spread, 56, r, 0, STATE)
+        mass_sum = joined(outer_direct, inner_direct, 32, r, 24, 8)
+        smoothing = joined(outer_spread, inner_spread, 56, r, 0, STATE)
         for g in range(2):
             inverse[r, g] = 1.0 / jnp.where(mass_sum[g] > 0.0, mass_sum[g], 1.0)
             smooth.append(smoothing[g] * jnp.concatenate([inverse[r, g]] * FIELDS, axis=0))
-    again = gradient(jnp.concatenate(smooth, axis=0), grad2_ref, grad_lo_ref)
+    again = gradient(jnp.concatenate(smooth, axis=0), matrices)
     flat = []
     for r in range(1, 7):
         parts = []
         for g in range(2):
-            at = (2 * r + g) * 24
             triple = tuple(
-                jnp.concatenate([coefs[at + 8 * k : at + 8 * k + 8, :]] * FIELDS, axis=0)
-                for k in range(3)
+                jnp.concatenate([coefficients(r, g, k)] * FIELDS, axis=0) for k in range(3)
             )
             start = (2 * (r - 1) + g) * STATE
             parts += list(fluxes(again[start : start + STATE, :], triple))
         flat.append(jnp.concatenate(parts, axis=1))
-    damped = divergence_joined(jnp.concatenate(flat, axis=0), div_hi_ref, div_lo_ref)
+    damped = divergence_joined(jnp.concatenate(flat, axis=0), matrices)
 
     ordered = []
     for r in range(2, 6):
-        straight = joined(direct, 32, r, 0, 24)
-        carried = joined(spread, 56, r, STATE, 16)
+        straight = joined(outer_direct, inner_direct, 32, r, 0, 24)
+        carried = joined(outer_spread, inner_spread, 56, r, STATE, 16)
         damping = rows_joined(
             damped[(r - 2) * STATE : (r - 1) * STATE, :],
             damped[(r - 1) * STATE : r * STATE, :],
@@ -463,19 +483,12 @@
             ordered.append(tile(r, g, 0, STATE) + change * scale)
     whole = jnp.concatenate(ordered, axis=1)
     whole_ref[...] = whole
-    columns = []
-    for k in range(3):
-        pieces = []
-        if k > 0:
-            pieces.append(jnp.zeros((STATE * k, 1024), F32))
-        pieces.append(whole)
-        if k < 2:
-            pieces.append(jnp.zeros((STATE * (2 - k), 1024), F32))
-        slot_row = jnp.where(
-            row_iota((8, 1024)) == k, jnp.broadcast_to(lists_ref[3:4, :], (8, 1024)), 0.0
-        )
-        columns.append(jnp.concatenate(pieces + [slot_row], axis=0))
-    upper, lower = halves(jnp.concatenate(columns, axis=1))
+    shares = [(lists_ref[k : k + 1, :] > 0.0).astype(F32) for k in range(3)]
+    slots = [jnp.broadcast_to(lists_ref[3:4, :] * shares[k], (8, 1024)) for k in range(3)]
+    row = row_iota((8, 1024))
+    slot_rows = sum(jnp.where(row == k, slots[k], 0.0) for k in range(3))
+    columns = jnp.concatenate([whole * share for share in shares] + [slot_rows], axis=0)
+    upper, lower = halves(columns)
     sent = dot_last(picks_ref[...], jnp.concatenate([upper, lower], axis=0))
     send_ref[...] = sent[:, :LANES] + sent[:, LANES:]
 
@@ -488,17 +501,19 @@
 
 def receive_kernel(received_ref, physics_ref):
     turned_over = received_ref[...].T
-    values = jnp.concatenate(
-        [turned_over[STATE * k : STATE * (k + 1), :] for k in range(3)], axis=1
-    )
-    first = values.astype(BF16).astype(F32)
-    both = jnp.concatenate([first, values - first], axis=0).astype(BF16)
-    hits = []
-    for k in range(3):
-        slot = turned_over[3 * STATE + k : 3 * STATE + k + 1, :].astype(jnp.int32) - 1
-        hits.append((row_iota((POINTS_DEV, POINTS_DEV)) == slot).astype(F32).astype(BF16))
-    placed = dot_last(both, jnp.concatenate(hits, axis=1))
-    physics_ref[...] = placed[:STATE] + placed[STATE:]
+    upper, lower = halves(turned_over)
+    places = slice(3 * STATE, 3 * STATE + 3)
+    slot = turned_over[places, :].astype(jnp.int32) - 1
+    row = row_iota((POINTS_DEV, POINTS_DEV))
+    hits = (row == slot[0:1]) | (row == slot[1:2]) | (row == slot[2:3])
+    rows = dot_last(jnp.concatenate([upper, lower], axis=0), hits.astype(F32).astype(BF16))
+    rows = rows[:LANES] + rows[LANES:]
+    own = rows[places, :] == (lane_iota((3, POINTS_DEV)) + 1).astype(F32)
+    physics_ref[...] = jnp.where(
+        own[0:1],
+        rows[:STATE],
+        jnp.where(own[1:2], rows[STATE : 2 * STATE], rows[2 * STATE : 3 * STATE]),
+    )
 
 
 def call(kernel, shapes, scratch=(), flops=0, moved=0, vmem=VMEM_LIMIT, **specs):
@@ -523,7 +538,6 @@
     evolving_state_array, point_id, neighbours, jacobian, inverse_metric, coriolis, column_slot
 ):
     anywhere = pl.BlockSpec(memory_space=pltpu.HBM)
-    vmem = pl.BlockSpec(memory_space=pltpu.VMEM)
     half = ((4 * TILE, LANES), F32)
     strip = ((TILE, LANES), F32)
     values_shape = ((TILE, POINTS_DEV), F32)
@@ -550,29 +564,34 @@
         flops=400_000_000,
         moved=1_000_000,
     )(values, neighbours, column_slot[None])
-    first, second = call(margin_kernel, [half, half])(low, high, from_far, from_close)
+    first, second, low, high = call(margin_kernel, [half] * 4)(low, high, from_far, from_close)
     second_far = lax.ppermute(second, "curve", swaps(rows, 1))
     first_far = lax.ppermute(first, "curve", swaps(rows, 0))
-    matrices = [jnp.asarray(m) for m in operators()]
-    picks, *matrices = call(
-        pick_kernel,
-        [((POINTS_DEV, 3 * 1024), BF16)] + [(m.shape, m.dtype) for m in matrices],
-        scratch=[pltpu.SemaphoreType.DMA((len(matrices),))],
-        in_specs=[vmem] + [anywhere] * len(matrices),
+    matrices = jnp.asarray(operators())
+    scratch = [
+        pltpu.VMEM((8 * TILE, 2 * LANES), F32),
+        pltpu.VMEM((4 * 56, 4 * LANES), F32),
+        pltpu.VMEM((4 * 32, 2 * LANES), F32),
+    ]
+    spread, direct, coefs, picks = call(
+        inner_kernel,
+        [
+            ((4 * 56, 2 * LANES), F32),
+            ((4 * 32, 2 * LANES), F32),
+            ((8 * 24, LANES), F32),
+            ((POINTS_DEV, 1024), BF16),
+        ],
+        scratch=scratch,
         flops=400_000_000,
         moved=1_000_000,
-    )(lists, *matrices)
+    )(low, high, lists, matrices)
     whole, sent = call(
         section_kernel,
         [((STATE, 1024), F32), ((POINTS_DEV, LANES), F32)],
-        scratch=[
-            pltpu.VMEM((4, 4 * TILE, LANES), F32),
-            pltpu.VMEM((16 * TILE, 2 * LANES), F32),
-            pltpu.VMEM((8 * 56, 4 * LANES), F32),
-            pltpu.VMEM((8 * 32, 2 * LANES), F32),
-            pltpu.VMEM((16 * 24, LANES), F32),
-        ],
-    )(first_far, first, second, second_far, lists, picks, *matrices)
+        scratch=[pltpu.VMEM((2, 4 * TILE, LANES), F32)]
+        + scratch
+        + [pltpu.VMEM((4 * 24, LANES), F32)],
+    )(first_far, second_far, low, high, lists, picks, matrices, spread, direct, coefs)
     received = lax.all_to_all(sent, "col", split_axis=0, concat_axis=0, tiled=True)
     (updated,) = call(
         restore_kernel, [((STATE, POINTS_DEV), F32)], flops=400_000_000, moved=1_000_000

time: 80.6 us -> 76.6 us (0.950)
  local copies, waits for them, and re-layouts: 7.52 us -> 2.29 us
  waiting for transfers between devices: 18.6 us -> 22.1 us
  Pallas kernels: 13.2 us -> 11.7 us
    unnamed x16 -> x6, local copies, waits for them, and re-layouts: 6.82 us -> 1.6 us
    ppermute x1, waiting for transfers between devices: 0.01 us -> 4.1 us  [body(): second_far = lax.ppermute(second, 'curve', swaps(rows, 1))]
    pallas_call x1, Pallas kernels: 4.56 us -> 3.11 us  [body(): call(section_kernel, [((STATE, 1024), F32), ((POINTS_DEV, LANES), F32)],...]
  transfers between devices with their start and end apart: 5 -> 5, of which waited for: 1 -> 2; matrix products, arithmetic and copies ran while one was open for 1% -> 1% of each run, Pallas kernels for 6% -> 6%
where the time goes in v2:
time: 76.6 us; the launch traced here: 76.2 us
  starting transfers between devices  39.4 us (51%)
  waiting for transfers between devices  22.1 us (29%)
  Pallas kernels  11.7 us (15%)
  local copies, waits for them, and re-layouts  2.29 us (3%)
    all_to_all x1, waiting for transfers between devices, body(): lax.all_to_all(sent, 'col', split_axis=0, concat_axis=0, tiled=True)  17.9 us
    ppermute x1, starting transfers between devices, body(): lax.ppermute(far, 'col', swaps(cols, 1) + [(cols - 1, 0), (0, cols - 1)])  17.6 us
    all_to_all x1, starting transfers between devices, body(): lax.all_to_all(sent, 'col', split_axis=0, concat_axis=0, tiled=True)  9.5 us
    ppermute x1, starting transfers between devices, body(): second_far = lax.ppermute(second, 'curve', swaps(rows, 1))  6.97 us
    ppermute x1, waiting for transfers between devices, body(): second_far = lax.ppermute(second, 'curve', swaps(rows, 1))  4.1 us
    ppermute x1, starting transfers between devices, body(): first_far = lax.ppermute(first, 'curve', swaps(rows, 0))  3.38 us
    pallas_call x1, Pallas kernels, body(): call(section_kernel, [((STATE, 1024), F32), ((POINTS_DEV, LANES), F32)],...  3.11 us
    pallas_call x1, Pallas kernels, body(): call(strip_kernel, [strip, strip, values_shape], scratch=[pltpu.VMEM((8,...  2.19 us
  transfers between devices with their start and end apart: 5, of which 2 were waited for; matrix products, arithmetic and copies ran while one was open for 1% of the time, Pallas kernels for 6%

profile of v2, /device:TPU:6, one launch (start us, length us, event | category | flops | bytes accessed | tf_op | source)
XLA Modules:
  0.0 76.2 jit_solution(6218829434461369797)
XLA Ops:
  0.6 2.2 %shard_map.86 = (f32[48,128]{1,0:T(8,128)}, f32[48,128]{1,0:T(8,128)}, f32[48,768]{1,0:T(8,128)}) custom-call(f32[5,8,768]{2,1,0:T(8,128)} %state_ref.1, f32[768]{0:T(1024)} %jacobian_ref.1, f32[768]{0:T(1024)} %coriolis_ref.1, f32[4,768]{1,0:T(4,128)} %metric_ref.1, s32[8,48]{1,0:T(8,128)} %near_ref.3), custom_call_target="tpu_custom_call" | custom-call | tf_op jit(solution)/shard_map/pallas_call | solution.py:544
  2.8 0.0 copy-start
  2.8 17.6 %collective-permute-start = (f32[48,128]{1,0:T(8,128)}, f32[48,128]{1,0:T(8,128)S(1)}, u32[]{:S(2)}, u32[]{:S(2)}) collective-permute-start(f32[48,128]{1,0:T(8,128)} %get-tuple-element.22), channel_id=1, source_target_pairs={{1,2},{2,1},{3,4},{4,3},{5,6},{6,5},{7,8},{8,7},{9,10},{10,9},{11,... | collective-permute-start | bytes 73736 | tf_op jit(solution)/shard_map/ppermute | solution.py:559
  20.5 1.9 %collective-permute-start.1 = (f32[48,128]{1,0:T(8,128)}, f32[48,128]{1,0:T(8,128)S(1)}, u32[]{:S(2)}, u32[]{:S(2)}) collective-permute-start(f32[48,128]{1,0:T(8,128)} %get-tuple-element.23), channel_id=1, source_target_pairs={{0,1},{1,0},{2,3},{3,2},{4,5},{5,4},{6,7},{7,6},{8,9},{9,8},{10,11... | collective-permute-start | bytes 73736 | tf_op jit(solution)/shard_map/ppermute | solution.py:560
  22.4 0.7 broadcast_in_dim.3.slot_ref
  23.1 0.0 copy-start.1
  23.1 0.7 copy-done.1
  23.8 0.0 copy-start.2
  23.8 0.9 %copy-done.2 = f32[48,768]{1,0:T(8,128)S(1)} copy-done((f32[48,768]{1,0:T(8,128)S(1)}, f32[48,768]{1,0:T(8,128)}, u32[]{:S(2)}) %copy-start.2) | copy-done | bytes 147480
  24.7 1.4 %shard_map.87 = (f32[192,128]{1,0:T(8,128)S(1)}, f32[192,128]{1,0:T(8,128)S(1)}, s32[8,768]{1,0:T(8,128)S(1)}, f32[8,1024]{1,0:T(8,128)S(1)}) custom-call(f32[48,768]{1,0:T(8,128)S(1)} %copy-done.2, s32[8,48]{1,0:T(8,128)S(1)} %copy-done.1, s32[1,768]{1,0:T(1,128)S(1)} %broadcast_in_dim.3.slot_ref), custom_call_target="tpu_custom_call" | custom-call | flops 400000000 | bytes 1000000 | tf_op jit(solution)/shard_map/pallas_call | solution.py:561
  26.1 0.0 collective-permute-done.from_far
  26.1 0.0 collective-permute-done.1.from_close
  26.1 0.1 shard_map.88
  26.3 3.4 %collective-permute-start.2 = (f32[192,128]{1,0:T(8,128)S(1)}, f32[192,128]{1,0:T(8,128)S(1)}, u32[]{:S(2)}, u32[]{:S(2)}) collective-permute-start(f32[192,128]{1,0:T(8,128)S(1)} %get-tuple-element.24), channel_id=1, source_target_pairs={{0,32},{32,0},{64,96},{96,64},{128,160},{160,128},{192,224},{224,1... | collective-permute-start | bytes 294920 | tf_op jit(solution)/shard_map/ppermute | solution.py:569
  29.6 7.0 %collective-permute-start.3 = (f32[192,128]{1,0:T(8,128)S(1)}, f32[192,128]{1,0:T(8,128)S(1)}, u32[]{:S(2)}, u32[]{:S(2)}) collective-permute-start(f32[192,128]{1,0:T(8,128)S(1)} %get-tuple-element.25), channel_id=1, source_target_pairs={{32,64},{64,32},{96,128},{128,96},{160,192},{192,160},{224,256},{2... | collective-permute-start | bytes 294920 | tf_op jit(solution)/shard_map/ppermute | solution.py:568
  36.6 0.0 copy-done
  36.6 1.4 %shard_map.89 = (f32[224,256]{1,0:T(8,128)S(1)}, f32[128,256]{1,0:T(8,128)S(1)}, f32[192,128]{1,0:T(8,128)S(1)}, bf16[768,1024]{1,0:T(8,128)(2,1)S(1)}) custom-call(f32[192,128]{1,0:T(8,128)S(1)} %get-tuple-element.26.low_ref, f32[192,128]{1,0:T(8,128)S(1)} %get-tuple-element.27.high_ref, f32[8,1024]{1,0:T(8,128)S(1)} %get-tuple-element.28.lists_ref, ...), custom_call_target="tpu_custom_call" | custom-call | flops 400000000 | bytes 1000000 | tf_op jit(solution)/shard_map/pallas_call | solution.py:576
  38.1 0.0 collective-permute-done.2.first_far_ref
  38.1 4.1 %collective-permute-done.3.second_far_ref = f32[192,128]{1,0:T(8,128)S(1)} collective-permute-done((f32[192,128]{1,0:T(8,128)S(1)}, f32[192,128]{1,0:T(8,128)S(1)}, u32[]{:S(2)}, u32[]{:S(2)}) %collective-permute-start.3) | collective-permute-done | bytes 98336 | tf_op jit(solution)/shard_map/ppermute | solution.py:568
  42.2 3.1 %shard_map.90 = (f32[40,1024]{1,0:T(8,128)S(1)}, f32[768,128]{1,0:T(8,128)}) custom-call(f32[192,128]{1,0:T(8,128)S(1)} %collective-permute-done.2.first_far_ref, f32[192,128]{1,0:T(8,128)S(1)} %collective-permute-done.3.second_far_ref, f32[192,128]{1,0:T(8,128)S(1)} %get-tuple-element.26.low_ref, f32[192,128]{1,0:T(8,128)S(1)} %get-tuple-element.27.high_ref, ...), custom_call_target="tpu_custom_call" | custom-call | tf_op jit(solution)/shard_map/pallas_call | solution.py:588
  45.3 9.5 %all-to-all-start = ((f32[32,24,128]{2,1,0:T(8,128)}), f32[32,24,128]{2,1,0:T(8,128)S(1)}, u32[]{:S(2)}, u32[]{:S(2)}) async-start(f32[32,24,128]{2,1,0:T(8,128)} %bitcast.1), calls=%async_computation | async-start | bytes 786432 | tf_op jit(solution)/shard_map/all_to_all | solution.py:595
  54.8 1.6 %shard_map.91 = f32[40,768]{1,0:T(8,128)} custom-call(f32[40,1024]{1,0:T(8,128)S(1)} %get-tuple-element.33.whole_ref, s32[8,768]{1,0:T(8,128)S(1)} %get-tuple-element.34.place_ref), custom_call_target="tpu_custom_call" | custom-call | flops 400000000 | bytes 1000000 | tf_op jit(solution)/shard_map/pallas_call | solution.py:596
  56.4 17.9 %all-to-all-done = f32[32,24,128]{2,1,0:T(8,128)S(1)} async-done(((f32[32,24,128]{2,1,0:T(8,128)}), f32[32,24,128]{2,1,0:T(8,128)S(1)}, u32[]{:S(2)}, u32[]{:S(2)}) %all-to-all-start) | async-done | bytes 393248 | tf_op jit(solution)/shard_map/all_to_all | solution.py:595
  74.4 1.8 %shard_map.92 = f32[40,768]{1,0:T(8,128)} custom-call(f32[768,128]{1,0:T(8,128)S(1)} %bitcast.4), custom_call_target="tpu_custom_call" | custom-call | tf_op jit(solution)/shard_map/pallas_call | solution.py:599
Async XLA Ops:
  2.8 33.8 %copy-start = (bf16[1664,256]{1,0:T(8,128)(2,1)S(1)}, bf16[1664,256]{1,0:T(8,128)(2,1)}, u32[]{:S(2)}) copy-start(bf16[1664,256]{1,0:T(8,128)(2,1)} %constant.2.clone.matrices) | copy-start | bytes 2555908
  2.8 23.3 %collective-permute-start = (f32[48,128]{1,0:T(8,128)}, f32[48,128]{1,0:T(8,128)S(1)}, u32[]{:S(2)}, u32[]{:S(2)}) collective-permute-start(f32[48,128]{1,0:T(8,128)} %get-tuple-element.22), channel_id=1, source_target_pairs={{1,2},{2,1},{3,4},{4,3},{5,6},{6,5},{7,8},{8,7},{9,10},{10,9},{11,... | collective-permute-start | bytes 73736 | tf_op jit(solution)/shard_map/ppermute | solution.py:559
  20.5 5.7 %collective-permute-start.1 = (f32[48,128]{1,0:T(8,128)}, f32[48,128]{1,0:T(8,128)S(1)}, u32[]{:S(2)}, u32[]{:S(2)}) collective-permute-start(f32[48,128]{1,0:T(8,128)} %get-tuple-element.23), channel_id=1, source_target_pairs={{0,1},{1,0},{2,3},{3,2},{4,5},{5,4},{6,7},{7,6},{8,9},{9,8},{10,11... | collective-permute-start | bytes 73736 | tf_op jit(solution)/shard_map/ppermute | solution.py:560
  23.1 0.7 copy-start.1
  23.8 0.9 %copy-start.2 = (f32[48,768]{1,0:T(8,128)S(1)}, f32[48,768]{1,0:T(8,128)}, u32[]{:S(2)}) copy-start(f32[48,768]{1,0:T(8,128)} %get-tuple-element.19.values_ref) | copy-start | bytes 442372
  26.3 11.8 %collective-permute-start.2 = (f32[192,128]{1,0:T(8,128)S(1)}, f32[192,128]{1,0:T(8,128)S(1)}, u32[]{:S(2)}, u32[]{:S(2)}) collective-permute-start(f32[192,128]{1,0:T(8,128)S(1)} %get-tuple-element.24), channel_id=1, source_target_pairs={{0,32},{32,0},{64,96},{96,64},{128,160},{160,128},{192,224},{224,1... | collective-permute-start | bytes 294920 | tf_op jit(solution)/shard_map/ppermute | solution.py:569
  29.6 12.5 %collective-permute-start.3 = (f32[192,128]{1,0:T(8,128)S(1)}, f32[192,128]{1,0:T(8,128)S(1)}, u32[]{:S(2)}, u32[]{:S(2)}) collective-permute-start(f32[192,128]{1,0:T(8,128)S(1)} %get-tuple-element.25), channel_id=1, source_target_pairs={{32,64},{64,32},{96,128},{128,96},{160,192},{192,160},{224,256},{2... | collective-permute-start | bytes 294920 | tf_op jit(solution)/shard_map/ppermute | solution.py:568
  45.3 29.1 %all-to-all-start = ((f32[32,24,128]{2,1,0:T(8,128)}), f32[32,24,128]{2,1,0:T(8,128)S(1)}, u32[]{:S(2)}, u32[]{:S(2)}) async-start(f32[32,24,128]{2,1,0:T(8,128)} %bitcast.1), calls=%async_computation | async-start | bytes 786432 | tf_op jit(solution)/shard_map/all_to_all | solution.py:595

commit v3 on v2

--- a/solution.py
+++ b/solution.py
@@ -381,8 +381,8 @@
 
 
 def section_kernel(
+    second_far_ref,
     first_far_ref,
-    second_far_ref,
     low_ref,
     high_ref,
     lists_ref,
@@ -591,7 +591,7 @@
         scratch=[pltpu.VMEM((2, 4 * TILE, LANES), F32)]
         + scratch
         + [pltpu.VMEM((4 * 24, LANES), F32)],
-    )(first_far, second_far, low, high, lists, picks, matrices, spread, direct, coefs)
+    )(second_far, first_far, low, high, lists, picks, matrices, spread, direct, coefs)
     received = lax.all_to_all(sent, "col", split_axis=0, concat_axis=0, tiled=True)
     (updated,) = call(
         restore_kernel, [((STATE, POINTS_DEV), F32)], flops=400_000_000, moved=1_000_000

time: 76.6 us -> 77.8 us (1.016)
  the two profiles are of different devices: /device:TPU:6 before, /device:TPU:70 now
where the time goes in v3:
time: 77.8 us; the launch traced here: 77.4 us
  starting transfers between devices  37.3 us (48%)
  waiting for transfers between devices  25.4 us (33%)
  Pallas kernels  11.7 us (15%)
  local copies, waits for them, and re-layouts  2.29 us (3%)
    all_to_all x1, waiting for transfers between devices, body(): lax.all_to_all(sent, 'col', split_axis=0, concat_axis=0, tiled=True)  23.5 us
    ppermute x1, starting transfers between devices, body(): lax.ppermute(far, 'col', swaps(cols, 1) + [(cols - 1, 0), (0, cols - 1)])  16.7 us
    all_to_all x1, starting transfers between devices, body(): lax.all_to_all(sent, 'col', split_axis=0, concat_axis=0, tiled=True)  8.88 us
    ppermute x1, starting transfers between devices, body(): first_far = lax.ppermute(first, 'curve', swaps(rows, 0))  6.97 us
    pallas_call x1, Pallas kernels, body(): call(section_kernel, [((STATE, 1024), F32), ((POINTS_DEV, LANES), F32)],...  3.12 us
    ppermute x1, starting transfers between devices, body(): second_far = lax.ppermute(second, 'curve', swaps(rows, 1))  2.78 us
    pallas_call x1, Pallas kernels, body(): call(strip_kernel, [strip, strip, values_shape], scratch=[pltpu.VMEM((8,...  2.19 us
    ppermute x1, starting transfers between devices, body(): from_close = lax.ppermute(close, 'col', swaps(cols, 0))  1.92 us
  transfers between devices with their start and end apart: 5, of which 2 were waited for; matrix products, arithmetic and copies ran while one was open for 1% of the time, Pallas kernels for 6%

profile of v3, /device:TPU:70, one launch (start us, length us, event | category | flops | bytes accessed | tf_op | source)
XLA Modules:
  0.0 77.4 jit_solution(16874629658050716030)
XLA Ops:
  0.6 2.2 %shard_map.86 = (f32[48,128]{1,0:T(8,128)}, f32[48,128]{1,0:T(8,128)}, f32[48,768]{1,0:T(8,128)}) custom-call(f32[5,8,768]{2,1,0:T(8,128)} %state_ref.1, f32[768]{0:T(1024)} %jacobian_ref.1, f32[768]{0:T(1024)} %coriolis_ref.1, f32[4,768]{1,0:T(4,128)} %metric_ref.1, s32[8,48]{1,0:T(8,128)} %near_ref.3), custom_call_target="tpu_custom_call" | custom-call | tf_op jit(solution)/shard_map/pallas_call | solution.py:544
  2.8 0.0 copy-start
  2.8 16.7 %collective-permute-start = (f32[48,128]{1,0:T(8,128)}, f32[48,128]{1,0:T(8,128)S(1)}, u32[]{:S(2)}, u32[]{:S(2)}) collective-permute-start(f32[48,128]{1,0:T(8,128)} %get-tuple-element.22), channel_id=1, source_target_pairs={{1,2},{2,1},{3,4},{4,3},{5,6},{6,5},{7,8},{8,7},{9,10},{10,9},{11,... | collective-permute-start | bytes 73736 | tf_op jit(solution)/shard_map/ppermute | solution.py:559
  19.6 1.9 %collective-permute-start.1 = (f32[48,128]{1,0:T(8,128)}, f32[48,128]{1,0:T(8,128)S(1)}, u32[]{:S(2)}, u32[]{:S(2)}) collective-permute-start(f32[48,128]{1,0:T(8,128)} %get-tuple-element.23), channel_id=1, source_target_pairs={{0,1},{1,0},{2,3},{3,2},{4,5},{5,4},{6,7},{7,6},{8,9},{9,8},{10,11... | collective-permute-start | bytes 73736 | tf_op jit(solution)/shard_map/ppermute | solution.py:560
  21.5 0.7 broadcast_in_dim.3.slot_ref
  22.2 0.0 copy-start.1
  22.2 0.7 copy-done.1
  22.9 0.0 copy-start.2
  22.9 0.9 %copy-done.2 = f32[48,768]{1,0:T(8,128)S(1)} copy-done((f32[48,768]{1,0:T(8,128)S(1)}, f32[48,768]{1,0:T(8,128)}, u32[]{:S(2)}) %copy-start.2) | copy-done | bytes 147480
  23.8 1.4 %shard_map.87 = (f32[192,128]{1,0:T(8,128)S(1)}, f32[192,128]{1,0:T(8,128)S(1)}, s32[8,768]{1,0:T(8,128)S(1)}, f32[8,1024]{1,0:T(8,128)S(1)}) custom-call(f32[48,768]{1,0:T(8,128)S(1)} %copy-done.2, s32[8,48]{1,0:T(8,128)S(1)} %copy-done.1, s32[1,768]{1,0:T(1,128)S(1)} %broadcast_in_dim.3.slot_ref), custom_call_target="tpu_custom_call" | custom-call | flops 400000000 | bytes 1000000 | tf_op jit(solution)/shard_map/pallas_call | solution.py:561
  25.2 0.0 collective-permute-done.from_far
  25.2 0.0 collective-permute-done.1.from_close
  25.2 0.1 shard_map.88
  25.4 2.8 %collective-permute-start.2 = (f32[192,128]{1,0:T(8,128)S(1)}, f32[192,128]{1,0:T(8,128)S(1)}, u32[]{:S(2)}, u32[]{:S(2)}) collective-permute-start(f32[192,128]{1,0:T(8,128)S(1)} %get-tuple-element.24), channel_id=1, source_target_pairs={{32,64},{64,32},{96,128},{128,96},{160,192},{192,160},{224,256},{2... | collective-permute-start | bytes 294920 | tf_op jit(solution)/shard_map/ppermute | solution.py:568
  28.1 7.0 %collective-permute-start.3 = (f32[192,128]{1,0:T(8,128)S(1)}, f32[192,128]{1,0:T(8,128)S(1)}, u32[]{:S(2)}, u32[]{:S(2)}) collective-permute-start(f32[192,128]{1,0:T(8,128)S(1)} %get-tuple-element.25), channel_id=1, source_target_pairs={{0,32},{32,0},{64,96},{96,64},{128,160},{160,128},{192,224},{224,1... | collective-permute-start | bytes 294920 | tf_op jit(solution)/shard_map/ppermute | solution.py:569
  35.1 0.0 copy-done
  35.1 1.4 %shard_map.89 = (f32[224,256]{1,0:T(8,128)S(1)}, f32[128,256]{1,0:T(8,128)S(1)}, f32[192,128]{1,0:T(8,128)S(1)}, bf16[768,1024]{1,0:T(8,128)(2,1)S(1)}) custom-call(f32[192,128]{1,0:T(8,128)S(1)} %get-tuple-element.26.low_ref, f32[192,128]{1,0:T(8,128)S(1)} %get-tuple-element.27.high_ref, f32[8,1024]{1,0:T(8,128)S(1)} %get-tuple-element.28.lists_ref, ...), custom_call_target="tpu_custom_call" | custom-call | flops 400000000 | bytes 1000000 | tf_op jit(solution)/shard_map/pallas_call | solution.py:576
  36.6 0.0 collective-permute-done.2.second_far_ref
  36.6 1.9 %collective-permute-done.3.first_far_ref = f32[192,128]{1,0:T(8,128)S(1)} collective-permute-done((f32[192,128]{1,0:T(8,128)S(1)}, f32[192,128]{1,0:T(8,128)S(1)}, u32[]{:S(2)}, u32[]{:S(2)}) %collective-permute-start.3) | collective-permute-done | bytes 98336 | tf_op jit(solution)/shard_map/ppermute | solution.py:569
  38.5 3.1 %shard_map.90 = (f32[40,1024]{1,0:T(8,128)S(1)}, f32[768,128]{1,0:T(8,128)}) custom-call(f32[192,128]{1,0:T(8,128)S(1)} %collective-permute-done.2.second_far_ref, f32[192,128]{1,0:T(8,128)S(1)} %collective-permute-done.3.first_far_ref, f32[192,128]{1,0:T(8,128)S(1)} %get-tuple-element.26.low_ref, f32[192,128]{1,0:T(8,128)S(1)} %get-tuple-element.27.high_ref, ...), custom_call_target="tpu_custom_call" | custom-call | tf_op jit(solution)/shard_map/pallas_call | solution.py:588
  41.6 8.9 %all-to-all-start = ((f32[32,24,128]{2,1,0:T(8,128)}), f32[32,24,128]{2,1,0:T(8,128)S(1)}, u32[]{:S(2)}, u32[]{:S(2)}) async-start(f32[32,24,128]{2,1,0:T(8,128)} %bitcast.1), calls=%async_computation | async-start | bytes 786432 | tf_op jit(solution)/shard_map/all_to_all | solution.py:595
  50.5 1.6 %shard_map.91 = f32[40,768]{1,0:T(8,128)} custom-call(f32[40,1024]{1,0:T(8,128)S(1)} %get-tuple-element.33.whole_ref, s32[8,768]{1,0:T(8,128)S(1)} %get-tuple-element.34.place_ref), custom_call_target="tpu_custom_call" | custom-call | flops 400000000 | bytes 1000000 | tf_op jit(solution)/shard_map/pallas_call | solution.py:596
  52.1 23.5 %all-to-all-done = f32[32,24,128]{2,1,0:T(8,128)S(1)} async-done(((f32[32,24,128]{2,1,0:T(8,128)}), f32[32,24,128]{2,1,0:T(8,128)S(1)}, u32[]{:S(2)}, u32[]{:S(2)}) %all-to-all-start) | async-done | bytes 393248 | tf_op jit(solution)/shard_map/all_to_all | solution.py:595
  75.6 1.8 %shard_map.92 = f32[40,768]{1,0:T(8,128)} custom-call(f32[768,128]{1,0:T(8,128)S(1)} %bitcast.4), custom_call_target="tpu_custom_call" | custom-call | tf_op jit(solution)/shard_map/pallas_call | solution.py:599
Async XLA Ops:
  2.8 32.3 %copy-start = (bf16[1664,256]{1,0:T(8,128)(2,1)S(1)}, bf16[1664,256]{1,0:T(8,128)(2,1)}, u32[]{:S(2)}) copy-start(bf16[1664,256]{1,0:T(8,128)(2,1)} %constant.2.clone.matrices) | copy-start | bytes 2555908
  2.8 22.4 %collective-permute-start = (f32[48,128]{1,0:T(8,128)}, f32[48,128]{1,0:T(8,128)S(1)}, u32[]{:S(2)}, u32[]{:S(2)}) collective-permute-start(f32[48,128]{1,0:T(8,128)} %get-tuple-element.22), channel_id=1, source_target_pairs={{1,2},{2,1},{3,4},{4,3},{5,6},{6,5},{7,8},{8,7},{9,10},{10,9},{11,... | collective-permute-start | bytes 73736 | tf_op jit(solution)/shard_map/ppermute | solution.py:559
  19.6 5.7 %collective-permute-start.1 = (f32[48,128]{1,0:T(8,128)}, f32[48,128]{1,0:T(8,128)S(1)}, u32[]{:S(2)}, u32[]{:S(2)}) collective-permute-start(f32[48,128]{1,0:T(8,128)} %get-tuple-element.23), channel_id=1, source_target_pairs={{0,1},{1,0},{2,3},{3,2},{4,5},{5,4},{6,7},{7,6},{8,9},{9,8},{10,11... | collective-permute-start | bytes 73736 | tf_op jit(solution)/shard_map/ppermute | solution.py:560
  22.2 0.7 copy-start.1
  22.9 0.9 %copy-start.2 = (f32[48,768]{1,0:T(8,128)S(1)}, f32[48,768]{1,0:T(8,128)}, u32[]{:S(2)}) copy-start(f32[48,768]{1,0:T(8,128)} %get-tuple-element.19.values_ref) | copy-start | bytes 442372
  25.4 11.2 %collective-permute-start.2 = (f32[192,128]{1,0:T(8,128)S(1)}, f32[192,128]{1,0:T(8,128)S(1)}, u32[]{:S(2)}, u32[]{:S(2)}) collective-permute-start(f32[192,128]{1,0:T(8,128)S(1)} %get-tuple-element.24), channel_id=1, source_target_pairs={{32,64},{64,32},{96,128},{128,96},{160,192},{192,160},{224,256},{2... | collective-permute-start | bytes 294920 | tf_op jit(solution)/shard_map/ppermute | solution.py:568
  28.1 10.3 %collective-permute-start.3 = (f32[192,128]{1,0:T(8,128)S(1)}, f32[192,128]{1,0:T(8,128)S(1)}, u32[]{:S(2)}, u32[]{:S(2)}) collective-permute-start(f32[192,128]{1,0:T(8,128)S(1)} %get-tuple-element.25), channel_id=1, source_target_pairs={{0,32},{32,0},{64,96},{96,64},{128,160},{160,128},{192,224},{224,1... | collective-permute-start | bytes 294920 | tf_op jit(solution)/shard_map/ppermute | solution.py:569
  41.6 34.0 %all-to-all-start = ((f32[32,24,128]{2,1,0:T(8,128)}), f32[32,24,128]{2,1,0:T(8,128)S(1)}, u32[]{:S(2)}, u32[]{:S(2)}) async-start(f32[32,24,128]{2,1,0:T(8,128)} %bitcast.1), calls=%async_computation | async-start | bytes 786432 | tf_op jit(solution)/shard_map/all_to_all | solution.py:595

commit v4 on v2

--- a/solution.py
+++ b/solution.py
@@ -137,8 +137,8 @@
 
 
 def strip_kernel(
-    state_ref, jacobian_ref, coriolis_ref, metric_ref, near_ref, far_ref, close_ref, values_ref,
-    near, jac, cor, metric, state, sems
+    state_ref, jacobian_ref, coriolis_ref, metric_ref, near_ref, slot_ref, far_ref, close_ref,
+    values_ref, near, jac, cor, metric, slot, state, sems
 ):
     copies = [
         pltpu.make_async_copy(source, target, sems.at[i])
@@ -149,6 +149,7 @@
                 (jacobian_ref, jac),
                 (coriolis_ref, cor),
                 (metric_ref, metric),
+                (slot_ref, slot),
             ]
         )
     ]
@@ -176,11 +177,13 @@
             jac[...].reshape(1, POINTS_DEV),
             cor[...].reshape(1, POINTS_DEV),
             metric[...],
-            jnp.zeros((2, POINTS_DEV), F32),
+            slot[...].astype(F32).reshape(1, POINTS_DEV),
+            jnp.zeros((1, POINTS_DEV), F32),
         ],
         axis=0,
     )
-    values_ref[...] = values
+    values_ref[0:TILE, :] = values
+    values_ref[TILE:, 0:ELEMS_DEV] = jnp.where(local, index, -1).astype(F32)
     parts = dot_last(jnp.concatenate(three_parts(values), axis=0), hits)
     strips = parts[0:TILE] + parts[TILE : 2 * TILE] + parts[2 * TILE :]
     even = lax.rem(lax.axis_index("col"), 2) == 0
@@ -189,26 +192,22 @@
     close_ref[...] = jnp.where(even, to_right, to_left)
 
 
-def arrange_kernel(values_ref, near_ref, slot_ref, low_ref, high_ref, place_ref, lists_ref):
-    index, local = local_lists(near_ref[...])
+def arrange_kernel(values_ref, low_ref, high_ref, place_ref):
+    index = values_ref[TILE:, 0:ELEMS_DEV].astype(jnp.int32)
+    local = index >= 0
     place = chain_length(local[0:1], index[0:1], 4)
     row = chain_length(local[2:3], index[2:3], 2)
     target = over_points(row * 16.0 + place + 2.0) * 16 + lane_iota((1, POINTS_DEV)) % 16
     place_ref[...] = jnp.broadcast_to(target, (8, POINTS_DEV))
     hits = (row_iota((1024, POINTS_DEV)) == target).astype(F32).astype(BF16)
-    columns = send_lists(slot_ref[...])
-    left = jnp.concatenate(three_parts(values_ref[...]), axis=0)
-    upper, rest = halves(columns)
-    left = jnp.concatenate([left, jnp.concatenate([columns, columns - upper.astype(F32)], axis=0).astype(BF16)], axis=0)
-    parts = dot_last(left, hits)
-    ordered = parts[0:TILE] + parts[TILE : 2 * TILE] + parts[2 * TILE : 3 * TILE]
+    parts = dot_last(jnp.concatenate(three_parts(values_ref[0:TILE, :]), axis=0), hits)
+    ordered = parts[0:TILE] + parts[TILE : 2 * TILE] + parts[2 * TILE :]
     for r in range(4):
         for g in range(2):
             block = ordered[:, (2 * r + g) * LANES : (2 * r + g + 1) * LANES]
             ref = low_ref if r < 2 else high_ref
             start = ((r % 2) * 2 + g) * TILE
             ref[start : start + TILE, :] = block
-    lists_ref[...] = parts[3 * TILE : 3 * TILE + 8] + parts[3 * TILE + 8 :]
 
 
 def turned(block, by):
@@ -247,33 +246,35 @@
     second_ref[...] = jnp.where(even, low, high)
 
 
-def send_lists(slot):
-    slot_value = slot.astype(F32)
-    device = jnp.floor((slot_value + 0.5) * (1.0 / POINTS_DEV))
-    within = slot_value - device * POINTS_DEV
-    wanted = jnp.broadcast_to(device.astype(jnp.int32), (N_COL, POINTS_DEV))
-    chosen = (wanted == row_iota((N_COL, POINTS_DEV))).astype(F32)
+def send_lists(slots):
     square = (LANES, LANES)
     upto = (row_iota(square) <= lane_iota(square)).astype(F32)
     count = jnp.concatenate([upto, jnp.ones(square, F32)], axis=1).astype(BF16)
-    groups = POINTS_DEV // LANES
-    stacked = jnp.concatenate(
-        [chosen[:, i * LANES : (i + 1) * LANES] for i in range(groups)], axis=0
-    )
-    counted = dot(stacked.astype(BF16), count)
+    lane = lane_iota((1, LANES))
+    chosen, devices, withins, owns = [], [], [], []
+    for i, slot in enumerate(slots):
+        own = lane >= 32 if i % 2 == 0 else lane < 96
+        device = jnp.where(own, jnp.floor((slot + 0.5) * (1.0 / POINTS_DEV)), -1.0)
+        wanted = jnp.broadcast_to(device.astype(jnp.int32), (N_COL, LANES))
+        chosen.append((wanted == row_iota((N_COL, LANES))).astype(F32))
+        devices.append(device)
+        withins.append(slot - device * POINTS_DEV)
+        owns.append(own)
+    counted = dot(jnp.concatenate(chosen, axis=0).astype(BF16), count)
     before = jnp.zeros((N_COL, LANES), F32)
-    ranks = []
-    for i in range(groups):
+    lists = []
+    for i, (device, within, own) in enumerate(zip(devices, withins, owns)):
         rows = counted[i * N_COL : (i + 1) * N_COL]
-        here = (rows[:, :LANES] + before) * stacked[i * N_COL : (i + 1) * N_COL]
-        ranks.append(jnp.sum(here, axis=0, keepdims=True))
+        rank = jnp.sum((rows[:, :LANES] + before) * chosen[i], axis=0, keepdims=True) - 1.0
         before = before + rows[:, LANES:]
-    rank = jnp.concatenate(ranks, axis=1) - 1.0
-    third = (rank >= CAP_ROWS).astype(F32) + (rank >= 2 * CAP_ROWS).astype(F32)
-    line = device * CAP_ROWS + rank - third * CAP_ROWS
-    lists = [jnp.where(third == float(k), line + 1.0, 0.0) for k in range(3)]
-    filler = jnp.zeros((4, POINTS_DEV), F32)
-    return jnp.concatenate(lists + [within + 1.0, filler], axis=0)
+        third = (rank >= CAP_ROWS).astype(F32) + (rank >= 2 * CAP_ROWS).astype(F32)
+        line = device * CAP_ROWS + rank - third * CAP_ROWS
+        parts = [jnp.where(own & (third == float(k)), line + 1.0, 0.0) for k in range(3)]
+        filler = jnp.zeros((4, LANES), F32)
+        lists.append(
+            jnp.concatenate(parts + [jnp.where(own, within + 1.0, 0.0), filler], axis=0)
+        )
+    return jnp.concatenate(lists, axis=1)
 
 
 def fluxes(slope, coefficients):
@@ -295,19 +296,49 @@
     return dot(upper, first) + dot(lower, first) + dot(upper, matrices[896:1408, :])
 
 
+def rows_joined(below, here, above, low_mask, high_mask):
+    parts = []
+    for g in range(2):
+        part = slice(g * LANES, (g + 1) * LANES)
+        parts.append(
+            here[:, part]
+            + low_mask * turned(below[:, part], -12)
+            + high_mask * turned(above[:, part], 12)
+        )
+    return parts
+
+
+def row_starts(rows):
+    slope, flux, plain = {}, {}, {}
+    at = [0, 0, 0]
+    for r in rows:
+        lean = r in (0, 7)
+        for g in range(2):
+            slope[r, g] = at[0]
+            at[0] += STATE if lean else TILE
+        flux[r] = at[1]
+        at[1] += STATE if lean else STATE + 16
+        plain[r] = at[2]
+        at[2] += 8 if lean else 32
+    return slope, flux, plain, at
+
+
 def local_terms(rows, tile, matrices, slopes, flux, plain, coefs, coefs_at):
-    cells = [(n, r, g) for n, r in enumerate(rows) for g in range(2)]
+    slope_at, flux_at, plain_at, _ = row_starts(rows)
+    cells = [(r, g) for r in rows for g in range(2)]
     stacked = []
-    for _, r, g in cells:
-        zonal, meridional = tile(r, g, 0, 8), tile(r, g, 8, 8)
-        energy = 0.5 * (zonal * zonal + meridional * meridional) + tile(r, g, 16, 8)
-        stacked += [tile(r, g, 0, STATE), energy]
+    for r, g in cells:
+        stacked.append(tile(r, g, 0, STATE))
+        if r not in (0, 7):
+            zonal, meridional = tile(r, g, 0, 8), tile(r, g, 8, 8)
+            energy = 0.5 * (zonal * zonal + meridional * meridional) + tile(r, g, 16, 8)
+            stacked.append(energy)
     slopes[...] = gradient(jnp.concatenate(stacked, axis=0), matrices)
     lane = lane_iota((8, LANES))
     inner_i = (lane % 4 == 1) | (lane % 4 == 2)
     inner_j = (lane // 4 % 4 == 1) | (lane // 4 % 4 == 2)
     weight = jnp.where(inner_i, 5.0 / 6.0, 1.0 / 6.0) * jnp.where(inner_j, 5.0 / 6.0, 1.0 / 6.0)
-    for n, r, g in cells:
+    for r, g in cells:
 
         def line(k):
             return jnp.broadcast_to(tile(r, g, STATE + k, 1), (8, LANES))
@@ -323,61 +354,138 @@
             coefs[at + 8 : at + 16, :] = cab
             coefs[at + 16 : at + 24, :] = cbb
         mass = jacobian * weight
-        at = (2 * n + g) * TILE
+        at = slope_at[r, g]
         first = slice(g * 2 * LANES, (g * 2 + 1) * LANES)
         second = slice((g * 2 + 1) * LANES, (g * 2 + 2) * LANES)
+        part = slice(g * LANES, (g + 1) * LANES)
+        to, direct = flux_at[r], plain_at[r]
         for f in range(FIELDS):
             one, two = fluxes(slopes[at + 8 * f : at + 8 * f + 8, :], (caa, cab, cbb))
-            flux[n * 56 + 8 * f : n * 56 + 8 * f + 8, first] = one
-            flux[n * 56 + 8 * f : n * 56 + 8 * f + 8, second] = two
+            flux[to + 8 * f : to + 8 * f + 8, first] = one
+            flux[to + 8 * f : to + 8 * f + 8, second] = two
+        plain[direct : direct + 8, part] = mass
+        if r in (0, 7):
+            continue
         zonal, meridional = tile(r, g, 0, 8), tile(r, g, 8, 8)
         flow1 = jacobian * (m11 * zonal + m12 * meridional)
         flow2 = jacobian * (m21 * zonal + m22 * meridional)
         for k in range(2):
             carried = tile(r, g, 24 + 8 * k, 8)
-            flux[n * 56 + 40 + 8 * k : n * 56 + 48 + 8 * k, first] = carried * flow1
-            flux[n * 56 + 40 + 8 * k : n * 56 + 48 + 8 * k, second] = carried * flow2
+            flux[to + 40 + 8 * k : to + 48 + 8 * k, first] = carried * flow1
+            flux[to + 40 + 8 * k : to + 48 + 8 * k, second] = carried * flow2
         ea, eb = slopes[at + 40 : at + 48, :LANES], slopes[at + 40 : at + 48, LANES:]
         ta, tb = slopes[at + 16 : at + 24, :LANES], slopes[at + 16 : at + 24, LANES:]
-        part = slice(g * LANES, (g + 1) * LANES)
-        plain[n * 32 : n * 32 + 8, part] = mass * (coriolis * meridional - (m11 * ea + m21 * eb))
-        plain[n * 32 + 8 : n * 32 + 16, part] = -mass * (coriolis * zonal + (m12 * ea + m22 * eb))
-        plain[n * 32 + 16 : n * 32 + 24, part] = -mass * (
+        plain[direct + 8 : direct + 16, part] = mass * (
+            coriolis * meridional - (m11 * ea + m21 * eb)
+        )
+        plain[direct + 16 : direct + 24, part] = -mass * (
+            coriolis * zonal + (m12 * ea + m22 * eb)
+        )
+        plain[direct + 24 : direct + 32, part] = -mass * (
             zonal * (m11 * ta + m21 * tb) + meridional * (m12 * ta + m22 * tb)
         )
-        plain[n * 32 + 24 : n * 32 + 32, part] = mass
     spread = divergence_joined(flux[...], matrices)
     upper, lower = halves(plain[...])
     join = matrices[1408:1664, :]
     return spread, dot(upper, join) + dot(lower, join)
 
 
+def face_masks():
+    lane = lane_iota((1, LANES)) % 16
+    return (lane < 4).astype(F32), (lane >= 12).astype(F32)
+
+
+def repeated(block):
+    return jnp.concatenate([block] * FIELDS, axis=0)
+
+
+def second_laplacian(rows, smoothing, inverse, coefficients, matrices):
+    smooth = [smoothing[r][g] * repeated(inverse[r, g]) for r in rows for g in range(2)]
+    again = gradient(jnp.concatenate(smooth, axis=0), matrices)
+    flat = []
+    for n, r in enumerate(rows):
+        parts = []
+        for g in range(2):
+            triple = tuple(repeated(coefficients(r, g, k)) for k in range(3))
+            start = (2 * n + g) * STATE
+            parts += list(fluxes(again[start : start + STATE, :], triple))
+        flat.append(jnp.concatenate(parts, axis=1))
+    return divergence_joined(jnp.concatenate(flat, axis=0), matrices)
+
+
+def mass_inverse(mass_sum):
+    return 1.0 / jnp.where(mass_sum > 0.0, mass_sum, 1.0)
+
+
+def advanced(state, straight, carried, inverse):
+    return state + (TIME_STEP * jnp.concatenate([straight, -carried], axis=0)) * repeated(inverse)
+
+
+OWN_ROWS = (2, 3, 4, 5)
+OUTER_ROWS = (0, 1, 6, 7)
+MIDDLE_ROWS = (3, 4)
+EDGE_ROWS = (1, 2, 5, 6)
+
+
 def inner_kernel(
-    low_ref, high_ref, lists_ref, matrices, spread_ref, direct_ref, coefs, picks_ref, slopes, flux, plain
+    low_ref,
+    high_ref,
+    matrices,
+    lists_ref,
+    spread_ref,
+    direct_ref,
+    coefs,
+    picks_ref,
+    middle_ref,
+    damped_ref,
+    inverse_ref,
+    slopes,
+    flux,
+    plain,
 ):
     def tile(r, g, start=0, size=TILE):
         offset = ((r % 2) * 2 + g) * TILE + start
-        return (low_ref if r < 2 else high_ref)[offset : offset + size, :]
-
+        return (low_ref if r < 4 else high_ref)[offset : offset + size, :]
+
+    def coefs_at(r, g):
+        return (2 * (r - 2) + g) * 24
+
+    lists = send_lists([tile(r, g, STATE + 6, 1) for r in OWN_ROWS for g in range(2)])
+    lists_ref[...] = lists
+    line = (lists[0:1] + lists[1:2] + lists[2:3]).astype(jnp.int32) - 1
+    picks_ref[...] = (row_iota((POINTS_DEV, 1024)) == line).astype(F32).astype(BF16)
     spread, direct = local_terms(
-        range(4), tile, matrices, slopes, flux, plain, coefs, lambda r, g: (2 * r + g) * 24
+        OWN_ROWS, tile, matrices, slopes, flux, plain, coefs, coefs_at
     )
     spread_ref[...] = spread
     direct_ref[...] = direct
-    line = (lists_ref[0:1, :] + lists_ref[1:2, :] + lists_ref[2:3, :]).astype(jnp.int32) - 1
-    picks_ref[...] = (row_iota((POINTS_DEV, 1024)) == line).astype(F32).astype(BF16)
-
-
-def rows_joined(below, here, above, low_mask, high_mask):
-    parts = []
-    for g in range(2):
-        part = slice(g * LANES, (g + 1) * LANES)
-        parts.append(
-            here[:, part]
-            + low_mask * turned(below[:, part], -12)
-            + high_mask * turned(above[:, part], 12)
-        )
-    return parts
+    masks = face_masks()
+
+    def joined(value, size, r, start, count):
+        def rows(k):
+            at = (k - 2) * size + start
+            return value[at : at + count, :]
+
+        return rows_joined(rows(r - 1), rows(r), rows(r + 1), *masks)
+
+    inverse, smoothing = {}, {}
+    for r in MIDDLE_ROWS:
+        mass_sum = joined(direct, 32, r, 0, 8)
+        smoothing[r] = joined(spread, 56, r, 0, STATE)
+        straight = joined(direct, 32, r, 8, 24)
+        carried = joined(spread, 56, r, STATE, 16)
+        for g in range(2):
+            inverse[r, g] = mass_inverse(mass_sum[g])
+            at = 2 * (r - 3) + g
+            inverse_ref[8 * at : 8 * at + 8, :] = inverse[r, g]
+            middle_ref[STATE * at : STATE * at + STATE, :] = advanced(
+                tile(r, g, 0, STATE), straight[g], carried[g], inverse[r, g]
+            )
+
+    def coefficients(r, g, k):
+        return coefs[coefs_at(r, g) + 8 * k : coefs_at(r, g) + 8 * k + 8, :]
+
+    damped_ref[...] = second_laplacian(MIDDLE_ROWS, smoothing, inverse, coefficients, matrices)
 
 
 def section_kernel(
@@ -391,6 +499,9 @@
     inner_spread,
     inner_direct,
     inner_coefs,
+    middle_ref,
+    middle_damped,
+    middle_inverse,
     whole_ref,
     send_ref,
     outside,
@@ -405,13 +516,12 @@
 
     def tile(r, g, start=0, size=TILE):
         offset = ((r % 2) * 2 + g) * TILE + start
-        if r in (0, 1, 6, 7):
+        if r in OUTER_ROWS:
             return outside[r // 6, offset : offset + size, :]
         return (low_ref if r < 4 else high_ref)[offset : offset + size, :]
 
-    outer_rows = (0, 1, 6, 7)
     outer_spread, outer_direct = local_terms(
-        outer_rows,
+        OUTER_ROWS,
         tile,
         matrices,
         slopes,
@@ -420,67 +530,60 @@
         outer_coefs,
         lambda r, g: {1: 24 * g, 6: 48 + 24 * g}.get(r),
     )
-
-    lane = lane_iota((1, LANES)) % 16
-    low_mask = (lane < 4).astype(F32)
-    high_mask = (lane >= 12).astype(F32)
-
-    def joined(outer, inner, size, r, start, count):
+    masks = face_masks()
+    _, outer_flux_at, outer_plain_at, _ = row_starts(OUTER_ROWS)
+    _, inner_flux_at, inner_plain_at, _ = row_starts(OWN_ROWS)
+
+    def joined(spread, r, start, count):
         def rows(k):
-            if k in outer_rows:
-                at = outer_rows.index(k) * size + start
-                return outer[at : at + count, :]
-            at = (k - 2) * size + start
-            return inner[at : at + count, :]
-
-        return rows_joined(rows(r - 1), rows(r), rows(r + 1), low_mask, high_mask)
+            if k in OUTER_ROWS:
+                at = (outer_flux_at if spread else outer_plain_at)[k] + start
+                return (outer_spread if spread else outer_direct)[at : at + count, :]
+            at = (inner_flux_at if spread else inner_plain_at)[k] + start
+            return (inner_spread if spread else inner_direct)[at : at + count, :]
+
+        return rows_joined(rows(r - 1), rows(r), rows(r + 1), *masks)
 
     def coefficients(r, g, k):
-        if r in outer_rows:
+        if r in OUTER_ROWS:
             at = (0 if r == 1 else 48) + 24 * g + 8 * k
             return outer_coefs[at : at + 8, :]
         at = (2 * (r - 2) + g) * 24 + 8 * k
         return inner_coefs[at : at + 8, :]
 
-    inverse = {}
-    smooth = []
-    for r in range(1, 7):
-        mass_sum = joined(outer_direct, inner_direct, 32, r, 24, 8)
-        smoothing = joined(outer_spread, inner_spread, 56, r, 0, STATE)
+    inverse, smoothing = {}, {}
+    for r in EDGE_ROWS:
+        mass_sum = joined(False, r, 0, 8)
+        smoothing[r] = joined(True, r, 0, STATE)
         for g in range(2):
-            inverse[r, g] = 1.0 / jnp.where(mass_sum[g] > 0.0, mass_sum[g], 1.0)
-            smooth.append(smoothing[g] * jnp.concatenate([inverse[r, g]] * FIELDS, axis=0))
-    again = gradient(jnp.concatenate(smooth, axis=0), matrices)
-    flat = []
-    for r in range(1, 7):
-        parts = []
+            inverse[r, g] = mass_inverse(mass_sum[g])
+    for r in MIDDLE_ROWS:
         for g in range(2):
-            triple = tuple(
-                jnp.concatenate([coefficients(r, g, k)] * FIELDS, axis=0) for k in range(3)
+            at = 8 * (2 * (r - 3) + g)
+            inverse[r, g] = middle_inverse[at : at + 8, :]
+    damped = second_laplacian(EDGE_ROWS, smoothing, inverse, coefficients, matrices)
+
+    def damped_row(r):
+        if r in MIDDLE_ROWS:
+            return middle_damped[(r - 3) * STATE : (r - 2) * STATE, :]
+        at = EDGE_ROWS.index(r) * STATE
+        return damped[at : at + STATE, :]
+
+    ordered = []
+    for r in OWN_ROWS:
+        damping = rows_joined(damped_row(r - 1), damped_row(r), damped_row(r + 1), *masks)
+        if r not in MIDDLE_ROWS:
+            straight = joined(False, r, 8, 24)
+            carried = joined(True, r, STATE, 16)
+        for g in range(2):
+            if r in MIDDLE_ROWS:
+                at = STATE * (2 * (r - 3) + g)
+                base = middle_ref[at : at + STATE, :]
+            else:
+                base = advanced(tile(r, g, 0, STATE), straight[g], carried[g], inverse[r, g])
+            ordered.append(
+                base - ((TIME_STEP * HYPER_NU) * damping[g]) * repeated(inverse[r, g])
             )
-            start = (2 * (r - 1) + g) * STATE
-            parts += list(fluxes(again[start : start + STATE, :], triple))
-        flat.append(jnp.concatenate(parts, axis=1))
-    damped = divergence_joined(jnp.concatenate(flat, axis=0), matrices)
-
-    ordered = []
-    for r in range(2, 6):
-        straight = joined(outer_direct, inner_direct, 32, r, 0, 24)
-        carried = joined(outer_spread, inner_spread, 56, r, STATE, 16)
-        damping = rows_joined(
-            damped[(r - 2) * STATE : (r - 1) * STATE, :],
-            damped[(r - 1) * STATE : r * STATE, :],
-            damped[r * STATE : (r + 1) * STATE, :],
-            low_mask,
-            high_mask,
-        )
-        for g in range(2):
-            change = (
-                TIME_STEP * jnp.concatenate([straight[g], -carried[g]], axis=0)
-                - (TIME_STEP * HYPER_NU) * damping[g]
-            )
-            scale = jnp.concatenate([inverse[r, g]] * FIELDS, axis=0)
-            ordered.append(tile(r, g, 0, STATE) + change * scale)
     whole = jnp.concatenate(ordered, axis=1)
     whole_ref[...] = whole
     shares = [(lists_ref[k : k + 1, :] > 0.0).astype(F32) for k in range(3)]
@@ -504,16 +607,19 @@
     upper, lower = halves(turned_over)
     places = slice(3 * STATE, 3 * STATE + 3)
     slot = turned_over[places, :].astype(jnp.int32) - 1
-    row = row_iota((POINTS_DEV, POINTS_DEV))
-    hits = (row == slot[0:1]) | (row == slot[1:2]) | (row == slot[2:3])
-    rows = dot_last(jnp.concatenate([upper, lower], axis=0), hits.astype(F32).astype(BF16))
-    rows = rows[:LANES] + rows[LANES:]
-    own = rows[places, :] == (lane_iota((3, POINTS_DEV)) + 1).astype(F32)
-    physics_ref[...] = jnp.where(
-        own[0:1],
-        rows[:STATE],
-        jnp.where(own[1:2], rows[STATE : 2 * STATE], rows[2 * STATE : 3 * STATE]),
-    )
+    both = jnp.concatenate([upper, lower], axis=0)
+    count = 2 * LANES
+    for start in range(0, POINTS_DEV, count):
+        row = row_iota((count, POINTS_DEV)) + start
+        hits = (row == slot[0:1]) | (row == slot[1:2]) | (row == slot[2:3])
+        rows = dot_last(both, hits.astype(F32).astype(BF16))
+        rows = rows[:LANES] + rows[LANES:]
+        own = rows[places, :] == (lane_iota((3, count)) + (start + 1)).astype(F32)
+        physics_ref[:, start : start + count] = jnp.where(
+            own[0:1],
+            rows[:STATE],
+            jnp.where(own[1:2], rows[STATE : 2 * STATE], rows[2 * STATE : 3 * STATE]),
+        )
 
 
 def call(kernel, shapes, scratch=(), flops=0, moved=0, vmem=VMEM_LIMIT, **specs):
@@ -540,7 +646,7 @@
     anywhere = pl.BlockSpec(memory_space=pltpu.HBM)
     half = ((4 * TILE, LANES), F32)
     strip = ((TILE, LANES), F32)
-    values_shape = ((TILE, POINTS_DEV), F32)
+    values_shape = ((TILE + 8, POINTS_DEV), F32)
     far, close, values = call(
         strip_kernel,
         [strip, strip, values_shape],
@@ -549,49 +655,72 @@
             pltpu.VMEM((POINTS_DEV,), F32),
             pltpu.VMEM((POINTS_DEV,), F32),
             pltpu.VMEM((4, POINTS_DEV), F32),
+            pltpu.VMEM((POINTS_DEV,), jnp.int32),
             pltpu.VMEM((FIELDS, LEV, POINTS_DEV), F32),
-            pltpu.SemaphoreType.DMA((5,)),
+            pltpu.SemaphoreType.DMA((6,)),
         ],
-        in_specs=[anywhere] * 5,
+        in_specs=[anywhere] * 6,
         vmem=64 * 1024 * 1024 - 524288,
-    )(evolving_state_array, jacobian, coriolis, inverse_metric, neighbours)
+    )(evolving_state_array, jacobian, coriolis, inverse_metric, neighbours, column_slot)
     cols, rows = lax.axis_size("col"), lax.axis_size("curve")
     from_far = lax.ppermute(far, "col", swaps(cols, 1) + [(cols - 1, 0), (0, cols - 1)])
     from_close = lax.ppermute(close, "col", swaps(cols, 0))
-    low, high, place, lists = call(
+    low, high, place = call(
         arrange_kernel,
-        [half, half, ((8, POINTS_DEV), jnp.int32), ((8, 1024), F32)],
+        [half, half, ((8, POINTS_DEV), jnp.int32)],
         flops=400_000_000,
         moved=1_000_000,
-    )(values, neighbours, column_slot[None])
+    )(values)
     first, second, low, high = call(margin_kernel, [half] * 4)(low, high, from_far, from_close)
     second_far = lax.ppermute(second, "curve", swaps(rows, 1))
     first_far = lax.ppermute(first, "curve", swaps(rows, 0))
     matrices = jnp.asarray(operators())
-    scratch = [
-        pltpu.VMEM((8 * TILE, 2 * LANES), F32),
-        pltpu.VMEM((4 * 56, 4 * LANES), F32),
-        pltpu.VMEM((4 * 32, 2 * LANES), F32),
-    ]
-    spread, direct, coefs, picks = call(
+    def scratch(rows):
+        slope_rows, flux_rows, plain_rows = row_starts(rows)[3]
+        return [
+            pltpu.VMEM((slope_rows, 2 * LANES), F32),
+            pltpu.VMEM((flux_rows, 4 * LANES), F32),
+            pltpu.VMEM((plain_rows, 2 * LANES), F32),
+        ]
+
+    inner = call(
         inner_kernel,
         [
+            ((8, 1024), F32),
             ((4 * 56, 2 * LANES), F32),
             ((4 * 32, 2 * LANES), F32),
             ((8 * 24, LANES), F32),
             ((POINTS_DEV, 1024), BF16),
+            ((4 * STATE, LANES), F32),
+            ((2 * STATE, 2 * LANES), F32),
+            ((4 * 8, LANES), F32),
         ],
-        scratch=scratch,
+        scratch=scratch(OWN_ROWS),
         flops=400_000_000,
         moved=1_000_000,
-    )(low, high, lists, matrices)
+    )(low, high, matrices)
+    lists, spread, direct, coefs, picks, middle, middle_damped, middle_inverse = inner
     whole, sent = call(
         section_kernel,
         [((STATE, 1024), F32), ((POINTS_DEV, LANES), F32)],
         scratch=[pltpu.VMEM((2, 4 * TILE, LANES), F32)]
-        + scratch
+        + scratch(OUTER_ROWS)
         + [pltpu.VMEM((4 * 24, LANES), F32)],
-    )(first_far, second_far, low, high, lists, picks, matrices, spread, direct, coefs)
+    )(
+        first_far,
+        second_far,
+        low,
+        high,
+        lists,
+        picks,
+        matrices,
+        spread,
+        direct,
+        coefs,
+        middle,
+        middle_damped,
+        middle_inverse,
+    )
     received = lax.all_to_all(sent, "col", split_axis=0, concat_axis=0, tiled=True)
     (updated,) = call(
         restore_kernel, [((STATE, POINTS_DEV), F32)], flops=400_000_000, moved=1_000_000

time: 76.6 us -> 76.3 us (level)
  starting transfers between devices: 39.4 us -> 40.8 us
  local copies, waits for them, and re-layouts: 2.29 us -> 0.92 us
    all_to_all x1, starting transfers between devices: 9.5 us -> 10.9 us  [body(): lax.all_to_all(sent, 'col', split_axis=0, concat_axis=0, tiled=True)]
    unnamed x6 -> x4, local copies, waits for them, and re-layouts: 1.6 us -> 0.92 us
  transfers between devices with their start and end apart: 5 -> 5, of which waited for: 2 -> 2; matrix products, arithmetic and copies ran while one was open for 1% -> 0% of each run, Pallas kernels for 6% -> 7%
where the time goes in v4:
time: 76.3 us; the launch traced here: 75.9 us
  starting transfers between devices  40.8 us (53%)
  waiting for transfers between devices  21.4 us (28%)
  Pallas kernels  12 us (16%)
  local copies, waits for them, and re-layouts  0.92 us (1%)
  between operations  0.77 us (1%)
    all_to_all x1, waiting for transfers between devices, body(): lax.all_to_all(sent, 'col', split_axis=0, concat_axis=0, tiled=True)  17.9 us
    ppermute x1, starting transfers between devices, body(): lax.ppermute(far, 'col', swaps(cols, 1) + [(cols - 1, 0), (0, cols - 1)])  17.6 us
    all_to_all x1, starting transfers between devices, body(): lax.all_to_all(sent, 'col', split_axis=0, concat_axis=0, tiled=True)  10.9 us
    ppermute x1, starting transfers between devices, body(): second_far = lax.ppermute(second, 'curve', swaps(rows, 1))  6.97 us
    ppermute x1, waiting for transfers between devices, body(): second_far = lax.ppermute(second, 'curve', swaps(rows, 1))  3.46 us
    ppermute x1, starting transfers between devices, body(): first_far = lax.ppermute(first, 'curve', swaps(rows, 0))  3.38 us
    pallas_call x1, Pallas kernels, body(): call(section_kernel, [((STATE, 1024), F32), ((POINTS_DEV, LANES), F32)],...  2.82 us
    pallas_call x1, Pallas kernels, body(): call(strip_kernel, [strip, strip, values_shape], scratch=[pltpu.VMEM((8,...  2.22 us
  transfers between devices with their start and end apart: 5, of which 2 were waited for; matrix products, arithmetic and copies ran while one was open for 0% of the time, Pallas kernels for 7%

profile of v4, /device:TPU:6, one launch (start us, length us, event | category | flops | bytes accessed | tf_op | source)
XLA Modules:
  0.0 75.9 jit_solution(14396041940726574977)
XLA Ops:
  0.6 2.2 %shard_map.86 = (f32[48,128]{1,0:T(8,128)}, f32[48,128]{1,0:T(8,128)}, f32[56,768]{1,0:T(8,128)}) custom-call(f32[5,8,768]{2,1,0:T(8,128)} %state_ref.1, f32[768]{0:T(1024)} %jacobian_ref.1, f32[768]{0:T(1024)} %coriolis_ref.1, f32[4,768]{1,0:T(4,128)} %metric_ref.1, s32[8,48]{1,0:T(8,128)} %near_ref.1, s32[768]{0:T(1024)} %slot_ref.1), custom_call_target="tpu_custom_call" | custom-call | tf_op jit(solution)/shard_map/pallas_call | solution.py:650
  2.9 0.0 copy-start
  2.9 17.6 %collective-permute-start = (f32[48,128]{1,0:T(8,128)}, f32[48,128]{1,0:T(8,128)S(1)}, u32[]{:S(2)}, u32[]{:S(2)}) collective-permute-start(f32[48,128]{1,0:T(8,128)} %get-tuple-element.25), channel_id=1, source_target_pairs={{1,2},{2,1},{3,4},{4,3},{5,6},{6,5},{7,8},{8,7},{9,10},{10,9},{11,... | collective-permute-start | bytes 73736 | tf_op jit(solution)/shard_map/ppermute | solution.py:666
  20.5 1.9 %collective-permute-start.1 = (f32[48,128]{1,0:T(8,128)}, f32[48,128]{1,0:T(8,128)S(1)}, u32[]{:S(2)}, u32[]{:S(2)}) collective-permute-start(f32[48,128]{1,0:T(8,128)} %get-tuple-element.26), channel_id=1, source_target_pairs={{0,1},{1,0},{2,3},{3,2},{4,5},{5,4},{6,7},{7,6},{8,9},{9,8},{10,11... | collective-permute-start | bytes 73736 | tf_op jit(solution)/shard_map/ppermute | solution.py:667
  22.4 0.0 copy-start.1
  22.4 0.9 %copy-done.1 = f32[56,768]{1,0:T(8,128)S(1)} copy-done((f32[56,768]{1,0:T(8,128)S(1)}, f32[56,768]{1,0:T(8,128)}, u32[]{:S(2)}) %copy-start.1) | copy-done | bytes 172056
  23.3 1.4 %shard_map.87 = (f32[192,128]{1,0:T(8,128)S(1)}, f32[192,128]{1,0:T(8,128)S(1)}, s32[8,768]{1,0:T(8,128)S(1)}) custom-call(f32[56,768]{1,0:T(8,128)S(1)} %copy-done.1), custom_call_target="tpu_custom_call" | custom-call | flops 400000000 | bytes 1000000 | tf_op jit(solution)/shard_map/pallas_call | solution.py:668
  24.7 0.0 collective-permute-done.from_far
  24.8 0.0 collective-permute-done.1.from_close
  24.8 0.1 shard_map.88
  24.9 3.4 %collective-permute-start.2 = (f32[192,128]{1,0:T(8,128)S(1)}, f32[192,128]{1,0:T(8,128)S(1)}, u32[]{:S(2)}, u32[]{:S(2)}) collective-permute-start(f32[192,128]{1,0:T(8,128)S(1)} %get-tuple-element.27), channel_id=1, source_target_pairs={{0,32},{32,0},{64,96},{96,64},{128,160},{160,128},{192,224},{224,1... | collective-permute-start | bytes 294920 | tf_op jit(solution)/shard_map/ppermute | solution.py:676
  28.3 7.0 %collective-permute-start.3 = (f32[192,128]{1,0:T(8,128)S(1)}, f32[192,128]{1,0:T(8,128)S(1)}, u32[]{:S(2)}, u32[]{:S(2)}) collective-permute-start(f32[192,128]{1,0:T(8,128)S(1)} %get-tuple-element.28), channel_id=1, source_target_pairs={{32,64},{64,32},{96,128},{128,96},{160,192},{192,160},{224,256},{2... | collective-permute-start | bytes 294920 | tf_op jit(solution)/shard_map/ppermute | solution.py:675
  35.3 0.0 copy-done
  35.3 2.1 %shard_map.89 = (f32[8,1024]{1,0:T(8,128)S(1)}, f32[224,256]{1,0:T(8,128)S(1)}, f32[128,256]{1,0:T(8,128)S(1)}, f32[192,128]{1,0:T(8,128)S(1)}, bf16[768,1024]{1...) custom-call(f32[192,128]{1,0:T(8,128)S(1)} %get-tuple-element.29.low_ref, ...), custom_call_target="tpu_custom_call" | custom-call | flops 400000000 | bytes 1000000 | tf_op jit(solution)/shard_map/pallas_call | solution.py:686
  37.3 0.0 collective-permute-done.2.first_far_ref
  37.3 3.5 %collective-permute-done.3.second_far_ref = f32[192,128]{1,0:T(8,128)S(1)} collective-permute-done((f32[192,128]{1,0:T(8,128)S(1)}, f32[192,128]{1,0:T(8,128)S(1)}, u32[]{:S(2)}, u32[]{:S(2)}) %collective-permute-start.3) | collective-permute-done | bytes 98336 | tf_op jit(solution)/shard_map/ppermute | solution.py:675
  40.8 2.8 %shard_map.90 = (f32[40,1024]{1,0:T(8,128)S(1)}, f32[768,128]{1,0:T(8,128)}) custom-call(f32[192,128]{1,0:T(8,128)S(1)} %collective-permute-done.2.first_far_ref, f32[192,128]{1,0:T(8,128)S(1)} %collective-permute-done.3.second_far_ref, f32[192,128]{1,0:T(8,128)S(1)} %get-tuple-element.29.low_ref, f32[192,128]{1,0:T(8,128)S(1)} %get-tuple-element.30.high_ref, ...), custom_call_target="tpu_custom_call" | custom-call | tf_op jit(solution)/shard_map/pallas_call | solution.py:703
  43.6 10.9 %all-to-all-start = ((f32[32,24,128]{2,1,0:T(8,128)}), f32[32,24,128]{2,1,0:T(8,128)S(1)}, u32[]{:S(2)}, u32[]{:S(2)}) async-start(f32[32,24,128]{2,1,0:T(8,128)} %bitcast.1), calls=%async_computation | async-start | bytes 786432 | tf_op jit(solution)/shard_map/all_to_all | solution.py:724
  54.5 1.6 %shard_map.91 = f32[40,768]{1,0:T(8,128)} custom-call(f32[40,1024]{1,0:T(8,128)S(1)} %get-tuple-element.39.whole_ref, s32[8,768]{1,0:T(8,128)S(1)} %get-tuple-element.40.place_ref), custom_call_target="tpu_custom_call" | custom-call | flops 400000000 | bytes 1000000 | tf_op jit(solution)/shard_map/pallas_call | solution.py:725
  56.2 17.9 %all-to-all-done = f32[32,24,128]{2,1,0:T(8,128)S(1)} async-done(((f32[32,24,128]{2,1,0:T(8,128)}), f32[32,24,128]{2,1,0:T(8,128)S(1)}, u32[]{:S(2)}, u32[]{:S(2)}) %all-to-all-start) | async-done | bytes 393248 | tf_op jit(solution)/shard_map/all_to_all | solution.py:724
  74.1 1.8 %shard_map.92 = f32[40,768]{1,0:T(8,128)} custom-call(f32[768,128]{1,0:T(8,128)S(1)} %bitcast.4), custom_call_target="tpu_custom_call" | custom-call | tf_op jit(solution)/shard_map/pallas_call | solution.py:728
Async XLA Ops:
  2.9 32.4 %copy-start = (bf16[1664,256]{1,0:T(8,128)(2,1)S(1)}, bf16[1664,256]{1,0:T(8,128)(2,1)}, u32[]{:S(2)}) copy-start(bf16[1664,256]{1,0:T(8,128)(2,1)} %constant.2.clone.matrices) | copy-start | bytes 2555908
  2.9 21.9 %collective-permute-start = (f32[48,128]{1,0:T(8,128)}, f32[48,128]{1,0:T(8,128)S(1)}, u32[]{:S(2)}, u32[]{:S(2)}) collective-permute-start(f32[48,128]{1,0:T(8,128)} %get-tuple-element.25), channel_id=1, source_target_pairs={{1,2},{2,1},{3,4},{4,3},{5,6},{6,5},{7,8},{8,7},{9,10},{10,9},{11,... | collective-permute-start | bytes 73736 | tf_op jit(solution)/shard_map/ppermute | solution.py:666
  20.5 4.3 %collective-permute-start.1 = (f32[48,128]{1,0:T(8,128)}, f32[48,128]{1,0:T(8,128)S(1)}, u32[]{:S(2)}, u32[]{:S(2)}) collective-permute-start(f32[48,128]{1,0:T(8,128)} %get-tuple-element.26), channel_id=1, source_target_pairs={{0,1},{1,0},{2,3},{3,2},{4,5},{5,4},{6,7},{7,6},{8,9},{9,8},{10,11... | collective-permute-start | bytes 73736 | tf_op jit(solution)/shard_map/ppermute | solution.py:667
  22.4 0.9 %copy-start.1 = (f32[56,768]{1,0:T(8,128)S(1)}, f32[56,768]{1,0:T(8,128)}, u32[]{:S(2)}) copy-start(f32[56,768]{1,0:T(8,128)} %get-tuple-element.22.values_ref) | copy-start | bytes 516100
  24.9 12.4 %collective-permute-start.2 = (f32[192,128]{1,0:T(8,128)S(1)}, f32[192,128]{1,0:T(8,128)S(1)}, u32[]{:S(2)}, u32[]{:S(2)}) collective-permute-start(f32[192,128]{1,0:T(8,128)S(1)} %get-tuple-element.27), channel_id=1, source_target_pairs={{0,32},{32,0},{64,96},{96,64},{128,160},{160,128},{192,224},{224,1... | collective-permute-start | bytes 294920 | tf_op jit(solution)/shard_map/ppermute | solution.py:676
  28.3 12.5 %collective-permute-start.3 = (f32[192,128]{1,0:T(8,128)S(1)}, f32[192,128]{1,0:T(8,128)S(1)}, u32[]{:S(2)}, u32[]{:S(2)}) collective-permute-start(f32[192,128]{1,0:T(8,128)S(1)} %get-tuple-element.28), channel_id=1, source_target_pairs={{32,64},{64,32},{96,128},{128,96},{160,192},{192,160},{224,256},{2... | collective-permute-start | bytes 294920 | tf_op jit(solution)/shard_map/ppermute | solution.py:675
  43.6 30.5 %all-to-all-start = ((f32[32,24,128]{2,1,0:T(8,128)}), f32[32,24,128]{2,1,0:T(8,128)S(1)}, u32[]{:S(2)}, u32[]{:S(2)}) async-start(f32[32,24,128]{2,1,0:T(8,128)} %bitcast.1), calls=%async_computation | async-start | bytes 786432 | tf_op jit(solution)/shard_map/all_to_all | solution.py:724

commit v5 on v4

--- a/solution.py
+++ b/solution.py
@@ -625,7 +625,9 @@
 def call(kernel, shapes, scratch=(), flops=0, moved=0, vmem=VMEM_LIMIT, **specs):
     return pl.pallas_call(
         kernel,
-        out_shape=[jax.ShapeDtypeStruct(s, d) for s, d in shapes],
+        out_shape=[
+            jax.ShapeDtypeStruct(*s) if isinstance(s, tuple) else s for s in shapes
+        ],
         scratch_shapes=list(scratch),
         **specs,
         compiler_params=pltpu.CompilerParams(vmem_limit_bytes=vmem),
@@ -649,7 +651,7 @@
     values_shape = ((TILE + 8, POINTS_DEV), F32)
     far, close, values = call(
         strip_kernel,
-        [strip, strip, values_shape],
+        [pltpu.VMEM(*strip), pltpu.VMEM(*strip), pltpu.VMEM(*values_shape)],
         scratch=[
             pltpu.VMEM((8, ELEMS_DEV), jnp.int32),
             pltpu.VMEM((POINTS_DEV,), F32),

time: 76.3 us -> 75.4 us (0.988)
  local copies, waits for them, and re-layouts: 0.92 us -> 0.01 us
    unnamed x4 -> x2, local copies, waits for them, and re-layouts: 0.92 us -> 0.01 us
where the time goes in v5:
time: 75.4 us; the launch traced here: 75 us
  starting transfers between devices  41.5 us (55%)
  waiting for transfers between devices  21.4 us (28%)
  Pallas kernels  11.4 us (15%)
  between operations  0.76 us (1%)
    all_to_all x1, waiting for transfers between devices, body(): lax.all_to_all(sent, 'col', split_axis=0, concat_axis=0, tiled=True)  17.9 us
    ppermute x1, starting transfers between devices, body(): lax.ppermute(far, 'col', swaps(cols, 1) + [(cols - 1, 0), (0, cols - 1)])  17.6 us
    all_to_all x1, starting transfers between devices, body(): lax.all_to_all(sent, 'col', split_axis=0, concat_axis=0, tiled=True)  11.6 us
    ppermute x1, starting transfers between devices, body(): second_far = lax.ppermute(second, 'curve', swaps(rows, 1))  6.97 us
    ppermute x1, waiting for transfers between devices, body(): second_far = lax.ppermute(second, 'curve', swaps(rows, 1))  3.46 us
    ppermute x1, starting transfers between devices, body(): first_far = lax.ppermute(first, 'curve', swaps(rows, 0))  3.38 us
    pallas_call x1, Pallas kernels, body(): call(section_kernel, [((STATE, 1024), F32), ((POINTS_DEV, LANES), F32)],...  2.82 us
    pallas_call x1, Pallas kernels, body(): call(inner_kernel, [((8, 1024), F32), ((4 * 56, 2 * LANES), F32), ((4 * 3...  2.05 us
  transfers between devices with their start and end apart: 5, of which 2 were waited for; matrix products, arithmetic and copies ran while one was open for 0% of the time, Pallas kernels for 7%

profile of v5, /device:TPU:6, one launch (start us, length us, event | category | flops | bytes accessed | tf_op | source)
XLA Modules:
  0.0 75.0 jit_solution(3515876369437230829)
XLA Ops:
  0.6 1.5 %shard_map.86 = (f32[48,128]{1,0:T(8,128)S(1)}, f32[48,128]{1,0:T(8,128)S(1)}, f32[56,768]{1,0:T(8,128)S(1)}) custom-call(f32[5,8,768]{2,1,0:T(8,128)} %state_ref.1, f32[768]{0:T(1024)} %jacobian_ref.1, f32[768]{0:T(1024)} %coriolis_ref.1, f32[4,768]{1,0:T(4,128)} %metric_ref.1, s32[8,48]{1,0:T(8,128)} %near_ref.1, s32[768]{0:T(1024)} %slot_ref.1), custom_call_target="tpu_custom_call" | custom-call | tf_op jit(solution)/shard_map/pallas_call | solution.py:652
  2.2 0.0 copy-start
  2.2 17.6 %collective-permute-start = (f32[48,128]{1,0:T(8,128)S(1)}, f32[48,128]{1,0:T(8,128)S(1)}, u32[]{:S(2)}, u32[]{:S(2)}) collective-permute-start(f32[48,128]{1,0:T(8,128)S(1)} %get-tuple-element.25), channel_id=1, source_target_pairs={{1,2},{2,1},{3,4},{4,3},{5,6},{6,5},{7,8},{8,7},{9,10},{10,9},{11,... | collective-permute-start | bytes 73736 | tf_op jit(solution)/shard_map/ppermute | solution.py:668
  19.8 1.9 %collective-permute-start.1 = (f32[48,128]{1,0:T(8,128)S(1)}, f32[48,128]{1,0:T(8,128)S(1)}, u32[]{:S(2)}, u32[]{:S(2)}) collective-permute-start(f32[48,128]{1,0:T(8,128)S(1)} %get-tuple-element.26), channel_id=1, source_target_pairs={{0,1},{1,0},{2,3},{3,2},{4,5},{5,4},{6,7},{7,6},{8,9},{9,8},{10,11... | collective-permute-start | bytes 73736 | tf_op jit(solution)/shard_map/ppermute | solution.py:669
  21.7 1.4 %shard_map.87 = (f32[192,128]{1,0:T(8,128)S(1)}, f32[192,128]{1,0:T(8,128)S(1)}, s32[8,768]{1,0:T(8,128)S(1)}) custom-call(f32[56,768]{1,0:T(8,128)S(1)} %get-tuple-element.22.values_ref), custom_call_target="tpu_custom_call" | custom-call | flops 400000000 | bytes 1000000 | tf_op jit(solution)/shard_map/pallas_call | solution.py:670
  23.1 0.0 collective-permute-done.from_far
  23.2 0.0 collective-permute-done.1.from_close
  23.2 0.1 shard_map.88
  23.3 3.4 %collective-permute-start.2 = (f32[192,128]{1,0:T(8,128)S(1)}, f32[192,128]{1,0:T(8,128)S(1)}, u32[]{:S(2)}, u32[]{:S(2)}) collective-permute-start(f32[192,128]{1,0:T(8,128)S(1)} %get-tuple-element.27), channel_id=1, source_target_pairs={{0,32},{32,0},{64,96},{96,64},{128,160},{160,128},{192,224},{224,1... | collective-permute-start | bytes 294920 | tf_op jit(solution)/shard_map/ppermute | solution.py:678
  26.7 7.0 %collective-permute-start.3 = (f32[192,128]{1,0:T(8,128)S(1)}, f32[192,128]{1,0:T(8,128)S(1)}, u32[]{:S(2)}, u32[]{:S(2)}) collective-permute-start(f32[192,128]{1,0:T(8,128)S(1)} %get-tuple-element.28), channel_id=1, source_target_pairs={{32,64},{64,32},{96,128},{128,96},{160,192},{192,160},{224,256},{2... | collective-permute-start | bytes 294920 | tf_op jit(solution)/shard_map/ppermute | solution.py:677
  33.7 0.0 copy-done
  33.7 2.1 %shard_map.89 = (f32[8,1024]{1,0:T(8,128)S(1)}, f32[224,256]{1,0:T(8,128)S(1)}, f32[128,256]{1,0:T(8,128)S(1)}, f32[192,128]{1,0:T(8,128)S(1)}, bf16[768,1024]{1...) custom-call(f32[192,128]{1,0:T(8,128)S(1)} %get-tuple-element.29.low_ref, ...), custom_call_target="tpu_custom_call" | custom-call | flops 400000000 | bytes 1000000 | tf_op jit(solution)/shard_map/pallas_call | solution.py:688
  35.7 0.0 collective-permute-done.2.first_far_ref
  35.7 3.5 %collective-permute-done.3.second_far_ref = f32[192,128]{1,0:T(8,128)S(1)} collective-permute-done((f32[192,128]{1,0:T(8,128)S(1)}, f32[192,128]{1,0:T(8,128)S(1)}, u32[]{:S(2)}, u32[]{:S(2)}) %collective-permute-start.3) | collective-permute-done | bytes 98336 | tf_op jit(solution)/shard_map/ppermute | solution.py:677
  39.2 2.8 %shard_map.90 = (f32[40,1024]{1,0:T(8,128)S(1)}, f32[768,128]{1,0:T(8,128)}) custom-call(f32[192,128]{1,0:T(8,128)S(1)} %collective-permute-done.2.first_far_ref, f32[192,128]{1,0:T(8,128)S(1)} %collective-permute-done.3.second_far_ref, f32[192,128]{1,0:T(8,128)S(1)} %get-tuple-element.29.low_ref, f32[192,128]{1,0:T(8,128)S(1)} %get-tuple-element.30.high_ref, ...), custom_call_target="tpu_custom_call" | custom-call | tf_op jit(solution)/shard_map/pallas_call | solution.py:705
  42.0 11.6 %all-to-all-start = ((f32[32,24,128]{2,1,0:T(8,128)}), f32[32,24,128]{2,1,0:T(8,128)S(1)}, u32[]{:S(2)}, u32[]{:S(2)}) async-start(f32[32,24,128]{2,1,0:T(8,128)} %bitcast.1), calls=%async_computation | async-start | bytes 786432 | tf_op jit(solution)/shard_map/all_to_all | solution.py:726
  53.6 1.6 %shard_map.91 = f32[40,768]{1,0:T(8,128)} custom-call(f32[40,1024]{1,0:T(8,128)S(1)} %get-tuple-element.39.whole_ref, s32[8,768]{1,0:T(8,128)S(1)} %get-tuple-element.40.place_ref), custom_call_target="tpu_custom_call" | custom-call | flops 400000000 | bytes 1000000 | tf_op jit(solution)/shard_map/pallas_call | solution.py:727
  55.3 17.9 %all-to-all-done = f32[32,24,128]{2,1,0:T(8,128)S(1)} async-done(((f32[32,24,128]{2,1,0:T(8,128)}), f32[32,24,128]{2,1,0:T(8,128)S(1)}, u32[]{:S(2)}, u32[]{:S(2)}) %all-to-all-start) | async-done | bytes 393248 | tf_op jit(solution)/shard_map/all_to_all | solution.py:726
  73.2 1.8 %shard_map.92 = f32[40,768]{1,0:T(8,128)} custom-call(f32[768,128]{1,0:T(8,128)S(1)} %bitcast.4), custom_call_target="tpu_custom_call" | custom-call | tf_op jit(solution)/shard_map/pallas_call | solution.py:730
Async XLA Ops:
  2.2 31.5 %copy-start = (bf16[1664,256]{1,0:T(8,128)(2,1)S(1)}, bf16[1664,256]{1,0:T(8,128)(2,1)}, u32[]{:S(2)}) copy-start(bf16[1664,256]{1,0:T(8,128)(2,1)} %constant.2.clone.matrices) | copy-start | bytes 2555908
  2.2 21.0 %collective-permute-start = (f32[48,128]{1,0:T(8,128)S(1)}, f32[48,128]{1,0:T(8,128)S(1)}, u32[]{:S(2)}, u32[]{:S(2)}) collective-permute-start(f32[48,128]{1,0:T(8,128)S(1)} %get-tuple-element.25), channel_id=1, source_target_pairs={{1,2},{2,1},{3,4},{4,3},{5,6},{6,5},{7,8},{8,7},{9,10},{10,9},{11,... | collective-permute-start | bytes 73736 | tf_op jit(solution)/shard_map/ppermute | solution.py:668
  19.8 3.4 %collective-permute-start.1 = (f32[48,128]{1,0:T(8,128)S(1)}, f32[48,128]{1,0:T(8,128)S(1)}, u32[]{:S(2)}, u32[]{:S(2)}) collective-permute-start(f32[48,128]{1,0:T(8,128)S(1)} %get-tuple-element.26), channel_id=1, source_target_pairs={{0,1},{1,0},{2,3},{3,2},{4,5},{5,4},{6,7},{7,6},{8,9},{9,8},{10,11... | collective-permute-start | bytes 73736 | tf_op jit(solution)/shard_map/ppermute | solution.py:669
  23.3 12.4 %collective-permute-start.2 = (f32[192,128]{1,0:T(8,128)S(1)}, f32[192,128]{1,0:T(8,128)S(1)}, u32[]{:S(2)}, u32[]{:S(2)}) collective-permute-start(f32[192,128]{1,0:T(8,128)S(1)} %get-tuple-element.27), channel_id=1, source_target_pairs={{0,32},{32,0},{64,96},{96,64},{128,160},{160,128},{192,224},{224,1... | collective-permute-start | bytes 294920 | tf_op jit(solution)/shard_map/ppermute | solution.py:678
  26.7 12.5 %collective-permute-start.3 = (f32[192,128]{1,0:T(8,128)S(1)}, f32[192,128]{1,0:T(8,128)S(1)}, u32[]{:S(2)}, u32[]{:S(2)}) collective-permute-start(f32[192,128]{1,0:T(8,128)S(1)} %get-tuple-element.28), channel_id=1, source_target_pairs={{32,64},{64,32},{96,128},{128,96},{160,192},{192,160},{224,256},{2... | collective-permute-start | bytes 294920 | tf_op jit(solution)/shard_map/ppermute | solution.py:677
  42.0 31.2 %all-to-all-start = ((f32[32,24,128]{2,1,0:T(8,128)}), f32[32,24,128]{2,1,0:T(8,128)S(1)}, u32[]{:S(2)}, u32[]{:S(2)}) async-start(f32[32,24,128]{2,1,0:T(8,128)} %bitcast.1), calls=%async_computation | async-start | bytes 786432 | tf_op jit(solution)/shard_map/all_to_all | solution.py:726

commit v6 on v5

--- a/solution.py
+++ b/solution.py
@@ -192,14 +192,14 @@
     close_ref[...] = jnp.where(even, to_right, to_left)
 
 
-def arrange_kernel(values_ref, low_ref, high_ref, place_ref):
+def arrange_kernel(values_ref, low_ref, high_ref, hits_ref):
     index = values_ref[TILE:, 0:ELEMS_DEV].astype(jnp.int32)
     local = index >= 0
     place = chain_length(local[0:1], index[0:1], 4)
     row = chain_length(local[2:3], index[2:3], 2)
     target = over_points(row * 16.0 + place + 2.0) * 16 + lane_iota((1, POINTS_DEV)) % 16
-    place_ref[...] = jnp.broadcast_to(target, (8, POINTS_DEV))
     hits = (row_iota((1024, POINTS_DEV)) == target).astype(F32).astype(BF16)
+    hits_ref[...] = hits
     parts = dot_last(jnp.concatenate(three_parts(values_ref[0:TILE, :]), axis=0), hits)
     ordered = parts[0:TILE] + parts[TILE : 2 * TILE] + parts[2 * TILE :]
     for r in range(4):
@@ -596,13 +596,15 @@
     send_ref[...] = sent[:, :LANES] + sent[:, LANES:]
 
 
-def restore_kernel(whole_ref, place_ref, updated_ref):
-    first, second, third = three_parts(whole_ref[...])
-    hits = (row_iota((1024, POINTS_DEV)) == place_ref[0:1, :]).astype(F32).astype(BF16)
-    updated_ref[...] = dot(first, hits) + dot(second, hits) + dot(third, hits)
-
-
-def receive_kernel(received_ref, physics_ref):
+def receive_kernel(
+    received_ref, whole_ref, hits_ref, updated_ref, physics_ref, updated, pieces, sems
+):
+    whole = whole_ref[...]
+    upper = whole.astype(BF16).astype(F32)
+    restored = dot(jnp.concatenate([upper, whole - upper], axis=0).astype(BF16), hits_ref[...])
+    updated[...] = restored[:STATE] + restored[STATE:]
+    copies = [pltpu.make_async_copy(updated, updated_ref, sems.at[3])]
+    copies[0].start()
     turned_over = received_ref[...].T
     upper, lower = halves(turned_over)
     places = slice(3 * STATE, 3 * STATE + 3)
@@ -615,11 +617,20 @@
         rows = dot_last(both, hits.astype(F32).astype(BF16))
         rows = rows[:LANES] + rows[LANES:]
         own = rows[places, :] == (lane_iota((3, count)) + (start + 1)).astype(F32)
-        physics_ref[:, start : start + count] = jnp.where(
+        piece = start // count
+        pieces[piece] = jnp.where(
             own[0:1],
             rows[:STATE],
             jnp.where(own[1:2], rows[STATE : 2 * STATE], rows[2 * STATE : 3 * STATE]),
         )
+        copies.append(
+            pltpu.make_async_copy(
+                pieces.at[piece], physics_ref.at[:, pl.ds(start, count)], sems.at[piece]
+            )
+        )
+        copies[-1].start()
+    for copy in copies:
+        copy.wait()
 
 
 def call(kernel, shapes, scratch=(), flops=0, moved=0, vmem=VMEM_LIMIT, **specs):
@@ -667,9 +678,9 @@
     cols, rows = lax.axis_size("col"), lax.axis_size("curve")
     from_far = lax.ppermute(far, "col", swaps(cols, 1) + [(cols - 1, 0), (0, cols - 1)])
     from_close = lax.ppermute(close, "col", swaps(cols, 0))
-    low, high, place = call(
+    low, high, hits = call(
         arrange_kernel,
-        [half, half, ((8, POINTS_DEV), jnp.int32)],
+        [half, half, pltpu.VMEM((1024, POINTS_DEV), BF16)],
         flops=400_000_000,
         moved=1_000_000,
     )(values)
@@ -724,10 +735,17 @@
         middle_inverse,
     )
     received = lax.all_to_all(sent, "col", split_axis=0, concat_axis=0, tiled=True)
-    (updated,) = call(
-        restore_kernel, [((STATE, POINTS_DEV), F32)], flops=400_000_000, moved=1_000_000
-    )(whole, place)
-    (physics,) = call(receive_kernel, [((STATE, POINTS_DEV), F32)])(received)
+    updated, physics = call(
+        receive_kernel,
+        [((STATE, POINTS_DEV), F32)] * 2,
+        scratch=[
+            pltpu.VMEM((STATE, POINTS_DEV), F32),
+            pltpu.VMEM((3, STATE, 2 * LANES), F32),
+            pltpu.SemaphoreType.DMA((4,)),
+        ],
+        in_specs=[pl.BlockSpec(memory_space=pltpu.VMEM)] * 3,
+        out_specs=[anywhere] * 2,
+    )(received, whole, hits)
     shape = evolving_state_array.shape
     return updated.reshape(shape), physics.reshape(shape)
 

time: 75.4 us -> 74.4 us (0.987)
  blocking collectives: 0 us -> 30.7 us
  waiting for transfers between devices: 21.4 us -> 3.47 us
  starting transfers between devices: 41.5 us -> 29.9 us
  Pallas kernels: 11.4 us -> 9.34 us
    all_to_all x0 -> x1, blocking collectives: none -> 30.7 us  [body(): lax.all_to_all(sent, 'col', split_axis=0, concat_axis=0, tiled=True)]
    all_to_all x1 -> x0, waiting for transfers between devices: 17.9 us -> none  [body(): lax.all_to_all(sent, 'col', split_axis=0, concat_axis=0, tiled=True)]
    all_to_all x1 -> x0, starting transfers between devices: 11.6 us -> none  [body(): lax.all_to_all(sent, 'col', split_axis=0, concat_axis=0, tiled=True)]
    pallas_call x3 -> x2, Pallas kernels: 4.84 us -> 3.57 us  [the longest x1 1.84 us: body(): call(receive_kernel, [((STATE, POINTS_DEV), F32)] * 2, scratch=[pltpu.VME...]
  transfers between devices with their start and end apart: 5 -> 4, of which waited for: 2 -> 1; matrix products, arithmetic and copies ran while one was open for 0% -> 0% of each run, Pallas kernels for 7% -> 5%
where the time goes in v6:
time: 74.4 us; the launch traced here: 74.1 us
  blocking collectives  30.7 us (41%)
  starting transfers between devices  29.9 us (40%)
  Pallas kernels  9.34 us (13%)
  waiting for transfers between devices  3.47 us (5%)
    all_to_all x1, blocking collectives, body(): lax.all_to_all(sent, 'col', split_axis=0, concat_axis=0, tiled=True)  30.7 us
    ppermute x1, starting transfers between devices, body(): lax.ppermute(far, 'col', swaps(cols, 1) + [(cols - 1, 0), (0, cols - 1)])  17.6 us
    ppermute x1, starting transfers between devices, body(): second_far = lax.ppermute(second, 'curve', swaps(rows, 1))  6.97 us
    ppermute x1, waiting for transfers between devices, body(): second_far = lax.ppermute(second, 'curve', swaps(rows, 1))  3.46 us
    ppermute x1, starting transfers between devices, body(): first_far = lax.ppermute(first, 'curve', swaps(rows, 0))  3.38 us
    pallas_call x1, Pallas kernels, body(): call(section_kernel, [((STATE, 1024), F32), ((POINTS_DEV, LANES), F32)],...  2.08 us
    pallas_call x1, Pallas kernels, body(): call(inner_kernel, [((8, 1024), F32), ((4 * 56, 2 * LANES), F32), ((4 * 3...  2.05 us
    ppermute x1, starting transfers between devices, body(): from_close = lax.ppermute(close, 'col', swaps(cols, 0))  1.92 us
  transfers between devices with their start and end apart: 4, of which 1 were waited for; matrix products, arithmetic and copies ran while one was open for 0% of the time, Pallas kernels for 5%

profile of v6, /device:TPU:6, one launch (start us, length us, event | category | flops | bytes accessed | tf_op | source)
XLA Modules:
  0.0 74.1 jit_solution(12533316998033038672)
XLA Ops:
  0.6 1.5 %shard_map.86 = (f32[48,128]{1,0:T(8,128)S(1)}, f32[48,128]{1,0:T(8,128)S(1)}, f32[56,768]{1,0:T(8,128)S(1)}) custom-call(f32[5,8,768]{2,1,0:T(8,128)} %state_ref.1, f32[768]{0:T(1024)} %jacobian_ref.1, f32[768]{0:T(1024)} %coriolis_ref.1, f32[4,768]{1,0:T(4,128)} %metric_ref.1, s32[8,48]{1,0:T(8,128)} %near_ref.1, s32[768]{0:T(1024)} %slot_ref.1), custom_call_target="tpu_custom_call" | custom-call | tf_op jit(solution)/shard_map/pallas_call | solution.py:663
  2.2 0.0 copy-start
  2.2 17.6 %collective-permute-start = (f32[48,128]{1,0:T(8,128)S(1)}, f32[48,128]{1,0:T(8,128)S(1)}, u32[]{:S(2)}, u32[]{:S(2)}) collective-permute-start(f32[48,128]{1,0:T(8,128)S(1)} %get-tuple-element.27), channel_id=1, source_target_pairs={{1,2},{2,1},{3,4},{4,3},{5,6},{6,5},{7,8},{8,7},{9,10},{10,9},{11,... | collective-permute-start | bytes 73736 | tf_op jit(solution)/shard_map/ppermute | solution.py:679
  19.8 1.9 %collective-permute-start.1 = (f32[48,128]{1,0:T(8,128)S(1)}, f32[48,128]{1,0:T(8,128)S(1)}, u32[]{:S(2)}, u32[]{:S(2)}) collective-permute-start(f32[48,128]{1,0:T(8,128)S(1)} %get-tuple-element.28), channel_id=1, source_target_pairs={{0,1},{1,0},{2,3},{3,2},{4,5},{5,4},{6,7},{7,6},{8,9},{9,8},{10,11... | collective-permute-start | bytes 73736 | tf_op jit(solution)/shard_map/ppermute | solution.py:680
  21.7 1.7 %shard_map.87 = (f32[192,128]{1,0:T(8,128)S(1)}, f32[192,128]{1,0:T(8,128)S(1)}, bf16[1024,768]{1,0:T(8,128)(2,1)S(1)}) custom-call(f32[56,768]{1,0:T(8,128)S(1)} %get-tuple-element.24.values_ref), custom_call_target="tpu_custom_call" | custom-call | flops 400000000 | bytes 1000000 | tf_op jit(solution)/shard_map/pallas_call | solution.py:681
  23.5 0.0 collective-permute-done.from_far
  23.5 0.0 collective-permute-done.1.from_close
  23.5 0.1 shard_map.88
  23.6 3.4 %collective-permute-start.2 = (f32[192,128]{1,0:T(8,128)S(1)}, f32[192,128]{1,0:T(8,128)S(1)}, u32[]{:S(2)}, u32[]{:S(2)}) collective-permute-start(f32[192,128]{1,0:T(8,128)S(1)} %get-tuple-element.29), channel_id=1, source_target_pairs={{0,32},{32,0},{64,96},{96,64},{128,160},{160,128},{192,224},{224,1... | collective-permute-start | bytes 294920 | tf_op jit(solution)/shard_map/ppermute | solution.py:689
  27.0 7.0 %collective-permute-start.3 = (f32[192,128]{1,0:T(8,128)S(1)}, f32[192,128]{1,0:T(8,128)S(1)}, u32[]{:S(2)}, u32[]{:S(2)}) collective-permute-start(f32[192,128]{1,0:T(8,128)S(1)} %get-tuple-element.30), channel_id=1, source_target_pairs={{32,64},{64,32},{96,128},{128,96},{160,192},{192,160},{224,256},{2... | collective-permute-start | bytes 294920 | tf_op jit(solution)/shard_map/ppermute | solution.py:688
  34.0 0.0 copy-done
  34.0 2.0 %shard_map.89 = (f32[8,1024]{1,0:T(8,128)S(1)}, f32[224,256]{1,0:T(8,128)S(1)}, f32[128,256]{1,0:T(8,128)S(1)}, f32[192,128]{1,0:T(8,128)S(1)}, bf16[768,1024]{1...) custom-call(f32[192,128]{1,0:T(8,128)S(1)} %get-tuple-element.31.low_ref, ...), custom_call_target="tpu_custom_call" | custom-call | flops 400000000 | bytes 1000000 | tf_op jit(solution)/shard_map/pallas_call | solution.py:699
  36.0 0.0 collective-permute-done.2.first_far_ref
  36.0 3.5 %collective-permute-done.3.second_far_ref = f32[192,128]{1,0:T(8,128)S(1)} collective-permute-done((f32[192,128]{1,0:T(8,128)S(1)}, f32[192,128]{1,0:T(8,128)S(1)}, u32[]{:S(2)}, u32[]{:S(2)}) %collective-permute-start.3) | collective-permute-done | bytes 98336 | tf_op jit(solution)/shard_map/ppermute | solution.py:688
  39.5 2.1 %shard_map.90 = (f32[40,1024]{1,0:T(8,128)S(1)}, f32[768,128]{1,0:T(8,128)S(1)}) custom-call(f32[192,128]{1,0:T(8,128)S(1)} %collective-permute-done.2.first_far_ref, f32[192,128]{1,0:T(8,128)S(1)} %collective-permute-done.3.second_far_ref, f32[192,128]{1,0:T(8,128)S(1)} %get-tuple-element.31.low_ref, f32[192,128]{1,0:T(8,128)S(1)} %get-tuple-element.32.high_ref, ...), custom_call_target="tpu_custom_call" | custom-call | tf_op jit(solution)/shard_map/pallas_call | solution.py:716
  41.6 30.7 %all_to_all.11 = f32[32,24,128]{2,1,0:T(8,128)S(1)} all-to-all(f32[32,24,128]{2,1,0:T(8,128)S(1)} %bitcast.5), channel_id=1, replica_groups=mesh['curve'=24,'col'=32] {'col'}, dimensions={0} | all-to-all | bytes 786432 | tf_op jit(solution)/shard_map/all_to_all | solution.py:737
  72.3 1.8 %shard_map.91 = (f32[40,768]{1,0:T(8,128)}, f32[40,768]{1,0:T(8,128)}) custom-call(f32[768,128]{1,0:T(8,128)S(1)} %bitcast.4, f32[40,1024]{1,0:T(8,128)S(1)} %get-tuple-element.42.whole_ref, bf16[1024,768]{1,0:T(8,128)(2,1)S(1)} %get-tuple-element.43.hits_ref), custom_call_target="tpu_custom_call" | custom-call | tf_op jit(solution)/shard_map/pallas_call | solution.py:738
Async XLA Ops:
  2.2 31.8 %copy-start = (bf16[1664,256]{1,0:T(8,128)(2,1)S(1)}, bf16[1664,256]{1,0:T(8,128)(2,1)}, u32[]{:S(2)}) copy-start(bf16[1664,256]{1,0:T(8,128)(2,1)} %constant.2.clone.matrices) | copy-start | bytes 2555908
  2.2 21.3 %collective-permute-start = (f32[48,128]{1,0:T(8,128)S(1)}, f32[48,128]{1,0:T(8,128)S(1)}, u32[]{:S(2)}, u32[]{:S(2)}) collective-permute-start(f32[48,128]{1,0:T(8,128)S(1)} %get-tuple-element.27), channel_id=1, source_target_pairs={{1,2},{2,1},{3,4},{4,3},{5,6},{6,5},{7,8},{8,7},{9,10},{10,9},{11,... | collective-permute-start | bytes 73736 | tf_op jit(solution)/shard_map/ppermute | solution.py:679
  19.8 3.7 %collective-permute-start.1 = (f32[48,128]{1,0:T(8,128)S(1)}, f32[48,128]{1,0:T(8,128)S(1)}, u32[]{:S(2)}, u32[]{:S(2)}) collective-permute-start(f32[48,128]{1,0:T(8,128)S(1)} %get-tuple-element.28), channel_id=1, source_target_pairs={{0,1},{1,0},{2,3},{3,2},{4,5},{5,4},{6,7},{7,6},{8,9},{9,8},{10,11... | collective-permute-start | bytes 73736 | tf_op jit(solution)/shard_map/ppermute | solution.py:680
  23.6 12.4 %collective-permute-start.2 = (f32[192,128]{1,0:T(8,128)S(1)}, f32[192,128]{1,0:T(8,128)S(1)}, u32[]{:S(2)}, u32[]{:S(2)}) collective-permute-start(f32[192,128]{1,0:T(8,128)S(1)} %get-tuple-element.29), channel_id=1, source_target_pairs={{0,32},{32,0},{64,96},{96,64},{128,160},{160,128},{192,224},{224,1... | collective-permute-start | bytes 294920 | tf_op jit(solution)/shard_map/ppermute | solution.py:689
  27.0 12.5 %collective-permute-start.3 = (f32[192,128]{1,0:T(8,128)S(1)}, f32[192,128]{1,0:T(8,128)S(1)}, u32[]{:S(2)}, u32[]{:S(2)}) collective-permute-start(f32[192,128]{1,0:T(8,128)S(1)} %get-tuple-element.30), channel_id=1, source_target_pairs={{32,64},{64,32},{96,128},{128,96},{160,192},{192,160},{224,256},{2... | collective-permute-start | bytes 294920 | tf_op jit(solution)/shard_map/ppermute | solution.py:688

commit v7 on v6

--- a/solution.py
+++ b/solution.py
@@ -157,7 +157,8 @@
         copy.start()
     copies[0].wait()
     index, local = local_lists(near[...])
-    row = chain_length(local[2:3], index[2:3], 2)
+    lower = wide(local[2:3])
+    row = lower + dot(lower.astype(BF16), one_step(local[2:3], index[2:3])) + wide(~local[3:4])
     sides = []
     for side in range(2):
         here, there = local[side : side + 1], index[side : side + 1]
@@ -184,8 +185,8 @@
     )
     values_ref[0:TILE, :] = values
     values_ref[TILE:, 0:ELEMS_DEV] = jnp.where(local, index, -1).astype(F32)
-    parts = dot_last(jnp.concatenate(three_parts(values), axis=0), hits)
-    strips = parts[0:TILE] + parts[TILE : 2 * TILE] + parts[2 * TILE :]
+    parts = dot_last(jnp.concatenate(halves(values), axis=0), hits)
+    strips = parts[:TILE] + parts[TILE:]
     even = lax.rem(lax.axis_index("col"), 2) == 0
     to_left, to_right = strips[:, :LANES], strips[:, LANES:]
     far_ref[...] = jnp.where(even, to_left, to_right)
@@ -609,12 +610,13 @@
     upper, lower = halves(turned_over)
     places = slice(3 * STATE, 3 * STATE + 3)
     slot = turned_over[places, :].astype(jnp.int32) - 1
+    slots = [slot[k : k + 1].astype(jnp.int16) for k in range(3)]
     both = jnp.concatenate([upper, lower], axis=0)
     count = 2 * LANES
     for start in range(0, POINTS_DEV, count):
-        row = row_iota((count, POINTS_DEV)) + start
-        hits = (row == slot[0:1]) | (row == slot[1:2]) | (row == slot[2:3])
-        rows = dot_last(both, hits.astype(F32).astype(BF16))
+        row = (row_iota((count, POINTS_DEV)) + start).astype(jnp.int16)
+        hits = (row == slots[0]) | (row == slots[1]) | (row == slots[2])
+        rows = dot_last(both, jnp.where(hits, jnp.bfloat16(1), jnp.bfloat16(0)))
         rows = rows[:LANES] + rows[LANES:]
         own = rows[places, :] == (lane_iota((3, count)) + (start + 1)).astype(F32)
         piece = start // count

time: 74.4 us -> 73.8 us (level)
  no operation moved by 1% of the time
where the time goes in v7:
time: 73.8 us; the launch traced here: 73.5 us
  blocking collectives  30.6 us (41%)
  starting transfers between devices  29.9 us (41%)
  Pallas kernels  8.76 us (12%)
  waiting for transfers between devices  3.47 us (5%)
  between operations  0.74 us (1%)
    all_to_all x1, blocking collectives, body(): lax.all_to_all(sent, 'col', split_axis=0, concat_axis=0, tiled=True)  30.6 us
    ppermute x1, starting transfers between devices, body(): lax.ppermute(far, 'col', swaps(cols, 1) + [(cols - 1, 0), (0, cols - 1)])  17.6 us
    ppermute x1, starting transfers between devices, body(): second_far = lax.ppermute(second, 'curve', swaps(rows, 1))  6.97 us
    ppermute x1, waiting for transfers between devices, body(): second_far = lax.ppermute(second, 'curve', swaps(rows, 1))  3.46 us
    ppermute x1, starting transfers between devices, body(): first_far = lax.ppermute(first, 'curve', swaps(rows, 0))  3.38 us
    pallas_call x1, Pallas kernels, body(): call(section_kernel, [((STATE, 1024), F32), ((POINTS_DEV, LANES), F32)],...  2.07 us
    pallas_call x1, Pallas kernels, body(): call(inner_kernel, [((8, 1024), F32), ((4 * 56, 2 * LANES), F32), ((4 * 3...  2.05 us
    ppermute x1, starting transfers between devices, body(): from_close = lax.ppermute(close, 'col', swaps(cols, 0))  1.92 us
  transfers between devices with their start and end apart: 4, of which 1 were waited for; matrix products, arithmetic and copies ran while one was open for 0% of the time, Pallas kernels for 5%

profile of v7, /device:TPU:6, one launch (start us, length us, event | category | flops | bytes accessed | tf_op | source)
XLA Modules:
  0.0 73.5 jit_solution(13092364995005122884)
XLA Ops:
  0.6 1.4 %shard_map.86 = (f32[48,128]{1,0:T(8,128)S(1)}, f32[48,128]{1,0:T(8,128)S(1)}, f32[56,768]{1,0:T(8,128)S(1)}) custom-call(f32[5,8,768]{2,1,0:T(8,128)} %state_ref.1, f32[768]{0:T(1024)} %jacobian_ref.1, f32[768]{0:T(1024)} %coriolis_ref.1, f32[4,768]{1,0:T(4,128)} %metric_ref.1, s32[8,48]{1,0:T(8,128)} %near_ref.1, s32[768]{0:T(1024)} %slot_ref.1), custom_call_target="tpu_custom_call" | custom-call | tf_op jit(solution)/shard_map/pallas_call | solution.py:665
  2.0 0.0 copy-start
  2.0 17.6 %collective-permute-start = (f32[48,128]{1,0:T(8,128)S(1)}, f32[48,128]{1,0:T(8,128)S(1)}, u32[]{:S(2)}, u32[]{:S(2)}) collective-permute-start(f32[48,128]{1,0:T(8,128)S(1)} %get-tuple-element.27), channel_id=1, source_target_pairs={{1,2},{2,1},{3,4},{4,3},{5,6},{6,5},{7,8},{8,7},{9,10},{10,9},{11,... | collective-permute-start | bytes 73736 | tf_op jit(solution)/shard_map/ppermute | solution.py:681
  19.7 1.9 %collective-permute-start.1 = (f32[48,128]{1,0:T(8,128)S(1)}, f32[48,128]{1,0:T(8,128)S(1)}, u32[]{:S(2)}, u32[]{:S(2)}) collective-permute-start(f32[48,128]{1,0:T(8,128)S(1)} %get-tuple-element.28), channel_id=1, source_target_pairs={{0,1},{1,0},{2,3},{3,2},{4,5},{5,4},{6,7},{7,6},{8,9},{9,8},{10,11... | collective-permute-start | bytes 73736 | tf_op jit(solution)/shard_map/ppermute | solution.py:682
  21.6 1.7 %shard_map.87 = (f32[192,128]{1,0:T(8,128)S(1)}, f32[192,128]{1,0:T(8,128)S(1)}, bf16[1024,768]{1,0:T(8,128)(2,1)S(1)}) custom-call(f32[56,768]{1,0:T(8,128)S(1)} %get-tuple-element.24.values_ref), custom_call_target="tpu_custom_call" | custom-call | flops 400000000 | bytes 1000000 | tf_op jit(solution)/shard_map/pallas_call | solution.py:683
  23.3 0.0 collective-permute-done.from_far
  23.3 0.0 collective-permute-done.1.from_close
  23.3 0.1 shard_map.88
  23.5 3.4 %collective-permute-start.2 = (f32[192,128]{1,0:T(8,128)S(1)}, f32[192,128]{1,0:T(8,128)S(1)}, u32[]{:S(2)}, u32[]{:S(2)}) collective-permute-start(f32[192,128]{1,0:T(8,128)S(1)} %get-tuple-element.29), channel_id=1, source_target_pairs={{0,32},{32,0},{64,96},{96,64},{128,160},{160,128},{192,224},{224,1... | collective-permute-start | bytes 294920 | tf_op jit(solution)/shard_map/ppermute | solution.py:691
  26.9 7.0 %collective-permute-start.3 = (f32[192,128]{1,0:T(8,128)S(1)}, f32[192,128]{1,0:T(8,128)S(1)}, u32[]{:S(2)}, u32[]{:S(2)}) collective-permute-start(f32[192,128]{1,0:T(8,128)S(1)} %get-tuple-element.30), channel_id=1, source_target_pairs={{32,64},{64,32},{96,128},{128,96},{160,192},{192,160},{224,256},{2... | collective-permute-start | bytes 294920 | tf_op jit(solution)/shard_map/ppermute | solution.py:690
  33.8 0.0 copy-done
  33.8 2.1 %shard_map.89 = (f32[8,1024]{1,0:T(8,128)S(1)}, f32[224,256]{1,0:T(8,128)S(1)}, f32[128,256]{1,0:T(8,128)S(1)}, f32[192,128]{1,0:T(8,128)S(1)}, bf16[768,1024]{1...) custom-call(f32[192,128]{1,0:T(8,128)S(1)} %get-tuple-element.31.low_ref, ...), custom_call_target="tpu_custom_call" | custom-call | flops 400000000 | bytes 1000000 | tf_op jit(solution)/shard_map/pallas_call | solution.py:701
  35.9 0.0 collective-permute-done.2.first_far_ref
  35.9 3.5 %collective-permute-done.3.second_far_ref = f32[192,128]{1,0:T(8,128)S(1)} collective-permute-done((f32[192,128]{1,0:T(8,128)S(1)}, f32[192,128]{1,0:T(8,128)S(1)}, u32[]{:S(2)}, u32[]{:S(2)}) %collective-permute-start.3) | collective-permute-done | bytes 98336 | tf_op jit(solution)/shard_map/ppermute | solution.py:690
  39.4 2.1 %shard_map.90 = (f32[40,1024]{1,0:T(8,128)S(1)}, f32[768,128]{1,0:T(8,128)S(1)}) custom-call(f32[192,128]{1,0:T(8,128)S(1)} %collective-permute-done.2.first_far_ref, f32[192,128]{1,0:T(8,128)S(1)} %collective-permute-done.3.second_far_ref, f32[192,128]{1,0:T(8,128)S(1)} %get-tuple-element.31.low_ref, f32[192,128]{1,0:T(8,128)S(1)} %get-tuple-element.32.high_ref, ...), custom_call_target="tpu_custom_call" | custom-call | tf_op jit(solution)/shard_map/pallas_call | solution.py:718
  41.5 30.6 %all_to_all.11 = f32[32,24,128]{2,1,0:T(8,128)S(1)} all-to-all(f32[32,24,128]{2,1,0:T(8,128)S(1)} %bitcast.5), channel_id=1, replica_groups=mesh['curve'=24,'col'=32] {'col'}, dimensions={0} | all-to-all | bytes 786432 | tf_op jit(solution)/shard_map/all_to_all | solution.py:739
  72.1 1.4 %shard_map.91 = (f32[40,768]{1,0:T(8,128)}, f32[40,768]{1,0:T(8,128)}) custom-call(f32[768,128]{1,0:T(8,128)S(1)} %bitcast.4, f32[40,1024]{1,0:T(8,128)S(1)} %get-tuple-element.42.whole_ref, bf16[1024,768]{1,0:T(8,128)(2,1)S(1)} %get-tuple-element.43.hits_ref), custom_call_target="tpu_custom_call" | custom-call | tf_op jit(solution)/shard_map/pallas_call | solution.py:740
Async XLA Ops:
  2.0 31.8 %copy-start = (bf16[1664,256]{1,0:T(8,128)(2,1)S(1)}, bf16[1664,256]{1,0:T(8,128)(2,1)}, u32[]{:S(2)}) copy-start(bf16[1664,256]{1,0:T(8,128)(2,1)} %constant.2.clone.matrices) | copy-start | bytes 2555908
  2.0 21.3 %collective-permute-start = (f32[48,128]{1,0:T(8,128)S(1)}, f32[48,128]{1,0:T(8,128)S(1)}, u32[]{:S(2)}, u32[]{:S(2)}) collective-permute-start(f32[48,128]{1,0:T(8,128)S(1)} %get-tuple-element.27), channel_id=1, source_target_pairs={{1,2},{2,1},{3,4},{4,3},{5,6},{6,5},{7,8},{8,7},{9,10},{10,9},{11,... | collective-permute-start | bytes 73736 | tf_op jit(solution)/shard_map/ppermute | solution.py:681
  19.7 3.7 %collective-permute-start.1 = (f32[48,128]{1,0:T(8,128)S(1)}, f32[48,128]{1,0:T(8,128)S(1)}, u32[]{:S(2)}, u32[]{:S(2)}) collective-permute-start(f32[48,128]{1,0:T(8,128)S(1)} %get-tuple-element.28), channel_id=1, source_target_pairs={{0,1},{1,0},{2,3},{3,2},{4,5},{5,4},{6,7},{7,6},{8,9},{9,8},{10,11... | collective-permute-start | bytes 73736 | tf_op jit(solution)/shard_map/ppermute | solution.py:682
  23.5 12.4 %collective-permute-start.2 = (f32[192,128]{1,0:T(8,128)S(1)}, f32[192,128]{1,0:T(8,128)S(1)}, u32[]{:S(2)}, u32[]{:S(2)}) collective-permute-start(f32[192,128]{1,0:T(8,128)S(1)} %get-tuple-element.29), channel_id=1, source_target_pairs={{0,32},{32,0},{64,96},{96,64},{128,160},{160,128},{192,224},{224,1... | collective-permute-start | bytes 294920 | tf_op jit(solution)/shard_map/ppermute | solution.py:691
  26.9 12.5 %collective-permute-start.3 = (f32[192,128]{1,0:T(8,128)S(1)}, f32[192,128]{1,0:T(8,128)S(1)}, u32[]{:S(2)}, u32[]{:S(2)}) collective-permute-start(f32[192,128]{1,0:T(8,128)S(1)} %get-tuple-element.30), channel_id=1, source_target_pairs={{32,64},{64,32},{96,128},{128,96},{160,192},{192,160},{224,256},{2... | collective-permute-start | bytes 294920 | tf_op jit(solution)/shard_map/ppermute | solution.py:690

commit v8 on v7

--- a/solution.py
+++ b/solution.py
@@ -169,7 +169,8 @@
     unit = (first + second) * (2.0 * row + 1.0 + second)
     unit = unit + (last + second_last) * (2.0 * row + 9.0 + last)
     lane = (over_points(unit) - 1) * 16 + lane_iota((1, POINTS_DEV)) % 16
-    hits = (row_iota((2 * LANES, POINTS_DEV)) == lane).astype(F32).astype(BF16)
+    row16 = row_iota((2 * LANES, POINTS_DEV)).astype(jnp.int16)
+    hits = jnp.where(row16 == lane.astype(jnp.int16), jnp.bfloat16(1), jnp.bfloat16(0))
     for copy in copies[1:]:
         copy.wait()
     values = jnp.concatenate(
@@ -291,10 +292,15 @@
     )
 
 
+def both_parts(upper, lower, matrix):
+    count = upper.shape[0]
+    result = dot(jnp.concatenate([upper, lower], axis=0), matrix)
+    return result[:count] + result[count:]
+
+
 def divergence_joined(values, matrices):
     upper, lower = halves(values)
-    first = matrices[384:896, :]
-    return dot(upper, first) + dot(lower, first) + dot(upper, matrices[896:1408, :])
+    return both_parts(upper, lower, matrices[384:896, :]) + dot(upper, matrices[896:1408, :])
 
 
 def rows_joined(below, here, above, low_mask, high_mask):
@@ -387,8 +393,7 @@
         )
     spread = divergence_joined(flux[...], matrices)
     upper, lower = halves(plain[...])
-    join = matrices[1408:1664, :]
-    return spread, dot(upper, join) + dot(lower, join)
+    return spread, both_parts(upper, lower, matrices[1408:1664, :])
 
 
 def face_masks():

time: 73.8 us -> 73.7 us (level)
  no operation moved by 1% of the time
where the time goes in v8:
time: 73.7 us; the launch traced here: 73.4 us
  blocking collectives  30.6 us (42%)
  starting transfers between devices  29.9 us (41%)
  Pallas kernels  8.63 us (12%)
  waiting for transfers between devices  3.53 us (5%)
  between operations  0.74 us (1%)
    all_to_all x1, blocking collectives, body(): lax.all_to_all(sent, 'col', split_axis=0, concat_axis=0, tiled=True)  30.6 us
    ppermute x1, starting transfers between devices, body(): lax.ppermute(far, 'col', swaps(cols, 1) + [(cols - 1, 0), (0, cols - 1)])  17.6 us
    ppermute x1, starting transfers between devices, body(): second_far = lax.ppermute(second, 'curve', swaps(rows, 1))  6.97 us
    ppermute x1, waiting for transfers between devices, body(): second_far = lax.ppermute(second, 'curve', swaps(rows, 1))  3.52 us
    ppermute x1, starting transfers between devices, body(): first_far = lax.ppermute(first, 'curve', swaps(rows, 0))  3.38 us
    pallas_call x1, Pallas kernels, body(): call(section_kernel, [((STATE, 1024), F32), ((POINTS_DEV, LANES), F32)],...  2.07 us
    pallas_call x1, Pallas kernels, body(): call(inner_kernel, [((8, 1024), F32), ((4 * 56, 2 * LANES), F32), ((4 * 3...  1.98 us
    ppermute x1, starting transfers between devices, body(): from_close = lax.ppermute(close, 'col', swaps(cols, 0))  1.92 us
  transfers between devices with their start and end apart: 4, of which 1 were waited for; matrix products, arithmetic and copies ran while one was open for 0% of the time, Pallas kernels for 5%

profile of v8, /device:TPU:6, one launch (start us, length us, event | category | flops | bytes accessed | tf_op | source)
XLA Modules:
  0.0 73.4 jit_solution(6713436452199611882)
XLA Ops:
  0.6 1.3 %shard_map.86 = (f32[48,128]{1,0:T(8,128)S(1)}, f32[48,128]{1,0:T(8,128)S(1)}, f32[56,768]{1,0:T(8,128)S(1)}) custom-call(f32[5,8,768]{2,1,0:T(8,128)} %state_ref.1, f32[768]{0:T(1024)} %jacobian_ref.1, f32[768]{0:T(1024)} %coriolis_ref.1, f32[4,768]{1,0:T(4,128)} %metric_ref.1, s32[8,48]{1,0:T(8,128)} %near_ref.1, s32[768]{0:T(1024)} %slot_ref.1), custom_call_target="tpu_custom_call" | custom-call | tf_op jit(solution)/shard_map/pallas_call | solution.py:670
  2.0 0.0 copy-start
  2.0 17.6 %collective-permute-start = (f32[48,128]{1,0:T(8,128)S(1)}, f32[48,128]{1,0:T(8,128)S(1)}, u32[]{:S(2)}, u32[]{:S(2)}) collective-permute-start(f32[48,128]{1,0:T(8,128)S(1)} %get-tuple-element.27), channel_id=1, source_target_pairs={{1,2},{2,1},{3,4},{4,3},{5,6},{6,5},{7,8},{8,7},{9,10},{10,9},{11,... | collective-permute-start | bytes 73736 | tf_op jit(solution)/shard_map/ppermute | solution.py:686
  19.6 1.9 %collective-permute-start.1 = (f32[48,128]{1,0:T(8,128)S(1)}, f32[48,128]{1,0:T(8,128)S(1)}, u32[]{:S(2)}, u32[]{:S(2)}) collective-permute-start(f32[48,128]{1,0:T(8,128)S(1)} %get-tuple-element.28), channel_id=1, source_target_pairs={{0,1},{1,0},{2,3},{3,2},{4,5},{5,4},{6,7},{7,6},{8,9},{9,8},{10,11... | collective-permute-start | bytes 73736 | tf_op jit(solution)/shard_map/ppermute | solution.py:687
  21.5 1.7 %shard_map.87 = (f32[192,128]{1,0:T(8,128)S(1)}, f32[192,128]{1,0:T(8,128)S(1)}, bf16[1024,768]{1,0:T(8,128)(2,1)S(1)}) custom-call(f32[56,768]{1,0:T(8,128)S(1)} %get-tuple-element.24.values_ref), custom_call_target="tpu_custom_call" | custom-call | flops 400000000 | bytes 1000000 | tf_op jit(solution)/shard_map/pallas_call | solution.py:688
  23.3 0.0 collective-permute-done.from_far
  23.3 0.0 collective-permute-done.1.from_close
  23.3 0.1 shard_map.88
  23.4 3.4 %collective-permute-start.2 = (f32[192,128]{1,0:T(8,128)S(1)}, f32[192,128]{1,0:T(8,128)S(1)}, u32[]{:S(2)}, u32[]{:S(2)}) collective-permute-start(f32[192,128]{1,0:T(8,128)S(1)} %get-tuple-element.29), channel_id=1, source_target_pairs={{0,32},{32,0},{64,96},{96,64},{128,160},{160,128},{192,224},{224,1... | collective-permute-start | bytes 294920 | tf_op jit(solution)/shard_map/ppermute | solution.py:696
  26.8 7.0 %collective-permute-start.3 = (f32[192,128]{1,0:T(8,128)S(1)}, f32[192,128]{1,0:T(8,128)S(1)}, u32[]{:S(2)}, u32[]{:S(2)}) collective-permute-start(f32[192,128]{1,0:T(8,128)S(1)} %get-tuple-element.30), channel_id=1, source_target_pairs={{32,64},{64,32},{96,128},{128,96},{160,192},{192,160},{224,256},{2... | collective-permute-start | bytes 294920 | tf_op jit(solution)/shard_map/ppermute | solution.py:695
  33.8 0.0 copy-done
  33.8 2.0 %shard_map.89 = (f32[8,1024]{1,0:T(8,128)S(1)}, f32[224,256]{1,0:T(8,128)S(1)}, f32[128,256]{1,0:T(8,128)S(1)}, f32[192,128]{1,0:T(8,128)S(1)}, bf16[768,1024]{1...) custom-call(f32[192,128]{1,0:T(8,128)S(1)} %get-tuple-element.31.low_ref, ...), custom_call_target="tpu_custom_call" | custom-call | flops 400000000 | bytes 1000000 | tf_op jit(solution)/shard_map/pallas_call | solution.py:706
  35.8 0.0 collective-permute-done.2.first_far_ref
  35.8 3.5 %collective-permute-done.3.second_far_ref = f32[192,128]{1,0:T(8,128)S(1)} collective-permute-done((f32[192,128]{1,0:T(8,128)S(1)}, f32[192,128]{1,0:T(8,128)S(1)}, u32[]{:S(2)}, u32[]{:S(2)}) %collective-permute-start.3) | collective-permute-done | bytes 98336 | tf_op jit(solution)/shard_map/ppermute | solution.py:695
  39.3 2.1 %shard_map.90 = (f32[40,1024]{1,0:T(8,128)S(1)}, f32[768,128]{1,0:T(8,128)S(1)}) custom-call(f32[192,128]{1,0:T(8,128)S(1)} %collective-permute-done.2.first_far_ref, f32[192,128]{1,0:T(8,128)S(1)} %collective-permute-done.3.second_far_ref, f32[192,128]{1,0:T(8,128)S(1)} %get-tuple-element.31.low_ref, f32[192,128]{1,0:T(8,128)S(1)} %get-tuple-element.32.high_ref, ...), custom_call_target="tpu_custom_call" | custom-call | tf_op jit(solution)/shard_map/pallas_call | solution.py:723
  41.4 30.6 %all_to_all.11 = f32[32,24,128]{2,1,0:T(8,128)S(1)} all-to-all(f32[32,24,128]{2,1,0:T(8,128)S(1)} %bitcast.5), channel_id=1, replica_groups=mesh['curve'=24,'col'=32] {'col'}, dimensions={0} | all-to-all | bytes 786432 | tf_op jit(solution)/shard_map/all_to_all | solution.py:744
  72.0 1.4 %shard_map.91 = (f32[40,768]{1,0:T(8,128)}, f32[40,768]{1,0:T(8,128)}) custom-call(f32[768,128]{1,0:T(8,128)S(1)} %bitcast.4, f32[40,1024]{1,0:T(8,128)S(1)} %get-tuple-element.42.whole_ref, bf16[1024,768]{1,0:T(8,128)(2,1)S(1)} %get-tuple-element.43.hits_ref), custom_call_target="tpu_custom_call" | custom-call | tf_op jit(solution)/shard_map/pallas_call | solution.py:745
Async XLA Ops:
  2.0 31.8 %copy-start = (bf16[1664,256]{1,0:T(8,128)(2,1)S(1)}, bf16[1664,256]{1,0:T(8,128)(2,1)}, u32[]{:S(2)}) copy-start(bf16[1664,256]{1,0:T(8,128)(2,1)} %constant.2.clone.matrices) | copy-start | bytes 2555908
  2.0 21.3 %collective-permute-start = (f32[48,128]{1,0:T(8,128)S(1)}, f32[48,128]{1,0:T(8,128)S(1)}, u32[]{:S(2)}, u32[]{:S(2)}) collective-permute-start(f32[48,128]{1,0:T(8,128)S(1)} %get-tuple-element.27), channel_id=1, source_target_pairs={{1,2},{2,1},{3,4},{4,3},{5,6},{6,5},{7,8},{8,7},{9,10},{10,9},{11,... | collective-permute-start | bytes 73736 | tf_op jit(solution)/shard_map/ppermute | solution.py:686
  19.6 3.7 %collective-permute-start.1 = (f32[48,128]{1,0:T(8,128)S(1)}, f32[48,128]{1,0:T(8,128)S(1)}, u32[]{:S(2)}, u32[]{:S(2)}) collective-permute-start(f32[48,128]{1,0:T(8,128)S(1)} %get-tuple-element.28), channel_id=1, source_target_pairs={{0,1},{1,0},{2,3},{3,2},{4,5},{5,4},{6,7},{7,6},{8,9},{9,8},{10,11... | collective-permute-start | bytes 73736 | tf_op jit(solution)/shard_map/ppermute | solution.py:687
  23.4 12.4 %collective-permute-start.2 = (f32[192,128]{1,0:T(8,128)S(1)}, f32[192,128]{1,0:T(8,128)S(1)}, u32[]{:S(2)}, u32[]{:S(2)}) collective-permute-start(f32[192,128]{1,0:T(8,128)S(1)} %get-tuple-element.29), channel_id=1, source_target_pairs={{0,32},{32,0},{64,96},{96,64},{128,160},{160,128},{192,224},{224,1... | collective-permute-start | bytes 294920 | tf_op jit(solution)/shard_map/ppermute | solution.py:696
  26.8 12.5 %collective-permute-start.3 = (f32[192,128]{1,0:T(8,128)S(1)}, f32[192,128]{1,0:T(8,128)S(1)}, u32[]{:S(2)}, u32[]{:S(2)}) collective-permute-start(f32[192,128]{1,0:T(8,128)S(1)} %get-tuple-element.30), channel_id=1, source_target_pairs={{32,64},{64,32},{96,128},{128,96},{160,192},{192,160},{224,256},{2... | collective-permute-start | bytes 294920 | tf_op jit(solution)/shard_map/ppermute | solution.py:695

commit v9 on v8

--- a/solution.py
+++ b/solution.py
@@ -200,10 +200,11 @@
     place = chain_length(local[0:1], index[0:1], 4)
     row = chain_length(local[2:3], index[2:3], 2)
     target = over_points(row * 16.0 + place + 2.0) * 16 + lane_iota((1, POINTS_DEV)) % 16
-    hits = (row_iota((1024, POINTS_DEV)) == target).astype(F32).astype(BF16)
+    row16 = row_iota((1024, POINTS_DEV)).astype(jnp.int16)
+    hits = jnp.where(row16 == target.astype(jnp.int16), jnp.bfloat16(1), jnp.bfloat16(0))
     hits_ref[...] = hits
-    parts = dot_last(jnp.concatenate(three_parts(values_ref[0:TILE, :]), axis=0), hits)
-    ordered = parts[0:TILE] + parts[TILE : 2 * TILE] + parts[2 * TILE :]
+    parts = dot_last(jnp.concatenate(halves(values_ref[0:TILE, :]), axis=0), hits)
+    ordered = parts[:TILE] + parts[TILE:]
     for r in range(4):
         for g in range(2):
             block = ordered[:, (2 * r + g) * LANES : (2 * r + g + 1) * LANES]

time: 73.7 us -> 73.7 us (level)
  no operation moved by 1% of the time
where the time goes in v9:
time: 73.7 us; the launch traced here: 73.4 us
  blocking collectives  31 us (42%)
  starting transfers between devices  29.9 us (41%)
  Pallas kernels  8.28 us (11%)
  waiting for transfers between devices  3.54 us (5%)
  between operations  0.74 us (1%)
    all_to_all x1, blocking collectives, body(): lax.all_to_all(sent, 'col', split_axis=0, concat_axis=0, tiled=True)  31 us
    ppermute x1, starting transfers between devices, body(): lax.ppermute(far, 'col', swaps(cols, 1) + [(cols - 1, 0), (0, cols - 1)])  17.6 us
    ppermute x1, starting transfers between devices, body(): second_far = lax.ppermute(second, 'curve', swaps(rows, 1))  6.97 us
    ppermute x1, waiting for transfers between devices, body(): second_far = lax.ppermute(second, 'curve', swaps(rows, 1))  3.53 us
    ppermute x1, starting transfers between devices, body(): first_far = lax.ppermute(first, 'curve', swaps(rows, 0))  3.38 us
    pallas_call x1, Pallas kernels, body(): call(section_kernel, [((STATE, 1024), F32), ((POINTS_DEV, LANES), F32)],...  2.07 us
    pallas_call x1, Pallas kernels, body(): call(inner_kernel, [((8, 1024), F32), ((4 * 56, 2 * LANES), F32), ((4 * 3...  1.98 us
    ppermute x1, starting transfers between devices, body(): from_close = lax.ppermute(close, 'col', swaps(cols, 0))  1.92 us
  transfers between devices with their start and end apart: 4, of which 1 were waited for; matrix products, arithmetic and copies ran while one was open for 0% of the time, Pallas kernels for 5%

profile of v9, /device:TPU:6, one launch (start us, length us, event | category | flops | bytes accessed | tf_op | source)
XLA Modules:
  0.0 73.4 jit_solution(11058050981332113731)
XLA Ops:
  0.6 1.3 %shard_map.86 = (f32[48,128]{1,0:T(8,128)S(1)}, f32[48,128]{1,0:T(8,128)S(1)}, f32[56,768]{1,0:T(8,128)S(1)}) custom-call(f32[5,8,768]{2,1,0:T(8,128)} %state_ref.1, f32[768]{0:T(1024)} %jacobian_ref.1, f32[768]{0:T(1024)} %coriolis_ref.1, f32[4,768]{1,0:T(4,128)} %metric_ref.1, s32[8,48]{1,0:T(8,128)} %near_ref.1, s32[768]{0:T(1024)} %slot_ref.1), custom_call_target="tpu_custom_call" | custom-call | tf_op jit(solution)/shard_map/pallas_call | solution.py:671
  2.0 0.0 copy-start
  2.0 17.6 %collective-permute-start = (f32[48,128]{1,0:T(8,128)S(1)}, f32[48,128]{1,0:T(8,128)S(1)}, u32[]{:S(2)}, u32[]{:S(2)}) collective-permute-start(f32[48,128]{1,0:T(8,128)S(1)} %get-tuple-element.27), channel_id=1, source_target_pairs={{1,2},{2,1},{3,4},{4,3},{5,6},{6,5},{7,8},{8,7},{9,10},{10,9},{11,... | collective-permute-start | bytes 73736 | tf_op jit(solution)/shard_map/ppermute | solution.py:687
  19.6 1.9 %collective-permute-start.1 = (f32[48,128]{1,0:T(8,128)S(1)}, f32[48,128]{1,0:T(8,128)S(1)}, u32[]{:S(2)}, u32[]{:S(2)}) collective-permute-start(f32[48,128]{1,0:T(8,128)S(1)} %get-tuple-element.28), channel_id=1, source_target_pairs={{0,1},{1,0},{2,3},{3,2},{4,5},{5,4},{6,7},{7,6},{8,9},{9,8},{10,11... | collective-permute-start | bytes 73736 | tf_op jit(solution)/shard_map/ppermute | solution.py:688
  21.5 1.4 %shard_map.87 = (f32[192,128]{1,0:T(8,128)S(1)}, f32[192,128]{1,0:T(8,128)S(1)}, bf16[1024,768]{1,0:T(8,128)(2,1)S(1)}) custom-call(f32[56,768]{1,0:T(8,128)S(1)} %get-tuple-element.24.values_ref), custom_call_target="tpu_custom_call" | custom-call | flops 400000000 | bytes 1000000 | tf_op jit(solution)/shard_map/pallas_call | solution.py:689
  22.9 0.0 collective-permute-done.from_far
  22.9 0.0 collective-permute-done.1.from_close
  22.9 0.1 shard_map.88
  23.1 3.4 %collective-permute-start.2 = (f32[192,128]{1,0:T(8,128)S(1)}, f32[192,128]{1,0:T(8,128)S(1)}, u32[]{:S(2)}, u32[]{:S(2)}) collective-permute-start(f32[192,128]{1,0:T(8,128)S(1)} %get-tuple-element.29), channel_id=1, source_target_pairs={{0,32},{32,0},{64,96},{96,64},{128,160},{160,128},{192,224},{224,1... | collective-permute-start | bytes 294920 | tf_op jit(solution)/shard_map/ppermute | solution.py:697
  26.5 7.0 %collective-permute-start.3 = (f32[192,128]{1,0:T(8,128)S(1)}, f32[192,128]{1,0:T(8,128)S(1)}, u32[]{:S(2)}, u32[]{:S(2)}) collective-permute-start(f32[192,128]{1,0:T(8,128)S(1)} %get-tuple-element.30), channel_id=1, source_target_pairs={{32,64},{64,32},{96,128},{128,96},{160,192},{192,160},{224,256},{2... | collective-permute-start | bytes 294920 | tf_op jit(solution)/shard_map/ppermute | solution.py:696
  33.4 0.0 copy-done
  33.4 2.0 %shard_map.89 = (f32[8,1024]{1,0:T(8,128)S(1)}, f32[224,256]{1,0:T(8,128)S(1)}, f32[128,256]{1,0:T(8,128)S(1)}, f32[192,128]{1,0:T(8,128)S(1)}, bf16[768,1024]{1...) custom-call(f32[192,128]{1,0:T(8,128)S(1)} %get-tuple-element.31.low_ref, ...), custom_call_target="tpu_custom_call" | custom-call | flops 400000000 | bytes 1000000 | tf_op jit(solution)/shard_map/pallas_call | solution.py:707
  35.4 0.0 collective-permute-done.2.first_far_ref
  35.4 3.5 %collective-permute-done.3.second_far_ref = f32[192,128]{1,0:T(8,128)S(1)} collective-permute-done((f32[192,128]{1,0:T(8,128)S(1)}, f32[192,128]{1,0:T(8,128)S(1)}, u32[]{:S(2)}, u32[]{:S(2)}) %collective-permute-start.3) | collective-permute-done | bytes 98336 | tf_op jit(solution)/shard_map/ppermute | solution.py:696
  39.0 2.1 %shard_map.90 = (f32[40,1024]{1,0:T(8,128)S(1)}, f32[768,128]{1,0:T(8,128)S(1)}) custom-call(f32[192,128]{1,0:T(8,128)S(1)} %collective-permute-done.2.first_far_ref, f32[192,128]{1,0:T(8,128)S(1)} %collective-permute-done.3.second_far_ref, f32[192,128]{1,0:T(8,128)S(1)} %get-tuple-element.31.low_ref, f32[192,128]{1,0:T(8,128)S(1)} %get-tuple-element.32.high_ref, ...), custom_call_target="tpu_custom_call" | custom-call | tf_op jit(solution)/shard_map/pallas_call | solution.py:724
  41.0 31.0 %all_to_all.11 = f32[32,24,128]{2,1,0:T(8,128)S(1)} all-to-all(f32[32,24,128]{2,1,0:T(8,128)S(1)} %bitcast.5), channel_id=1, replica_groups=mesh['curve'=24,'col'=32] {'col'}, dimensions={0} | all-to-all | bytes 786432 | tf_op jit(solution)/shard_map/all_to_all | solution.py:745
  72.0 1.4 %shard_map.91 = (f32[40,768]{1,0:T(8,128)}, f32[40,768]{1,0:T(8,128)}) custom-call(f32[768,128]{1,0:T(8,128)S(1)} %bitcast.4, f32[40,1024]{1,0:T(8,128)S(1)} %get-tuple-element.42.whole_ref, bf16[1024,768]{1,0:T(8,128)(2,1)S(1)} %get-tuple-element.43.hits_ref), custom_call_target="tpu_custom_call" | custom-call | tf_op jit(solution)/shard_map/pallas_call | solution.py:746
Async XLA Ops:
  2.0 31.5 %copy-start = (bf16[1664,256]{1,0:T(8,128)(2,1)S(1)}, bf16[1664,256]{1,0:T(8,128)(2,1)}, u32[]{:S(2)}) copy-start(bf16[1664,256]{1,0:T(8,128)(2,1)} %constant.2.clone.matrices) | copy-start | bytes 2555908
  2.0 20.9 %collective-permute-start = (f32[48,128]{1,0:T(8,128)S(1)}, f32[48,128]{1,0:T(8,128)S(1)}, u32[]{:S(2)}, u32[]{:S(2)}) collective-permute-start(f32[48,128]{1,0:T(8,128)S(1)} %get-tuple-element.27), channel_id=1, source_target_pairs={{1,2},{2,1},{3,4},{4,3},{5,6},{6,5},{7,8},{8,7},{9,10},{10,9},{11,... | collective-permute-start | bytes 73736 | tf_op jit(solution)/shard_map/ppermute | solution.py:687
  19.6 3.3 %collective-permute-start.1 = (f32[48,128]{1,0:T(8,128)S(1)}, f32[48,128]{1,0:T(8,128)S(1)}, u32[]{:S(2)}, u32[]{:S(2)}) collective-permute-start(f32[48,128]{1,0:T(8,128)S(1)} %get-tuple-element.28), channel_id=1, source_target_pairs={{0,1},{1,0},{2,3},{3,2},{4,5},{5,4},{6,7},{7,6},{8,9},{9,8},{10,11... | collective-permute-start | bytes 73736 | tf_op jit(solution)/shard_map/ppermute | solution.py:688
  23.1 12.4 %collective-permute-start.2 = (f32[192,128]{1,0:T(8,128)S(1)}, f32[192,128]{1,0:T(8,128)S(1)}, u32[]{:S(2)}, u32[]{:S(2)}) collective-permute-start(f32[192,128]{1,0:T(8,128)S(1)} %get-tuple-element.29), channel_id=1, source_target_pairs={{0,32},{32,0},{64,96},{96,64},{128,160},{160,128},{192,224},{224,1... | collective-permute-start | bytes 294920 | tf_op jit(solution)/shard_map/ppermute | solution.py:697
  26.5 12.5 %collective-permute-start.3 = (f32[192,128]{1,0:T(8,128)S(1)}, f32[192,128]{1,0:T(8,128)S(1)}, u32[]{:S(2)}, u32[]{:S(2)}) collective-permute-start(f32[192,128]{1,0:T(8,128)S(1)} %get-tuple-element.30), channel_id=1, source_target_pairs={{32,64},{64,32},{96,128},{128,96},{160,192},{192,160},{224,256},{2... | collective-permute-start | bytes 294920 | tf_op jit(solution)/shard_map/ppermute | solution.py:696

commit v10 on v9

--- a/solution.py
+++ b/solution.py
@@ -460,7 +460,10 @@
     lists = send_lists([tile(r, g, STATE + 6, 1) for r in OWN_ROWS for g in range(2)])
     lists_ref[...] = lists
     line = (lists[0:1] + lists[1:2] + lists[2:3]).astype(jnp.int32) - 1
-    picks_ref[...] = (row_iota((POINTS_DEV, 1024)) == line).astype(F32).astype(BF16)
+    row16 = row_iota((POINTS_DEV, 1024)).astype(jnp.int16)
+    picks_ref[...] = jnp.where(
+        row16 == line.astype(jnp.int16), jnp.bfloat16(1), jnp.bfloat16(0)
+    )
     spread, direct = local_terms(
         OWN_ROWS, tile, matrices, slopes, flux, plain, coefs, coefs_at
     )

time: 73.7 us -> 73.7 us (level)
  transfers between devices with their start and end apart: 4 -> 4, of which waited for: 1 -> 1; matrix products, arithmetic and copies ran while one was open for 0% -> 0% of each run, Pallas kernels for 5% -> 4%
where the time goes in v10:
time: 73.7 us; the launch traced here: 73.4 us
  blocking collectives  31 us (42%)
  starting transfers between devices  29.9 us (41%)
  Pallas kernels  7.87 us (11%)
  waiting for transfers between devices  3.95 us (5%)
  between operations  0.74 us (1%)
    all_to_all x1, blocking collectives, body(): lax.all_to_all(sent, 'col', split_axis=0, concat_axis=0, tiled=True)  31 us
    ppermute x1, starting transfers between devices, body(): lax.ppermute(far, 'col', swaps(cols, 1) + [(cols - 1, 0), (0, cols - 1)])  17.6 us
    ppermute x1, starting transfers between devices, body(): second_far = lax.ppermute(second, 'curve', swaps(rows, 1))  6.97 us
    ppermute x1, waiting for transfers between devices, body(): second_far = lax.ppermute(second, 'curve', swaps(rows, 1))  3.94 us
    ppermute x1, starting transfers between devices, body(): first_far = lax.ppermute(first, 'curve', swaps(rows, 0))  3.38 us
    pallas_call x1, Pallas kernels, body(): call(section_kernel, [((STATE, 1024), F32), ((POINTS_DEV, LANES), F32)],...  2.07 us
    ppermute x1, starting transfers between devices, body(): from_close = lax.ppermute(close, 'col', swaps(cols, 0))  1.92 us
    pallas_call x1, Pallas kernels, body(): call(inner_kernel, [((8, 1024), F32), ((4 * 56, 2 * LANES), F32), ((4 * 3...  1.57 us
  transfers between devices with their start and end apart: 4, of which 1 were waited for; matrix products, arithmetic and copies ran while one was open for 0% of the time, Pallas kernels for 4%

profile of v10, /device:TPU:6, one launch (start us, length us, event | category | flops | bytes accessed | tf_op | source)
XLA Modules:
  0.0 73.4 jit_solution(5835017099304930457)
XLA Ops:
  0.6 1.3 %shard_map.86 = (f32[48,128]{1,0:T(8,128)S(1)}, f32[48,128]{1,0:T(8,128)S(1)}, f32[56,768]{1,0:T(8,128)S(1)}) custom-call(f32[5,8,768]{2,1,0:T(8,128)} %state_ref.1, f32[768]{0:T(1024)} %jacobian_ref.1, f32[768]{0:T(1024)} %coriolis_ref.1, f32[4,768]{1,0:T(4,128)} %metric_ref.1, s32[8,48]{1,0:T(8,128)} %near_ref.1, s32[768]{0:T(1024)} %slot_ref.1), custom_call_target="tpu_custom_call" | custom-call | tf_op jit(solution)/shard_map/pallas_call | solution.py:674
  2.0 0.0 copy-start
  2.0 17.6 %collective-permute-start = (f32[48,128]{1,0:T(8,128)S(1)}, f32[48,128]{1,0:T(8,128)S(1)}, u32[]{:S(2)}, u32[]{:S(2)}) collective-permute-start(f32[48,128]{1,0:T(8,128)S(1)} %get-tuple-element.27), channel_id=1, source_target_pairs={{1,2},{2,1},{3,4},{4,3},{5,6},{6,5},{7,8},{8,7},{9,10},{10,9},{11,... | collective-permute-start | bytes 73736 | tf_op jit(solution)/shard_map/ppermute | solution.py:690
  19.6 1.9 %collective-permute-start.1 = (f32[48,128]{1,0:T(8,128)S(1)}, f32[48,128]{1,0:T(8,128)S(1)}, u32[]{:S(2)}, u32[]{:S(2)}) collective-permute-start(f32[48,128]{1,0:T(8,128)S(1)} %get-tuple-element.28), channel_id=1, source_target_pairs={{0,1},{1,0},{2,3},{3,2},{4,5},{5,4},{6,7},{7,6},{8,9},{9,8},{10,11... | collective-permute-start | bytes 73736 | tf_op jit(solution)/shard_map/ppermute | solution.py:691
  21.5 1.4 %shard_map.87 = (f32[192,128]{1,0:T(8,128)S(1)}, f32[192,128]{1,0:T(8,128)S(1)}, bf16[1024,768]{1,0:T(8,128)(2,1)S(1)}) custom-call(f32[56,768]{1,0:T(8,128)S(1)} %get-tuple-element.24.values_ref), custom_call_target="tpu_custom_call" | custom-call | flops 400000000 | bytes 1000000 | tf_op jit(solution)/shard_map/pallas_call | solution.py:692
  22.9 0.0 collective-permute-done.from_far
  22.9 0.0 collective-permute-done.1.from_close
  22.9 0.1 shard_map.88
  23.1 3.4 %collective-permute-start.2 = (f32[192,128]{1,0:T(8,128)S(1)}, f32[192,128]{1,0:T(8,128)S(1)}, u32[]{:S(2)}, u32[]{:S(2)}) collective-permute-start(f32[192,128]{1,0:T(8,128)S(1)} %get-tuple-element.29), channel_id=1, source_target_pairs={{0,32},{32,0},{64,96},{96,64},{128,160},{160,128},{192,224},{224,1... | collective-permute-start | bytes 294920 | tf_op jit(solution)/shard_map/ppermute | solution.py:700
  26.5 7.0 %collective-permute-start.3 = (f32[192,128]{1,0:T(8,128)S(1)}, f32[192,128]{1,0:T(8,128)S(1)}, u32[]{:S(2)}, u32[]{:S(2)}) collective-permute-start(f32[192,128]{1,0:T(8,128)S(1)} %get-tuple-element.30), channel_id=1, source_target_pairs={{32,64},{64,32},{96,128},{128,96},{160,192},{192,160},{224,256},{2... | collective-permute-start | bytes 294920 | tf_op jit(solution)/shard_map/ppermute | solution.py:699
  33.4 0.0 copy-done
  33.4 1.6 %shard_map.89 = (f32[8,1024]{1,0:T(8,128)S(1)}, f32[224,256]{1,0:T(8,128)S(1)}, f32[128,256]{1,0:T(8,128)S(1)}, f32[192,128]{1,0:T(8,128)S(1)}, bf16[768,1024]{1...) custom-call(f32[192,128]{1,0:T(8,128)S(1)} %get-tuple-element.31.low_ref, ...), custom_call_target="tpu_custom_call" | custom-call | flops 400000000 | bytes 1000000 | tf_op jit(solution)/shard_map/pallas_call | solution.py:710
  35.0 0.0 collective-permute-done.2.first_far_ref
  35.0 3.9 %collective-permute-done.3.second_far_ref = f32[192,128]{1,0:T(8,128)S(1)} collective-permute-done((f32[192,128]{1,0:T(8,128)S(1)}, f32[192,128]{1,0:T(8,128)S(1)}, u32[]{:S(2)}, u32[]{:S(2)}) %collective-permute-start.3) | collective-permute-done | bytes 98336 | tf_op jit(solution)/shard_map/ppermute | solution.py:699
  39.0 2.1 %shard_map.90 = (f32[40,1024]{1,0:T(8,128)S(1)}, f32[768,128]{1,0:T(8,128)S(1)}) custom-call(f32[192,128]{1,0:T(8,128)S(1)} %collective-permute-done.2.first_far_ref, f32[192,128]{1,0:T(8,128)S(1)} %collective-permute-done.3.second_far_ref, f32[192,128]{1,0:T(8,128)S(1)} %get-tuple-element.31.low_ref, f32[192,128]{1,0:T(8,128)S(1)} %get-tuple-element.32.high_ref, ...), custom_call_target="tpu_custom_call" | custom-call | tf_op jit(solution)/shard_map/pallas_call | solution.py:727
  41.0 31.0 %all_to_all.11 = f32[32,24,128]{2,1,0:T(8,128)S(1)} all-to-all(f32[32,24,128]{2,1,0:T(8,128)S(1)} %bitcast.5), channel_id=1, replica_groups=mesh['curve'=24,'col'=32] {'col'}, dimensions={0} | all-to-all | bytes 786432 | tf_op jit(solution)/shard_map/all_to_all | solution.py:748
  72.0 1.4 %shard_map.91 = (f32[40,768]{1,0:T(8,128)}, f32[40,768]{1,0:T(8,128)}) custom-call(f32[768,128]{1,0:T(8,128)S(1)} %bitcast.4, f32[40,1024]{1,0:T(8,128)S(1)} %get-tuple-element.42.whole_ref, bf16[1024,768]{1,0:T(8,128)(2,1)S(1)} %get-tuple-element.43.hits_ref), custom_call_target="tpu_custom_call" | custom-call | tf_op jit(solution)/shard_map/pallas_call | solution.py:749
Async XLA Ops:
  2.0 31.5 %copy-start = (bf16[1664,256]{1,0:T(8,128)(2,1)S(1)}, bf16[1664,256]{1,0:T(8,128)(2,1)}, u32[]{:S(2)}) copy-start(bf16[1664,256]{1,0:T(8,128)(2,1)} %constant.2.clone.matrices) | copy-start | bytes 2555908
  2.0 20.9 %collective-permute-start = (f32[48,128]{1,0:T(8,128)S(1)}, f32[48,128]{1,0:T(8,128)S(1)}, u32[]{:S(2)}, u32[]{:S(2)}) collective-permute-start(f32[48,128]{1,0:T(8,128)S(1)} %get-tuple-element.27), channel_id=1, source_target_pairs={{1,2},{2,1},{3,4},{4,3},{5,6},{6,5},{7,8},{8,7},{9,10},{10,9},{11,... | collective-permute-start | bytes 73736 | tf_op jit(solution)/shard_map/ppermute | solution.py:690
  19.6 3.3 %collective-permute-start.1 = (f32[48,128]{1,0:T(8,128)S(1)}, f32[48,128]{1,0:T(8,128)S(1)}, u32[]{:S(2)}, u32[]{:S(2)}) collective-permute-start(f32[48,128]{1,0:T(8,128)S(1)} %get-tuple-element.28), channel_id=1, source_target_pairs={{0,1},{1,0},{2,3},{3,2},{4,5},{5,4},{6,7},{7,6},{8,9},{9,8},{10,11... | collective-permute-start | bytes 73736 | tf_op jit(solution)/shard_map/ppermute | solution.py:691
  23.1 12.0 %collective-permute-start.2 = (f32[192,128]{1,0:T(8,128)S(1)}, f32[192,128]{1,0:T(8,128)S(1)}, u32[]{:S(2)}, u32[]{:S(2)}) collective-permute-start(f32[192,128]{1,0:T(8,128)S(1)} %get-tuple-element.29), channel_id=1, source_target_pairs={{0,32},{32,0},{64,96},{96,64},{128,160},{160,128},{192,224},{224,1... | collective-permute-start | bytes 294920 | tf_op jit(solution)/shard_map/ppermute | solution.py:700
  26.5 12.5 %collective-permute-start.3 = (f32[192,128]{1,0:T(8,128)S(1)}, f32[192,128]{1,0:T(8,128)S(1)}, u32[]{:S(2)}, u32[]{:S(2)}) collective-permute-start(f32[192,128]{1,0:T(8,128)S(1)} %get-tuple-element.30), channel_id=1, source_target_pairs={{32,64},{64,32},{96,128},{128,96},{160,192},{192,160},{224,256},{2... | collective-permute-start | bytes 294920 | tf_op jit(solution)/shard_map/ppermute | solution.py:699

commit v11 on v10

--- a/solution.py
+++ b/solution.py
@@ -125,7 +125,9 @@
 
 def over_points(element_values):
     shape = (ELEMS_DEV, POINTS_DEV)
-    spread = (lane_iota(shape) // 16 == row_iota(shape)).astype(F32).astype(BF16)
+    first = row_iota(shape) * 16
+    spread = (lane_iota(shape) >= first) & (lane_iota(shape) < first + 16)
+    spread = spread.astype(F32).astype(BF16)
     return dot(element_values.astype(BF16), spread)[0:1].astype(jnp.int32)
 
 

time: 73.7 us -> 73.7 us (level)
  no operation moved by 1% of the time
where the time goes in v11:
time: 73.7 us; the launch traced here: 73.5 us
  blocking collectives  31 us (42%)
  starting transfers between devices  29.9 us (41%)
  Pallas kernels  7.87 us (11%)
  waiting for transfers between devices  3.95 us (5%)
  between operations  0.74 us (1%)
    all_to_all x1, blocking collectives, body(): lax.all_to_all(sent, 'col', split_axis=0, concat_axis=0, tiled=True)  31 us
    ppermute x1, starting transfers between devices, body(): lax.ppermute(far, 'col', swaps(cols, 1) + [(cols - 1, 0), (0, cols - 1)])  17.6 us
    ppermute x1, starting transfers between devices, body(): second_far = lax.ppermute(second, 'curve', swaps(rows, 1))  6.96 us
    ppermute x1, waiting for transfers between devices, body(): second_far = lax.ppermute(second, 'curve', swaps(rows, 1))  3.94 us
    ppermute x1, starting transfers between devices, body(): first_far = lax.ppermute(first, 'curve', swaps(rows, 0))  3.38 us
    pallas_call x1, Pallas kernels, body(): call(section_kernel, [((STATE, 1024), F32), ((POINTS_DEV, LANES), F32)],...  2.07 us
    ppermute x1, starting transfers between devices, body(): from_close = lax.ppermute(close, 'col', swaps(cols, 0))  1.92 us
    pallas_call x1, Pallas kernels, body(): call(inner_kernel, [((8, 1024), F32), ((4 * 56, 2 * LANES), F32), ((4 * 3...  1.57 us
  transfers between devices with their start and end apart: 4, of which 1 were waited for; matrix products, arithmetic and copies ran while one was open for 0% of the time, Pallas kernels for 4%

profile of v11, /device:TPU:6, one launch (start us, length us, event | category | flops | bytes accessed | tf_op | source)
XLA Modules:
  0.0 73.5 jit_solution(3952362676927796930)
XLA Ops:
  0.6 1.3 %shard_map.86 = (f32[48,128]{1,0:T(8,128)S(1)}, f32[48,128]{1,0:T(8,128)S(1)}, f32[56,768]{1,0:T(8,128)S(1)}) custom-call(f32[5,8,768]{2,1,0:T(8,128)} %state_ref.1, f32[768]{0:T(1024)} %jacobian_ref.1, f32[768]{0:T(1024)} %coriolis_ref.1, f32[4,768]{1,0:T(4,128)} %metric_ref.1, s32[8,48]{1,0:T(8,128)} %near_ref.1, s32[768]{0:T(1024)} %slot_ref.1), custom_call_target="tpu_custom_call" | custom-call | tf_op jit(solution)/shard_map/pallas_call | solution.py:676
  1.9 0.0 copy-start
  2.0 17.6 %collective-permute-start = (f32[48,128]{1,0:T(8,128)S(1)}, f32[48,128]{1,0:T(8,128)S(1)}, u32[]{:S(2)}, u32[]{:S(2)}) collective-permute-start(f32[48,128]{1,0:T(8,128)S(1)} %get-tuple-element.27), channel_id=1, source_target_pairs={{1,2},{2,1},{3,4},{4,3},{5,6},{6,5},{7,8},{8,7},{9,10},{10,9},{11,... | collective-permute-start | bytes 73736 | tf_op jit(solution)/shard_map/ppermute | solution.py:692
  19.6 1.9 %collective-permute-start.1 = (f32[48,128]{1,0:T(8,128)S(1)}, f32[48,128]{1,0:T(8,128)S(1)}, u32[]{:S(2)}, u32[]{:S(2)}) collective-permute-start(f32[48,128]{1,0:T(8,128)S(1)} %get-tuple-element.28), channel_id=1, source_target_pairs={{0,1},{1,0},{2,3},{3,2},{4,5},{5,4},{6,7},{7,6},{8,9},{9,8},{10,11... | collective-permute-start | bytes 73736 | tf_op jit(solution)/shard_map/ppermute | solution.py:693
  21.5 1.4 %shard_map.87 = (f32[192,128]{1,0:T(8,128)S(1)}, f32[192,128]{1,0:T(8,128)S(1)}, bf16[1024,768]{1,0:T(8,128)(2,1)S(1)}) custom-call(f32[56,768]{1,0:T(8,128)S(1)} %get-tuple-element.24.values_ref), custom_call_target="tpu_custom_call" | custom-call | flops 400000000 | bytes 1000000 | tf_op jit(solution)/shard_map/pallas_call | solution.py:694
  22.9 0.0 collective-permute-done.from_far
  22.9 0.0 collective-permute-done.1.from_close
  22.9 0.1 shard_map.88
  23.1 3.4 %collective-permute-start.2 = (f32[192,128]{1,0:T(8,128)S(1)}, f32[192,128]{1,0:T(8,128)S(1)}, u32[]{:S(2)}, u32[]{:S(2)}) collective-permute-start(f32[192,128]{1,0:T(8,128)S(1)} %get-tuple-element.29), channel_id=1, source_target_pairs={{0,32},{32,0},{64,96},{96,64},{128,160},{160,128},{192,224},{224,1... | collective-permute-start | bytes 294920 | tf_op jit(solution)/shard_map/ppermute | solution.py:702
  26.4 7.0 %collective-permute-start.3 = (f32[192,128]{1,0:T(8,128)S(1)}, f32[192,128]{1,0:T(8,128)S(1)}, u32[]{:S(2)}, u32[]{:S(2)}) collective-permute-start(f32[192,128]{1,0:T(8,128)S(1)} %get-tuple-element.30), channel_id=1, source_target_pairs={{32,64},{64,32},{96,128},{128,96},{160,192},{192,160},{224,256},{2... | collective-permute-start | bytes 294920 | tf_op jit(solution)/shard_map/ppermute | solution.py:701
  33.4 0.0 copy-done
  33.4 1.6 %shard_map.89 = (f32[8,1024]{1,0:T(8,128)S(1)}, f32[224,256]{1,0:T(8,128)S(1)}, f32[128,256]{1,0:T(8,128)S(1)}, f32[192,128]{1,0:T(8,128)S(1)}, bf16[768,1024]{1...) custom-call(f32[192,128]{1,0:T(8,128)S(1)} %get-tuple-element.31.low_ref, ...), custom_call_target="tpu_custom_call" | custom-call | flops 400000000 | bytes 1000000 | tf_op jit(solution)/shard_map/pallas_call | solution.py:712
  35.0 0.0 collective-permute-done.2.first_far_ref
  35.0 3.9 %collective-permute-done.3.second_far_ref = f32[192,128]{1,0:T(8,128)S(1)} collective-permute-done((f32[192,128]{1,0:T(8,128)S(1)}, f32[192,128]{1,0:T(8,128)S(1)}, u32[]{:S(2)}, u32[]{:S(2)}) %collective-permute-start.3) | collective-permute-done | bytes 98336 | tf_op jit(solution)/shard_map/ppermute | solution.py:701
  39.0 2.1 %shard_map.90 = (f32[40,1024]{1,0:T(8,128)S(1)}, f32[768,128]{1,0:T(8,128)S(1)}) custom-call(f32[192,128]{1,0:T(8,128)S(1)} %collective-permute-done.2.first_far_ref, f32[192,128]{1,0:T(8,128)S(1)} %collective-permute-done.3.second_far_ref, f32[192,128]{1,0:T(8,128)S(1)} %get-tuple-element.31.low_ref, f32[192,128]{1,0:T(8,128)S(1)} %get-tuple-element.32.high_ref, ...), custom_call_target="tpu_custom_call" | custom-call | tf_op jit(solution)/shard_map/pallas_call | solution.py:729
  41.0 31.0 %all_to_all.11 = f32[32,24,128]{2,1,0:T(8,128)S(1)} all-to-all(f32[32,24,128]{2,1,0:T(8,128)S(1)} %bitcast.5), channel_id=1, replica_groups=mesh['curve'=24,'col'=32] {'col'}, dimensions={0} | all-to-all | bytes 786432 | tf_op jit(solution)/shard_map/all_to_all | solution.py:750
  72.0 1.4 %shard_map.91 = (f32[40,768]{1,0:T(8,128)}, f32[40,768]{1,0:T(8,128)}) custom-call(f32[768,128]{1,0:T(8,128)S(1)} %bitcast.4, f32[40,1024]{1,0:T(8,128)S(1)} %get-tuple-element.42.whole_ref, bf16[1024,768]{1,0:T(8,128)(2,1)S(1)} %get-tuple-element.43.hits_ref), custom_call_target="tpu_custom_call" | custom-call | tf_op jit(solution)/shard_map/pallas_call | solution.py:751
Async XLA Ops:
  1.9 31.5 %copy-start = (bf16[1664,256]{1,0:T(8,128)(2,1)S(1)}, bf16[1664,256]{1,0:T(8,128)(2,1)}, u32[]{:S(2)}) copy-start(bf16[1664,256]{1,0:T(8,128)(2,1)} %constant.2.clone.matrices) | copy-start | bytes 2555908
  2.0 20.9 %collective-permute-start = (f32[48,128]{1,0:T(8,128)S(1)}, f32[48,128]{1,0:T(8,128)S(1)}, u32[]{:S(2)}, u32[]{:S(2)}) collective-permute-start(f32[48,128]{1,0:T(8,128)S(1)} %get-tuple-element.27), channel_id=1, source_target_pairs={{1,2},{2,1},{3,4},{4,3},{5,6},{6,5},{7,8},{8,7},{9,10},{10,9},{11,... | collective-permute-start | bytes 73736 | tf_op jit(solution)/shard_map/ppermute | solution.py:692
  19.6 3.3 %collective-permute-start.1 = (f32[48,128]{1,0:T(8,128)S(1)}, f32[48,128]{1,0:T(8,128)S(1)}, u32[]{:S(2)}, u32[]{:S(2)}) collective-permute-start(f32[48,128]{1,0:T(8,128)S(1)} %get-tuple-element.28), channel_id=1, source_target_pairs={{0,1},{1,0},{2,3},{3,2},{4,5},{5,4},{6,7},{7,6},{8,9},{9,8},{10,11... | collective-permute-start | bytes 73736 | tf_op jit(solution)/shard_map/ppermute | solution.py:693
  23.1 12.0 %collective-permute-start.2 = (f32[192,128]{1,0:T(8,128)S(1)}, f32[192,128]{1,0:T(8,128)S(1)}, u32[]{:S(2)}, u32[]{:S(2)}) collective-permute-start(f32[192,128]{1,0:T(8,128)S(1)} %get-tuple-element.29), channel_id=1, source_target_pairs={{0,32},{32,0},{64,96},{96,64},{128,160},{160,128},{192,224},{224,1... | collective-permute-start | bytes 294920 | tf_op jit(solution)/shard_map/ppermute | solution.py:702
  26.4 12.5 %collective-permute-start.3 = (f32[192,128]{1,0:T(8,128)S(1)}, f32[192,128]{1,0:T(8,128)S(1)}, u32[]{:S(2)}, u32[]{:S(2)}) collective-permute-start(f32[192,128]{1,0:T(8,128)S(1)} %get-tuple-element.30), channel_id=1, source_target_pairs={{32,64},{64,32},{96,128},{128,96},{160,192},{192,160},{224,256},{2... | collective-permute-start | bytes 294920 | tf_op jit(solution)/shard_map/ppermute | solution.py:701
